TPU v7x, 32 devices: a whole 2x2x4 slice. The times are simulated.
32 devices in a mesh: row: 8 (over y, x, core), col: 4 (over z).
Axes of the slice: x: 2, y: 2, z: 4, core: 2. Of those that a mesh axis runs over, the one named last changes fastest.
Arguments:
- object_re: float32 [3072, 2048], P('row', 'col'), may hold values from -6 to 6
- object_im: float32 [3072, 2048], P('row', 'col'), may hold values from -6 to 6
- probe_re: float32 [256, 256], replicated, may hold values from -6 to 6
- probe_im: float32 [256, 256], replicated, may hold values from -6 to 6
- frames: bfloat16 [8, 4, 8, 256, 256], P('row', 'col'), may hold values from 0.049804688 to 20
- counts: int32 [8, 4], P('row', 'col'), may hold values from 1 to 8, as said below
- offsets: int32 [8, 4, 8, 2], P('row', 'col'), may hold values from -32 to 288, as said below
- frame_index: int32 [8, 4, 8], P('row', 'col'), may hold values from 0 to 7
Outputs:
- new_re: float32 [3072, 2048], P('row', 'col')
- new_im: float32 [3072, 2048], P('row', 'col')
Inputs may be any that keep to these rules, and one draw needn't show every extreme that they name: `counts`: in every draw some tile has 8 positions and some tile has one. Row offsets are -32 plus multiples of 16, at most 160; column offsets likewise, at most 288; in every draw some live position has both offsets at the lowest value and some has both at the highest.
All inputs are finite; a program needn't handle non-finite values.
Results may differ from a plain program's by a relative error of at most 0.0003.
Values sent between devices are 32-bit elements; how exact they have to be, the bound alone decides.
No kernel may reach another device: no remote copies, remote signals or barrier semaphores. Data moves between devices by JAX's collectives and lax.ppermute only.
A program may use at most 64 MiB of HBM per device.

v0:
```python
import functools
import math

import jax
import jax.numpy as jnp
import ml_dtypes
import numpy as np
from jax import lax
from jax.experimental import pallas as pl
from jax.experimental.pallas import tpu as pltpu
from jax.sharding import PartitionSpec as P

P_SIZE = 256
HALF = P_SIZE // 2
HALO = 32
LANES = 128
GROUPS = LANES // HALO
MARKS = 8
PAIR = 2

floor_amp = 0.5
ridge = 1.0

VMEM = pl.BlockSpec(memory_space=pltpu.VMEM)
SMEM = pl.BlockSpec(memory_space=pltpu.SMEM)
HBM = pl.BlockSpec(memory_space=pltpu.HBM)
PARAMS = pltpu.CompilerParams(vmem_limit_bytes=32 * 1024 * 1024)
SMALL = pltpu.CompilerParams(vmem_limit_bytes=16 * 1024 * 1024)
BUSY = pl.CostEstimate(flops=4_000_000_000, bytes_accessed=8_000_000, transcendentals=0)


def transform_tables():
    index = np.arange(HALF)
    plain = []
    for parity in (0, 1):
        angle = 2.0 * math.pi / P_SIZE * (index[:, None] * (2 * index[None, :] + parity) % P_SIZE)
        cos, sin = np.cos(angle), np.sin(angle)
        plain.append(np.block([[cos, -sin], [sin, cos]]) / math.sqrt(P_SIZE))
    parts = []
    for table in plain + [t.T for t in plain]:
        high = table.astype(np.float32).astype(ml_dtypes.bfloat16)
        low = (table - high.astype(np.float64)).astype(np.float32).astype(ml_dtypes.bfloat16)
        parts += [high, low]
    order = np.concatenate([np.arange(0, P_SIZE, 2), np.arange(1, P_SIZE, 2)])
    sort = np.zeros((P_SIZE, P_SIZE), np.float32)
    sort[np.arange(P_SIZE), order] = 1.0
    parts += [sort.astype(ml_dtypes.bfloat16), sort.T.astype(ml_dtypes.bfloat16)]
    return np.stack(parts)


def lane_index(rows):
    return lax.broadcasted_iota(jnp.int32, (rows, LANES), 1)


def pack_lanes(ref, rows, first):
    lane = lane_index(rows)
    packed = None
    for g in range(GROUPS):
        part = ref[g * rows : (g + 1) * rows, :]
        if g:
            part = pltpu.roll(part, HALO * g, 1)
        low = (first + HALO * g) % LANES
        mine = (lane >= low) & (lane < low + HALO)
        packed = part if packed is None else jnp.where(mine, part, packed)
    return packed


def unpack_lanes(packed, group):
    return pltpu.roll(packed, LANES - HALO * group, 1) if group else packed


def split(x):
    high = x.astype(jnp.bfloat16)
    return high, (x - high.astype(jnp.float32)).astype(jnp.bfloat16)


def product(left, right):
    return jnp.dot(left, right, preferred_element_type=jnp.float32)


def times_table(x, table, which):
    high, low = split(x)
    t_high, t_low = table[2 * which], table[2 * which + 1]
    return product(high, t_high) + (product(high, t_low) + product(low, t_high))


def table_times(table, which, x):
    high, low = split(x)
    t_high, t_low = table[2 * which], table[2 * which + 1]
    return product(t_high, high) + (product(t_low, high) + product(t_high, low))


def beside(*blocks):
    return jnp.concatenate(blocks, axis=1)


def below(*blocks):
    return jnp.concatenate(blocks, axis=0)


def ends(x):
    return x[:, :HALF], x[:, HALF:]


def forward_columns(exit_re, exit_im, table):
    re_lo, re_hi = ends(exit_re)
    im_lo, im_hi = ends(exit_im)
    even = times_table(beside(re_lo + re_hi, im_lo + im_hi), table, 0)
    odd = times_table(beside(re_lo - re_hi, im_lo - im_hi), table, 1)
    return even, odd


def forward_rows(even, odd, table):
    out = []
    for parity in (0, 1):
        if parity == 0:
            se, so = even[:HALF] + even[HALF:], odd[:HALF] + odd[HALF:]
        else:
            se, so = even[:HALF] - even[HALF:], odd[:HALF] - odd[HALF:]
        e_re, e_im = ends(se)
        o_re, o_im = ends(so)
        out.append(table_times(table, 2 + parity, below(beside(e_re, o_re), beside(e_im, o_im))))
    return out


def residual(far, frame):
    out = []
    for parity in (0, 1):
        re, im = far[parity][:HALF], far[parity][HALF:]
        level = jnp.maximum(re * re + im * im, floor_amp * floor_amp)
        inten = frame[parity * HALF : (parity + 1) * HALF]
        factor = 1.0 - inten * lax.rsqrt(inten * level)
        out.append(below(re * factor, im * factor))
    return out


def back_rows(res, table):
    first = table_times(table, 0, res[0])
    second = table_times(table, 1, res[1])
    upper, lower = first + second, first - second
    out = []
    for cols in (slice(0, HALF), slice(HALF, P_SIZE)):
        out.append(
            below(
                beside(upper[:HALF, cols], upper[HALF:, cols]),
                beside(lower[:HALF, cols], lower[HALF:, cols]),
            )
        )
    return out


def back_columns(parts, table):
    even = times_table(parts[0], table, 2)
    odd = times_table(parts[1], table, 3)
    lo, hi = even + odd, even - odd
    return beside(lo[:, :HALF], hi[:, :HALF]), beside(lo[:, HALF:], hi[:, HALF:])


def is_odd(axis):
    return lax.rem(lax.axis_index(axis), 2) == 1


def fetch(pairs, sems):
    copies = [pltpu.make_async_copy(far, near, sems.at[i]) for i, (far, near) in enumerate(pairs)]
    for copy in copies:
        copy.start()
    return copies


def finish_all(copies):
    for copy in copies:
        copy.wait()


def row_edges(counts, obj_re, obj_im, offsets, chosen, to_inner, to_outer, marked, places, frame_of, sems):
    tile_r = obj_re.shape[0]
    odd = is_odd("row")
    low = pl.multiple_of(jnp.where(odd, 0, tile_r - HALO), 16)
    high = pl.multiple_of(jnp.where(odd, tile_r - HALO, 0), 16)
    pairs = [(offsets, places), (chosen, frame_of)]
    for k, ref in enumerate((obj_re, obj_im)):
        rows = slice(k * HALO, (k + 1) * HALO)
        pairs.append((ref.at[pl.ds(high, HALO)], to_outer.at[rows]))
        pairs.append((ref.at[pl.ds(low, HALO)], to_inner.at[rows]))
    copies = fetch(pairs, sems)
    finish_all(copies[:2])
    place = places[0, 0]
    live = lax.broadcasted_iota(jnp.int32, place.shape, 1) < counts[0, 0]
    place = jnp.where(live, place, 2 * tile_r)
    marked[0:2, :] = place
    marked[2:3, :] = frame_of[0]
    for message in (to_inner, to_outer):
        message[2 * HALO : 2 * HALO + 2, 0 : place.shape[1]] = place.astype(jnp.float32)
    finish_all(copies[2:])


def window_place(slots, slot):
    row = pl.multiple_of(slots[0, slot] + HALO, 16)
    col = slots[1, slot] + LANES
    turn = lax.rem(col, LANES)
    return row, pl.multiple_of(col - turn, LANES), turn


def add_window(acc, layer, where, keep, term, tiles=(0, 1, 2)):
    row, base, _ = where
    lo, hi = ends(term)
    parts = (jnp.where(keep, lo, 0.0), hi, jnp.where(keep, 0.0, lo))
    for t in tiles:
        acc[layer, pl.ds(row, term.shape[0]), pl.ds(base + t * LANES, LANES)] += parts[t]


def load_state(
    obj_re, obj_im, probe_re_far, probe_im_far, table_far, frames_far,
    cells, probe_re, probe_im, table, frames, sems,
):
    tile_r, tile_c = obj_re.shape
    inner = slice(HALO, HALO + tile_r)
    middle = slice(LANES, LANES + tile_c)
    pairs = (
        (table_far, table),
        (frames_far, frames),
        (obj_re, cells.at[0, inner, middle]),
        (obj_im, cells.at[1, inner, middle]),
        (probe_re_far, probe_re),
        (probe_im_far, probe_im),
    )
    finish_all(fetch(pairs, sems))


def fill_strip(strip, parts):
    done = 0
    for part in parts:
        strip[done : done + part.shape[0], :] = part
        done += part.shape[0]


def send_columns(to_left, to_right, to_inner, to_outer):
    odd = is_odd("col")
    to_inner[0 : to_left.shape[0], :] = jnp.where(odd, to_left, to_right)
    to_outer[0 : to_left.shape[0], :] = jnp.where(odd, to_right, to_left)


def received(by_inner, by_outer, axis):
    odd = is_odd(axis)
    index = lax.axis_index(axis)
    inside = (index > 0) & (index < lax.axis_size(axis) - 1)
    by_outer = jnp.where(inside, by_outer[...], 0.0)
    if len(by_inner.shape) > len(by_outer.shape):
        before, after = by_inner[0], by_inner[1]
    else:
        before = after = by_inner[...]
    return jnp.where(odd, before, by_outer), jnp.where(odd, by_outer, after)


def pieces(packed, layers, rows):
    group_rows = layers * rows // GROUPS
    for g in range(GROUPS):
        part = unpack_lanes(packed, g)
        done = 0
        while done < group_rows:
            layer, row = divmod(g * group_rows + done, rows)
            size = min(group_rows - done, rows - row)
            yield layer, row, part[done : done + size]
            done += size


def row_halos(cells_in, own, by_inner, by_outer, cells, marks, to_inner, to_outer, strip):
    rows, width = cells.shape[1:]
    middle = slice(LANES, width - LANES)
    before, after = received(by_inner, by_outer, "row")
    for k in (0, 1):
        cells[k, 0:HALO, middle] = before[k * HALO : (k + 1) * HALO]
        cells[k, rows - HALO : rows, middle] = after[k * HALO : (k + 1) * HALO]
    first_mark = 2 * HALO
    for i, message in enumerate((own[...], before, after)):
        marks[2 * i : 2 * i + 2, :] = message[first_mark : first_mark + 2, 0:LANES]
    group_rows = 2 * rows // GROUPS
    first, last = slice(LANES, 2 * LANES), slice(width - 2 * LANES, width - LANES)
    fill_strip(strip, (cells[0, :, first], cells[1, :, first]))
    to_left = pack_lanes(strip, group_rows, 0)
    fill_strip(strip, (cells[0, :, last], cells[1, :, last]))
    to_right = pack_lanes(strip, group_rows, LANES - HALO)
    send_columns(to_left, to_right, to_inner, to_outer)
    to_inner[group_rows:, :] = marks[...]
    to_outer[group_rows:, :] = marks[...]


def live_slots(slots, cells):
    tile_r = cells.shape[1] - 2 * HALO
    count = jnp.int32(0)
    for slot in range(slots.shape[1]):
        count += (slots[0, slot] < tile_r).astype(jnp.int32)
    return count


def run_windows(wanted, slots, cells, acc, probe_re, probe_im, table, frames, order):
    tile_c = cells.shape[2] - 2 * LANES
    count = live_slots(slots, cells)
    every = range(slots.shape[1])
    over = []
    for slot in every:
        col = slots[1, slot]
        over.append((col < 0) | (col > tile_c - P_SIZE))
    total = jnp.int32(0)
    for slot in every:
        total += ((slot < count) & ~over[slot]).astype(jnp.int32)
    limit = jnp.where(total < len(every) - 1, PAIR, 2 * PAIR)
    seen, found = jnp.int32(0), jnp.int32(0)
    for slot in every:
        live = slot < count
        mine = live & wanted(over[slot], seen, limit)

        @pl.when(mine)
        def _():
            order[found] = slot

        seen += (live & ~over[slot]).astype(jnp.int32)
        found += mine.astype(jnp.int32)

    lane = lane_index(P_SIZE)

    def load(slot):
        where = row, base, turn = window_place(slots, slot)
        keep = lane >= turn
        w_re = pltpu.roll(probe_re[...], turn, 1)
        w_im = pltpu.roll(probe_im[...], turn, 1)
        patch = []
        for k in (0, 1):
            block = cells[k, pl.ds(row, P_SIZE), pl.ds(base, 3 * LANES)]
            patch.append(
                beside(jnp.where(keep, block[:, :LANES], block[:, 2 * LANES :]), block[:, LANES : 2 * LANES])
            )
        exit_re = w_re * patch[0] - w_im * patch[1]
        exit_im = w_re * patch[1] + w_im * patch[0]
        return (where, keep, w_re, w_im), exit_re, exit_im

    def frame_of(slot):
        sort, unsort = table[8], table[9]
        half = product(sort, frames[slots[2, slot]]).astype(jnp.bfloat16)
        return product(half, unsort)

    def place(at, back_re, back_im):
        where, keep, w_re, w_im = at
        add_window(acc, 0, where, keep, w_re * back_re + w_im * back_im)
        add_window(acc, 1, where, keep, w_re * back_im - w_im * back_re)

    def step(group):
        frame = [frame_of(slot) for slot in group]
        loaded = [load(slot) for slot in group]
        state = [forward_columns(x[1], x[2], table) for x in loaded]
        state = [forward_rows(*x, table) for x in state]
        state = [residual(x, f) for x, f in zip(state, frame)]
        state = [back_rows(x, table) for x in state]
        state = [back_columns(x, table) for x in state]
        for x, back in zip(loaded, state):
            place(x[0], *back)

    def pair_step(pair, carry):
        step([order[pair * PAIR + i] for i in range(PAIR)])
        return carry

    lax.fori_loop(0, found // PAIR, pair_step, 0)

    @pl.when(found % PAIR == 1)
    def _():
        step([order[found - 1]])


def windows_before(
    slots, cells, probe_re, probe_im, table, frames, acc, order, power,
):
    acc[...] = jnp.zeros_like(acc)
    power[...] = probe_re[...] * probe_re[...] + probe_im[...] * probe_im[...]
    lane = lane_index(P_SIZE)

    def step(slot, carry):
        where = window_place(slots, slot)
        add_window(acc, 2, where, lane >= where[2], pltpu.roll(power[...], where[2], 1))
        return carry

    lax.fori_loop(0, live_slots(slots, cells), step, 0)
    run_windows(
        lambda over, seen, limit: ~over & (seen < limit),
        slots, cells, acc, probe_re, probe_im, table, frames, order,
    )


def reaching(place, right, tile_r, tile_c):
    shape = place.shape
    index = lax.broadcasted_iota(jnp.int32, shape, 0)
    lane = lax.broadcasted_iota(jnp.int32, shape, 1)
    col = pltpu.roll(place, shape[0] - 1, 0)
    low = jnp.where(index == 2, tile_r - P_SIZE, -tile_r).astype(jnp.float32)
    high = jnp.where(index == 4, 0, tile_r).astype(jnp.float32)
    reaches = (lane < MARKS) & (index % 2 == 0) & (index < 6) & (place > low) & (place < high)
    if right < 0:
        reaches &= col > tile_c - P_SIZE
    if right > 0:
        reaches &= col < 0
    bit = lax.shift_left(jnp.ones(shape, jnp.int32), jnp.minimum(lane, MARKS)).astype(jnp.float32)
    bits = jnp.sum(jnp.where(reaches, bit, 0.0), axis=1, keepdims=True)
    return jnp.where(lane < MARKS, place, bits).astype(jnp.int32)


def add_neighbours_light(places, acc, power):
    rows, width = acc.shape[1:]
    tile_r, tile_c = rows - 2 * HALO, width - 2 * LANES
    for right in (-1, 0, 1):
        for i, down in enumerate((0, -1, 1)):
            if not right and not down:
                continue
            first, last = {-1: (P_SIZE - HALO, P_SIZE), 0: (0, P_SIZE), 1: (0, HALO)}[down]
            tiles = {-1: (2,), 0: (0, 1, 2), 1: (0,)}[right]
            lane = lane_index(last - first)
            bits = places[right + 1, 2 * i, MARKS]

            def step(slot, carry):
                row, col = places[right + 1, 2 * i, slot], places[right + 1, 2 * i + 1, slot]

                @pl.when(lax.shift_right_logical(bits, slot) % 2 == 1)
                def _():
                    turn = lax.rem(col + LANES, LANES)
                    at = pl.multiple_of(row + HALO + (down * tile_r + first), 16)
                    base = pl.multiple_of(col + LANES - turn + right * tile_c, LANES)
                    part = pltpu.roll(power[first:last, :], turn, 1)
                    add_window(acc, 2, (at, base, turn), lane >= turn, part, tiles)

                return carry

            @pl.when(bits != 0)
            def _():
                lax.fori_loop(0, MARKS, step, 0)


def windows_after(
    slots, cells, acc_in, probe_re, probe_im, table, frames, marks, by_inner, by_outer,
    acc, order, power, whole, places, sem,
):
    rows, width = acc.shape[1:]
    before, after = received(by_inner, by_outer, "col")
    for i, part in enumerate((before[-MARKS:], marks[...], after[-MARKS:])):
        whole[i] = reaching(part, i - 1, rows - 2 * HALO, width - 2 * LANES)
    copy = pltpu.make_async_copy(whole, places, sem)
    copy.start()
    power[...] = probe_re[...] * probe_re[...] + probe_im[...] * probe_im[...]
    run_windows(
        lambda over, seen, limit: ~over & (seen >= limit),
        slots, cells, acc, probe_re, probe_im, table, frames, order,
    )
    copy.wait()
    add_neighbours_light(places, acc, power)


def windows_over_edge(
    slots, cells_in, acc_in, probe_re, probe_im, table, frames, by_inner, by_outer,
    cells, acc, to_inner, to_outer, order, strip,
):
    rows, width = acc.shape[1:]
    before, after = received(by_inner, by_outer, "col")
    for layer, row, part in pieces(before, 2, rows):
        cells[layer, row : row + part.shape[0], 0:LANES] = part
    for layer, row, part in pieces(after, 2, rows):
        cells[layer, row : row + part.shape[0], width - LANES :] = part
    run_windows(
        lambda over, seen, limit: over,
        slots, cells, acc, probe_re, probe_im, table, frames, order,
    )
    group_rows = 2 * rows // GROUPS
    fill_strip(strip, (acc[0, :, 0:LANES], acc[1, :, 0:LANES]))
    to_left = pack_lanes(strip, group_rows, LANES - HALO)
    fill_strip(strip, (acc[0, :, width - LANES :], acc[1, :, width - LANES :]))
    to_right = pack_lanes(strip, group_rows, 0)
    send_columns(to_left, to_right, to_inner, to_outer)


def row_spill(acc_in, by_inner, by_outer, acc, to_inner, to_outer):
    rows, width = acc.shape[1:]
    before, after = received(by_inner, by_outer, "col")
    lane = lane_index(rows)[0:1]
    for layer, row, part in pieces(before, 2, rows):
        here = slice(row, row + part.shape[0])
        acc[layer, here, LANES : 2 * LANES] += jnp.where(lane < HALO, part, 0.0)
    for layer, row, part in pieces(after, 2, rows):
        here = slice(row, row + part.shape[0])
        acc[layer, here, width - 2 * LANES : width - LANES] += jnp.where(lane >= LANES - HALO, part, 0.0)
    odd = is_odd("row")
    for k in (0, 1):
        up = acc[k, 0:HALO, LANES : width - LANES]
        down = acc[k, rows - HALO : rows, LANES : width - LANES]
        to_inner[k] = jnp.where(odd, up, down)
        to_outer[k] = jnp.where(odd, down, up)


def new_rows(cells, acc, extra, start, size, new_re, new_im):
    here = slice(HALO + start, HALO + start + size)
    middle = slice(LANES, acc.shape[2] - LANES)
    part = [acc[k, here, middle] for k in range(acc.shape[0])]
    if extra is not None:
        part[:2] = [part[k] + extra[k] for k in (0, 1)]
    scale = 1.0 / (part[2] + ridge)
    new_re[start : start + size, :] = cells[0, here, middle] - part[0] * scale
    new_im[start : start + size, :] = cells[1, here, middle] - part[1] * scale


def finish_inner(cells, acc, new_re, new_im, near_re, near_im, sems):
    tile_r = near_re.shape[0]
    new_rows(cells, acc, None, HALO, tile_r - 2 * HALO, near_re, near_im)
    rows = slice(HALO, tile_r - HALO)
    finish_all(fetch([(near_re.at[rows], new_re.at[rows]), (near_im.at[rows], new_im.at[rows])], sems))


def finish_edges(cells, acc, by_inner, by_outer, re_in, im_in, new_re, new_im, near_re, near_im, sems):
    tile_r = near_re.shape[0]
    copies = []
    for i, (start, extra) in enumerate(zip((0, tile_r - HALO), received(by_inner, by_outer, "row"))):
        new_rows(cells, acc, extra, start, HALO, near_re, near_im)
        rows = slice(start, start + HALO)
        pairs = ((near_re.at[rows], new_re.at[rows]), (near_im.at[rows], new_im.at[rows]))
        copies += fetch(pairs, sems.at[2 * i : 2 * i + 2])
    finish_all(copies)


def swap(to_inner, to_outer, axis, gather):
    devices = lax.axis_size(axis)
    inner = [(i, i + 1) for i in range(0, devices, 2)]
    partner = {i: i + 1 if i % 2 else i - 1 for i in range(1, devices - 1)}
    n_row, n_col = lax.axis_size("row"), lax.axis_size("col")
    pairs = []
    for row in range(n_row):
        for col in range(n_col):
            if axis == "row":
                there = (partner[row], col) if row in partner else (row, col ^ 1)
            else:
                there = (row, partner[col]) if col in partner else (row ^ 1, col)
            pairs.append((row * n_col + col, there[0] * n_col + there[1]))
    by_outer = lax.ppermute(to_outer, ("row", "col"), pairs)
    if gather:
        by_inner = lax.all_gather(to_inner, axis, axis_index_groups=[list(pair) for pair in inner])
    else:
        by_inner = lax.ppermute(to_inner, axis, inner + [(j, i) for i, j in inner])
    return by_inner, by_outer


def far(x):
    return pltpu.with_memory_space_constraint(x, pltpu.HBM)


def f32(*shape):
    return jax.ShapeDtypeStruct(shape, jnp.float32)


def shards(object_re, object_im, probe_re, probe_im, frames, counts, offsets, frame_index):
    tile_r, tile_c = object_re.shape
    rows, width = tile_r + 2 * HALO, tile_c + 2 * LANES
    layers = 3
    slots = offsets.shape[2]
    table = jnp.asarray(transform_tables())
    frames = frames.reshape(frames.shape[2:])
    cells_shape, acc_shape = f32(2, rows, width), f32(layers, rows, width)
    dma = pltpu.SemaphoreType.DMA

    places = jnp.swapaxes(offsets, 2, 3)
    edge = f32(2 * HALO + MARKS, tile_c)
    to_inner, to_outer, marked = pl.pallas_call(
        row_edges,
        out_shape=(edge, edge, jax.ShapeDtypeStruct((3, slots), jnp.int32)),
        in_specs=[SMEM] + [HBM] * 4,
        out_specs=(VMEM, VMEM, VMEM),
        scratch_shapes=[
            pltpu.VMEM(places.shape, jnp.int32), pltpu.VMEM(frame_index.shape, jnp.int32), dma((6,)),
        ],
        compiler_params=SMALL,
        name="row_edges",
    )(counts, far(object_re), far(object_im), far(places), far(frame_index))
    by_inner, by_outer = swap(to_inner, to_outer, "row", True)

    cells, *fixed = pl.pallas_call(
        load_state,
        out_shape=(
            cells_shape, f32(*probe_re.shape), f32(*probe_im.shape),
            jax.ShapeDtypeStruct(table.shape, table.dtype), jax.ShapeDtypeStruct(frames.shape, frames.dtype),
        ),
        in_specs=[HBM] * 6,
        out_specs=(VMEM,) * 5,
        scratch_shapes=[dma((6,))],
        compiler_params=SMALL,
        cost_estimate=BUSY,
        name="load_state",
    )(*map(far, (object_re, object_im, probe_re, probe_im, table, frames)))

    strip = pltpu.VMEM((2 * rows, LANES), jnp.float32)
    packed = f32(2 * rows // GROUPS + MARKS, LANES)
    cells, marks, to_inner, to_outer = pl.pallas_call(
        row_halos,
        out_shape=(cells_shape, f32(MARKS, LANES), packed, packed),
        in_specs=[VMEM] * 4,
        out_specs=(VMEM,) * 4,
        scratch_shapes=[strip],
        input_output_aliases={0: 0},
        compiler_params=SMALL,
        name="row_halos",
    )(cells, to_outer, by_inner, by_outer)
    edges = swap(to_inner, to_outer, "col", False)

    order = pltpu.SMEM((slots,), jnp.int32)
    acc = pl.pallas_call(
        windows_before,
        out_shape=acc_shape,
        in_specs=[SMEM] + [VMEM] * 5,
        out_specs=VMEM,
        scratch_shapes=[order, pltpu.VMEM(probe_re.shape, jnp.float32)],
        compiler_params=PARAMS,
        cost_estimate=BUSY,
        name="windows_before",
    )(marked, cells, *fixed)

    packed = f32(2 * rows // GROUPS, LANES)
    cells, acc, to_inner, to_outer = pl.pallas_call(
        windows_over_edge,
        out_shape=(cells_shape, acc_shape, packed, packed),
        in_specs=[SMEM] + [VMEM] * 8,
        out_specs=(VMEM,) * 4,
        scratch_shapes=[order, strip],
        input_output_aliases={1: 0, 2: 1},
        compiler_params=PARAMS,
        cost_estimate=BUSY,
        name="windows_over_edge",
    )(marked, cells, acc, *fixed, *edges)
    by_inner, by_outer = swap(to_inner, to_outer, "col", False)

    acc = pl.pallas_call(
        windows_after,
        out_shape=acc_shape,
        in_specs=[SMEM] + [VMEM] * 9,
        out_specs=VMEM,
        scratch_shapes=[
            order, pltpu.VMEM(probe_re.shape, jnp.float32),
            pltpu.VMEM((3, MARKS, LANES), jnp.int32), pltpu.SMEM((3, MARKS, LANES), jnp.int32), dma(()),
        ],
        input_output_aliases={2: 0},
        compiler_params=PARAMS,
        cost_estimate=BUSY,
        name="windows_after",
    )(marked, cells, acc, *fixed, marks, *edges)

    edge = f32(2, HALO, tile_c)
    acc, to_inner, to_outer = pl.pallas_call(
        row_spill,
        out_shape=(acc_shape, edge, edge),
        in_specs=[VMEM] * 3,
        out_specs=(VMEM,) * 3,
        input_output_aliases={0: 0},
        compiler_params=SMALL,
        name="row_spill",
    )(acc, by_inner, by_outer)
    by_inner, by_outer = swap(to_inner, to_outer, "row", True)

    near = [pltpu.VMEM((tile_r, tile_c), jnp.float32)] * 2
    new = (f32(tile_r, tile_c), f32(tile_r, tile_c))
    new_re, new_im = pl.pallas_call(
        finish_inner,
        out_shape=new,
        in_specs=[VMEM] * 2,
        out_specs=(HBM, HBM),
        scratch_shapes=near + [dma((2,))],
        compiler_params=SMALL,
        cost_estimate=BUSY,
        name="finish_inner",
    )(cells, acc)
    return pl.pallas_call(
        finish_edges,
        out_shape=new,
        in_specs=[VMEM] * 4 + [HBM] * 2,
        out_specs=(HBM, HBM),
        scratch_shapes=near + [dma((4,))],
        input_output_aliases={4: 0, 5: 1},
        compiler_params=SMALL,
        name="finish_edges",
    )(cells, acc, by_inner, by_outer, far(new_re), far(new_im))


def solution(mesh):
    return jax.shard_map(
        shards,
        mesh=mesh,
        in_specs=(
            P("row", "col"),
            P("row", "col"),
            P(),
            P(),
            P("row", "col", None, None, None),
            P("row", "col"),
            P("row", "col", None, None),
            P("row", "col", None),
        ),
        out_specs=(P("row", "col"), P("row", "col")),
        check_vma=False,
    )
```

profile of v0, /device:TPU:0, one launch (start us, length us, event | category | flops | bytes accessed | tf_op | source)
XLA Modules:
  0.0 34.0 jit_solution(5414508871926638715)
XLA Ops:
  1.3 1.0 %row_edges.1 = (f32[72,512]{1,0:T(8,128)S(1)}, f32[72,512]{1,0:T(8,128)S(1)}, s32[3,8]{1,0:T(4,128)S(1)}) custom-call(s32[1,1]{1,0:T(1,128)S(6)} %copy.25.counts, f32[384,512]{1,0:T(8,128)} %obj_re.3, f32[384,512]{1,0:T(8,128)} %obj_im.3, s32[1,1,2,8]{3,2,1,0:T(2,128)} %bitcast.6, s32[1,1,8]{2,1,0:T(1,128)} %chosen.1), custom_call_target="tpu_custom_call" | custom-call | tf_op jit(solution)/shard_map/row_edges/pallas_call | solution.py:564
  2.3 3.1 %collective-permute-start = (f32[72,512]{1,0:T(8,128)S(1)}, f32[72,512]{1,0:T(8,128)S(1)}, u32[]{:S(2)}, u32[]{:S(2)}) collective-permute-start(f32[72,512]{1,0:T(8,128)S(1)} %get-tuple-element.25.own), channel_id=1, source_target_pairs={{0,1},{1,0},{2,3},{3,2},{4,8},{5,9},{6,10},{7,11},{8,4},{9,5},{10,... | collective-permute-start | bytes 442376 | tf_op jit(solution)/shard_map/ppermute | solution.py:536
  5.4 2.3 %load_state.1 = (f32[2,448,768]{2,1,0:T(8,128)S(1)}, f32[256,256]{1,0:T(8,128)S(1)}, f32[256,256]{1,0:T(8,128)S(1)}, bf16[10,256,256]{2,1,0:T(8,128)(2,1)S(1)}, bf16[8,256,256]{2,1,0:T(8,128)(2,1)S(1)}) custom-call(f32[384,512]{1,0:T(8,128)} %obj_re.3, f32[384,512]{1,0:T(8,128)} %obj_im.3, f32[256,256]{1,0:T(8,128)} %probe_re_far.1, ...), custom_call_target="tpu_custom_call" | custom-call | flops 4000000000 | bytes 8000000 | tf_op jit(solution)/shard_map/load_state/pallas_call | solution.py:577
  7.7 2.0 %all-gather = f32[144,512]{1,0:T(8,128)S(1)} all-gather(f32[72,512]{1,0:T(8,128)S(1)} %get-tuple-element.26), channel_id=2, replica_groups={{0,4},{8,12},{16,20},{24,28},{1,5},{9,13},{17,21},{25,29},{2,6},{10,14}..., dimensions={0}, use_global_device_ids=true | all-gather | bytes 442368 | tf_op jit(solution)/shard_map/all_gather | solution.py:538
  9.7 0.0 collective-permute-done.by_outer
  9.7 0.3 row_halos.1
  10.0 1.3 %collective-permute-start.1 = (f32[232,128]{1,0:T(8,128)S(1)}, f32[232,128]{1,0:T(8,128)S(1)}, u32[]{:S(2)}, u32[]{:S(2)}) collective-permute-start(f32[232,128]{1,0:T(8,128)S(1)} %get-tuple-element.32), channel_id=1, source_target_pairs={{0,1},{2,3},{1,0},{3,2},{4,5},{6,7},{5,4},{7,6},{8,9},{10,11},{9,8... | collective-permute-start | bytes 356360 | tf_op jit(solution)/shard_map/ppermute | solution.py:540
  11.3 0.1 collective-permute-start.2
  11.3 3.6 %windows_before.1.acc_in = f32[3,448,768]{2,1,0:T(8,128)S(1)} custom-call(s32[3,8]{1,0:T(4,128)S(1)} %get-tuple-element.23.slots, f32[2,448,768]{2,1,0:T(8,128)S(1)} %get-tuple-element.27.cells.cells_in, f32[256,256]{1,0:T(8,128)S(1)} %get-tuple-element.28.probe_re, f32[256,256]{1,0:T(8,128)S(1)} %get-tuple-element.29.probe_im, ...), custom_call_target="tpu_custom_call" | custom-call | flops 4000000000 | bytes 8000000 | tf_op jit(solution)/shard_map/windows_before/pallas_call | solution.py:606
  15.0 0.3 %collective-permute-done.1.by_inner = f32[232,128]{1,0:T(8,128)S(1)} collective-permute-done((f32[232,128]{1,0:T(8,128)S(1)}, f32[232,128]{1,0:T(8,128)S(1)}, u32[]{:S(2)}, u32[]{:S(2)}) %collective-permute-start.1) | collective-permute-done | bytes 118816 | tf_op jit(solution)/shard_map/ppermute | solution.py:540
  15.3 0.0 collective-permute-done.2.by_outer
  15.3 1.1 %windows_over_edge.1 = (f32[2,448,768]{2,1,0:T(8,128)S(1)}, f32[3,448,768]{2,1,0:T(8,128)S(1)}, f32[224,128]{1,0:T(8,128)S(1)}, f32[224,128]{1,0:T(8,128)S(1)}) custom-call(s32[3,8]{1,0:T(4,128)S(1)} %get-tuple-element.23.slots, f32[2,448,768]{2,1,0:T(8,128)S(1)} %get-tuple-element.27.cells.cells_in, ...), custom_call_target="tpu_custom_call", output_to_operand_aliasing={{0}: (1, {}), {1}: (2, {})} | custom-call | flops 4000000000 | bytes 8000000 | tf_op jit(solution)/shard_map/windows_over_edge/pallas_call | solution.py:618
  16.4 8.0 %collective-permute-start.3 = (f32[224,128]{1,0:T(8,128)S(1)}, f32[224,128]{1,0:T(8,128)S(1)}, u32[]{:S(2)}, u32[]{:S(2)}) collective-permute-start(f32[224,128]{1,0:T(8,128)S(1)} %get-tuple-element.37), channel_id=1, source_target_pairs={{0,1},{2,3},{1,0},{3,2},{4,5},{6,7},{5,4},{7,6},{8,9},{10,11},{9,8... | collective-permute-start | bytes 344072 | tf_op jit(solution)/shard_map/ppermute | solution.py:540
  24.4 0.0 collective-permute-start.4
  24.4 1.7 %windows_after.1.acc_in = f32[3,448,768]{2,1,0:T(8,128)S(1)} custom-call(s32[3,8]{1,0:T(4,128)S(1)} %get-tuple-element.23.slots, f32[2,448,768]{2,1,0:T(8,128)S(1)} %get-tuple-element.34.cells, f32[3,448,768]{2,1,0:T(8,128)S(1)} %get-tuple-element.35.acc_in, f32[256,256]{1,0:T(8,128)S(1)} %get-tuple-element.28.probe_re, ...), custom_call_target="tpu_custom_call", output_to_operand_aliasing={{}: (2, {})} | custom-call | flops 4000000000 | bytes 8000000 | tf_op jit(solution)/shard_map/windows_after/pallas_call | solution.py:631
  26.1 1.0 %collective-permute-done.3.by_inner = f32[224,128]{1,0:T(8,128)S(1)} collective-permute-done((f32[224,128]{1,0:T(8,128)S(1)}, f32[224,128]{1,0:T(8,128)S(1)}, u32[]{:S(2)}, u32[]{:S(2)}) %collective-permute-start.3) | collective-permute-done | bytes 114720 | tf_op jit(solution)/shard_map/ppermute | solution.py:540
  27.2 0.0 collective-permute-done.4.by_outer
  27.2 0.3 row_spill.1
  27.4 2.6 %collective-permute-start.5 = (f32[2,32,512]{2,1,0:T(8,128)S(1)}, f32[2,32,512]{2,1,0:T(8,128)S(1)}, u32[]{:S(2)}, u32[]{:S(2)}) collective-permute-start(f32[2,32,512]{2,1,0:T(8,128)S(1)} %get-tuple-element.41), channel_id=1, source_target_pairs={{0,1},{1,0},{2,3},{3,2},{4,8},{5,9},{6,10},{7,11},{8,4},{9,5},{10,... | collective-permute-start | bytes 393224 | tf_op jit(solution)/shard_map/ppermute | solution.py:536
  30.0 1.2 %finish_inner.1 = (f32[384,512]{1,0:T(8,128)}, f32[384,512]{1,0:T(8,128)}) custom-call(f32[2,448,768]{2,1,0:T(8,128)S(1)} %get-tuple-element.34.cells, f32[3,448,768]{2,1,0:T(8,128)S(1)} %get-tuple-element.39.acc), custom_call_target="tpu_custom_call" | custom-call | flops 4000000000 | bytes 8000000 | tf_op jit(solution)/shard_map/finish_inner/pallas_call | solution.py:660
  31.2 2.0 %all-gather.1 = f32[4,32,512]{2,1,0:T(8,128)S(1)} all-gather(f32[2,32,512]{2,1,0:T(8,128)S(1)} %get-tuple-element.40), channel_id=3, replica_groups={{0,4},{8,12},{16,20},{24,28},{1,5},{9,13},{17,21},{25,29},{2,6},{10,14}..., dimensions={0}, use_global_device_ids=true | all-gather | bytes 393216 | tf_op jit(solution)/shard_map/all_gather | solution.py:538
  33.2 0.0 collective-permute-done.5.by_outer
  33.2 0.8 %finish_edges.1 = (f32[384,512]{1,0:T(8,128)}, f32[384,512]{1,0:T(8,128)}) custom-call(f32[2,448,768]{2,1,0:T(8,128)S(1)} %get-tuple-element.34.cells, f32[3,448,768]{2,1,0:T(8,128)S(1)} %get-tuple-element.39.acc, f32[2,2,32,512]{3,2,1,0:T(8,128)S(1)} %bitcast.5, ...), custom_call_target="tpu_custom_call", output_to_operand_aliasing={{0}: (4, {}), {1}: (5, {})} | custom-call | tf_op jit(solution)/shard_map/finish_edges/pallas_call | solution.py:670
Async XLA Ops:
  2.3 7.4 %collective-permute-start = (f32[72,512]{1,0:T(8,128)S(1)}, f32[72,512]{1,0:T(8,128)S(1)}, u32[]{:S(2)}, u32[]{:S(2)}) collective-permute-start(f32[72,512]{1,0:T(8,128)S(1)} %get-tuple-element.25.own), channel_id=1, source_target_pairs={{0,1},{1,0},{2,3},{3,2},{4,8},{5,9},{6,10},{7,11},{8,4},{9,5},{10,... | collective-permute-start | bytes 442376 | tf_op jit(solution)/shard_map/ppermute | solution.py:536
  10.0 5.4 %collective-permute-start.1 = (f32[232,128]{1,0:T(8,128)S(1)}, f32[232,128]{1,0:T(8,128)S(1)}, u32[]{:S(2)}, u32[]{:S(2)}) collective-permute-start(f32[232,128]{1,0:T(8,128)S(1)} %get-tuple-element.32), channel_id=1, source_target_pairs={{0,1},{2,3},{1,0},{3,2},{4,5},{6,7},{5,4},{7,6},{8,9},{10,11},{9,8... | collective-permute-start | bytes 356360 | tf_op jit(solution)/shard_map/ppermute | solution.py:540
  11.3 4.0 %collective-permute-start.2 = (f32[232,128]{1,0:T(8,128)S(1)}, f32[232,128]{1,0:T(8,128)S(1)}, u32[]{:S(2)}, u32[]{:S(2)}) collective-permute-start(f32[232,128]{1,0:T(8,128)S(1)} %get-tuple-element.33), channel_id=1, source_target_pairs={{0,4},{1,2},{2,1},{3,7},{4,0},{5,6},{6,5},{7,3},{8,12},{9,10},{10,... | collective-permute-start | bytes 356360 | tf_op jit(solution)/shard_map/ppermute | solution.py:536
  16.4 10.8 %collective-permute-start.3 = (f32[224,128]{1,0:T(8,128)S(1)}, f32[224,128]{1,0:T(8,128)S(1)}, u32[]{:S(2)}, u32[]{:S(2)}) collective-permute-start(f32[224,128]{1,0:T(8,128)S(1)} %get-tuple-element.37), channel_id=1, source_target_pairs={{0,1},{2,3},{1,0},{3,2},{4,5},{6,7},{5,4},{7,6},{8,9},{10,11},{9,8... | collective-permute-start | bytes 344072 | tf_op jit(solution)/shard_map/ppermute | solution.py:540
  24.4 2.8 %collective-permute-start.4 = (f32[224,128]{1,0:T(8,128)S(1)}, f32[224,128]{1,0:T(8,128)S(1)}, u32[]{:S(2)}, u32[]{:S(2)}) collective-permute-start(f32[224,128]{1,0:T(8,128)S(1)} %get-tuple-element.38), channel_id=1, source_target_pairs={{0,4},{1,2},{2,1},{3,7},{4,0},{5,6},{6,5},{7,3},{8,12},{9,10},{10,... | collective-permute-start | bytes 344072 | tf_op jit(solution)/shard_map/ppermute | solution.py:536
  27.4 5.8 %collective-permute-start.5 = (f32[2,32,512]{2,1,0:T(8,128)S(1)}, f32[2,32,512]{2,1,0:T(8,128)S(1)}, u32[]{:S(2)}, u32[]{:S(2)}) collective-permute-start(f32[2,32,512]{2,1,0:T(8,128)S(1)} %get-tuple-element.41), channel_id=1, source_target_pairs={{0,1},{1,0},{2,3},{3,2},{4,8},{5,9},{6,10},{7,11},{8,4},{9,5},{10,... | collective-permute-start | bytes 393224 | tf_op jit(solution)/shard_map/ppermute | solution.py:536
where the time goes:
time: 33.4 us; the launch traced here: 34 us
  starting transfers between devices  15.1 us (45%)
  Pallas kernels  12.2 us (37%)
  blocking collectives  4.01 us (12%)
  waiting for transfers between devices  1.38 us (4%)
  between operations  1.34 us (4%)
    ppermute x2, starting transfers between devices, swap(): by_inner = lax.ppermute(to_inner, axis, inner + [(j, i) for i, j in inner])  9.33 us
    ppermute x4, starting transfers between devices, swap(): by_outer = lax.ppermute(to_outer, ('row', 'col'), pairs)  5.73 us
    all_gather x2, blocking collectives, swap(): lax.all_gather(to_inner, axis, axis_index_groups=[list(pair) for pair in...  4.01 us
    pallas_call x1, Pallas kernels, shards(): pl.pallas_call(windows_before, out_shape=acc_shape, in_specs=[SMEM] + [VM...  3.6 us
    pallas_call x1, Pallas kernels, shards(): pl.pallas_call(load_state, out_shape=(cells_shape, f32(*probe_re.shape),...  2.26 us
    pallas_call x1, Pallas kernels, shards(): pl.pallas_call(windows_after, out_shape=acc_shape, in_specs=[SMEM] + [VME...  1.74 us
    ppermute x2, waiting for transfers between devices, swap(): by_inner = lax.ppermute(to_inner, axis, inner + [(j, i) for i, j in inner])  1.37 us
    pallas_call x1, Pallas kernels, shards(): pl.pallas_call(finish_inner, out_shape=new, in_specs=[VMEM] * 2, out_spec...  1.21 us
  transfers between devices with their start and end apart: 6, of which 2 were waited for; matrix products, arithmetic and copies ran while one was open for 0% of the time, Pallas kernels for 26%

commit v1 on v0

--- a/solution.py
+++ b/solution.py
@@ -81,13 +81,13 @@
 def times_table(x, table, which):
     high, low = split(x)
     t_high, t_low = table[2 * which], table[2 * which + 1]
-    return product(high, t_high) + (product(high, t_low) + product(low, t_high))
+    return product(beside(high, high, low), below(t_high, t_low, t_high))
 
 
 def table_times(table, which, x):
     high, low = split(x)
     t_high, t_low = table[2 * which], table[2 * which + 1]
-    return product(t_high, high) + (product(t_low, high) + product(t_high, low))
+    return product(beside(t_high, t_low, t_high), below(high, high, low))
 
 
 def beside(*blocks):
@@ -224,7 +224,16 @@
         (probe_re_far, probe_re),
         (probe_im_far, probe_im),
     )
-    finish_all(fetch(pairs, sems))
+    copies = fetch(pairs, sems)
+    finish_all(copies[:2])
+
+    def sort(i, carry):
+        half = product(table[8], frames[i]).astype(jnp.bfloat16)
+        frames[i] = product(half, table[9]).astype(jnp.bfloat16)
+        return carry
+
+    lax.fori_loop(0, frames.shape[0], sort, 0, unroll=2)
+    finish_all(copies[2:])
 
 
 def fill_strip(strip, parts):
@@ -335,9 +344,7 @@
         return (where, keep, w_re, w_im), exit_re, exit_im
 
     def frame_of(slot):
-        sort, unsort = table[8], table[9]
-        half = product(sort, frames[slots[2, slot]]).astype(jnp.bfloat16)
-        return product(half, unsort)
+        return frames[slots[2, slot]].astype(jnp.float32)
 
     def place(at, back_re, back_im):
         where, keep, w_re, w_im = at

time: 33.4 us -> 32.6 us (0.976)
  the two profiles are of different devices: /device:TPU:0 before, /device:TPU:20 now
where the time goes in v1:
time: 32.6 us; the launch traced here: 32.9 us
  Pallas kernels  20.2 us (62%)
  blocking collectives  4.38 us (13%)
  waiting for transfers between devices  3.5 us (11%)
  starting transfers between devices  3.46 us (11%)
  between operations  1.38 us (4%)
    pallas_call x1, Pallas kernels, shards(): pl.pallas_call(windows_after, out_shape=acc_shape, in_specs=[SMEM] + [VME...  6.07 us
    pallas_call x1, Pallas kernels, shards(): pl.pallas_call(windows_before, out_shape=acc_shape, in_specs=[SMEM] + [VM...  4.48 us
    all_gather x2, blocking collectives, swap(): lax.all_gather(to_inner, axis, axis_index_groups=[list(pair) for pair in...  4.38 us
    ppermute x4, waiting for transfers between devices, swap(): by_outer = lax.ppermute(to_outer, ('row', 'col'), pairs)  3.49 us
    pallas_call x1, Pallas kernels, shards(): pl.pallas_call(load_state, out_shape=(cells_shape, f32(*probe_re.shape),...  3.32 us
    pallas_call x1, Pallas kernels, shards(): pl.pallas_call(windows_over_edge, out_shape=(cells_shape, acc_shape, pack...  2.82 us
    ppermute x4, starting transfers between devices, swap(): by_outer = lax.ppermute(to_outer, ('row', 'col'), pairs)  1.73 us
    ppermute x2, starting transfers between devices, swap(): by_inner = lax.ppermute(to_inner, axis, inner + [(j, i) for i, j in inner])  1.73 us
  transfers between devices with their start and end apart: 6, of which 2 were waited for; matrix products, arithmetic and copies ran while one was open for 0% of the time, Pallas kernels for 46%

profile of v1, /device:TPU:20, one launch (start us, length us, event | category | flops | bytes accessed | tf_op | source)
XLA Modules:
  0.0 32.9 jit_solution(17177739650453291056)
XLA Ops:
  1.3 1.0 %row_edges.1 = (f32[72,512]{1,0:T(8,128)S(1)}, f32[72,512]{1,0:T(8,128)S(1)}, s32[3,8]{1,0:T(4,128)S(1)}) custom-call(s32[1,1]{1,0:T(1,128)S(6)} %copy.25.counts, f32[384,512]{1,0:T(8,128)} %obj_re.3, f32[384,512]{1,0:T(8,128)} %obj_im.3, s32[1,1,2,8]{3,2,1,0:T(2,128)} %bitcast.6, s32[1,1,8]{2,1,0:T(1,128)} %chosen.1), custom_call_target="tpu_custom_call" | custom-call | tf_op jit(solution)/shard_map/row_edges/pallas_call | solution.py:571
  2.3 0.9 %collective-permute-start = (f32[72,512]{1,0:T(8,128)S(1)}, f32[72,512]{1,0:T(8,128)S(1)}, u32[]{:S(2)}, u32[]{:S(2)}) collective-permute-start(f32[72,512]{1,0:T(8,128)S(1)} %get-tuple-element.25.own), channel_id=1, source_target_pairs={{0,1},{1,0},{2,3},{3,2},{4,8},{5,9},{6,10},{7,11},{8,4},{9,5},{10,... | collective-permute-start | bytes 442376 | tf_op jit(solution)/shard_map/ppermute | solution.py:543
  3.2 3.3 %load_state.1 = (f32[2,448,768]{2,1,0:T(8,128)S(1)}, f32[256,256]{1,0:T(8,128)S(1)}, f32[256,256]{1,0:T(8,128)S(1)}, bf16[10,256,256]{2,1,0:T(8,128)(2,1)S(1)}, bf16[8,256,256]{2,1,0:T(8,128)(2,1)S(1)}) custom-call(f32[384,512]{1,0:T(8,128)} %obj_re.3, f32[384,512]{1,0:T(8,128)} %obj_im.3, f32[256,256]{1,0:T(8,128)} %probe_re_far.1, ...), custom_call_target="tpu_custom_call" | custom-call | flops 4000000000 | bytes 8000000 | tf_op jit(solution)/shard_map/load_state/pallas_call | solution.py:584
  6.6 2.4 %all-gather = f32[144,512]{1,0:T(8,128)S(1)} all-gather(f32[72,512]{1,0:T(8,128)S(1)} %get-tuple-element.26), channel_id=2, replica_groups={{0,4},{8,12},{16,20},{24,28},{1,5},{9,13},{17,21},{25,29},{2,6},{10,14}..., dimensions={0}, use_global_device_ids=true | all-gather | bytes 442368 | tf_op jit(solution)/shard_map/all_gather | solution.py:545
  9.0 0.0 collective-permute-done.by_outer
  9.0 0.3 row_halos.1
  9.2 1.7 %collective-permute-start.1 = (f32[232,128]{1,0:T(8,128)S(1)}, f32[232,128]{1,0:T(8,128)S(1)}, u32[]{:S(2)}, u32[]{:S(2)}) collective-permute-start(f32[232,128]{1,0:T(8,128)S(1)} %get-tuple-element.32), channel_id=1, source_target_pairs={{0,1},{2,3},{1,0},{3,2},{4,5},{6,7},{5,4},{7,6},{8,9},{10,11},{9,8... | collective-permute-start | bytes 356360 | tf_op jit(solution)/shard_map/ppermute | solution.py:547
  10.9 0.0 collective-permute-start.2
  10.9 4.5 %windows_before.1.acc_in = f32[3,448,768]{2,1,0:T(8,128)S(1)} custom-call(s32[3,8]{1,0:T(4,128)S(1)} %get-tuple-element.23.slots, f32[2,448,768]{2,1,0:T(8,128)S(1)} %get-tuple-element.27.cells.cells_in, f32[256,256]{1,0:T(8,128)S(1)} %get-tuple-element.28.probe_re, f32[256,256]{1,0:T(8,128)S(1)} %get-tuple-element.29.probe_im, ...), custom_call_target="tpu_custom_call" | custom-call | flops 4000000000 | bytes 8000000 | tf_op jit(solution)/shard_map/windows_before/pallas_call | solution.py:613
  15.4 0.0 collective-permute-done.1.by_inner
  15.4 0.7 %collective-permute-done.2.by_outer = f32[232,128]{1,0:T(8,128)S(1)} collective-permute-done((f32[232,128]{1,0:T(8,128)S(1)}, f32[232,128]{1,0:T(8,128)S(1)}, u32[]{:S(2)}, u32[]{:S(2)}) %collective-permute-start.2) | collective-permute-done | bytes 118816 | tf_op jit(solution)/shard_map/ppermute | solution.py:543
  16.1 2.8 %windows_over_edge.1 = (f32[2,448,768]{2,1,0:T(8,128)S(1)}, f32[3,448,768]{2,1,0:T(8,128)S(1)}, f32[224,128]{1,0:T(8,128)S(1)}, f32[224,128]{1,0:T(8,128)S(1)}) custom-call(s32[3,8]{1,0:T(4,128)S(1)} %get-tuple-element.23.slots, f32[2,448,768]{2,1,0:T(8,128)S(1)} %get-tuple-element.27.cells.cells_in, ...), custom_call_target="tpu_custom_call", output_to_operand_aliasing={{0}: (1, {}), {1}: (2, {})} | custom-call | flops 4000000000 | bytes 8000000 | tf_op jit(solution)/shard_map/windows_over_edge/pallas_call | solution.py:625
  18.9 0.1 collective-permute-start.3
  19.0 0.7 %collective-permute-start.4 = (f32[224,128]{1,0:T(8,128)S(1)}, f32[224,128]{1,0:T(8,128)S(1)}, u32[]{:S(2)}, u32[]{:S(2)}) collective-permute-start(f32[224,128]{1,0:T(8,128)S(1)} %get-tuple-element.38), channel_id=1, source_target_pairs={{0,4},{1,2},{2,1},{3,7},{4,0},{5,6},{6,5},{7,3},{8,12},{9,10},{10,... | collective-permute-start | bytes 344072 | tf_op jit(solution)/shard_map/ppermute | solution.py:543
  19.7 6.1 %windows_after.1.acc_in = f32[3,448,768]{2,1,0:T(8,128)S(1)} custom-call(s32[3,8]{1,0:T(4,128)S(1)} %get-tuple-element.23.slots, f32[2,448,768]{2,1,0:T(8,128)S(1)} %get-tuple-element.34.cells, f32[3,448,768]{2,1,0:T(8,128)S(1)} %get-tuple-element.35.acc_in, f32[256,256]{1,0:T(8,128)S(1)} %get-tuple-element.28.probe_re, ...), custom_call_target="tpu_custom_call", output_to_operand_aliasing={{}: (2, {})} | custom-call | flops 4000000000 | bytes 8000000 | tf_op jit(solution)/shard_map/windows_after/pallas_call | solution.py:638
  25.8 0.0 collective-permute-done.3.by_inner
  25.8 0.0 collective-permute-done.4.by_outer
  25.8 0.3 row_spill.1
  26.1 0.1 collective-permute-start.5
  26.2 1.2 %finish_inner.1 = (f32[384,512]{1,0:T(8,128)}, f32[384,512]{1,0:T(8,128)}) custom-call(f32[2,448,768]{2,1,0:T(8,128)S(1)} %get-tuple-element.34.cells, f32[3,448,768]{2,1,0:T(8,128)S(1)} %get-tuple-element.39.acc), custom_call_target="tpu_custom_call" | custom-call | flops 4000000000 | bytes 8000000 | tf_op jit(solution)/shard_map/finish_inner/pallas_call | solution.py:667
  27.4 2.0 %all-gather.1 = f32[4,32,512]{2,1,0:T(8,128)S(1)} all-gather(f32[2,32,512]{2,1,0:T(8,128)S(1)} %get-tuple-element.40), channel_id=3, replica_groups={{0,4},{8,12},{16,20},{24,28},{1,5},{9,13},{17,21},{25,29},{2,6},{10,14}..., dimensions={0}, use_global_device_ids=true | all-gather | bytes 393216 | tf_op jit(solution)/shard_map/all_gather | solution.py:545
  29.4 2.8 %collective-permute-done.5.by_outer = f32[2,32,512]{2,1,0:T(8,128)S(1)} collective-permute-done((f32[2,32,512]{2,1,0:T(8,128)S(1)}, f32[2,32,512]{2,1,0:T(8,128)S(1)}, u32[]{:S(2)}, u32[]{:S(2)}) %collective-permute-start.5) | collective-permute-done | bytes 131104 | tf_op jit(solution)/shard_map/ppermute | solution.py:543
  32.2 0.8 %finish_edges.1 = (f32[384,512]{1,0:T(8,128)}, f32[384,512]{1,0:T(8,128)}) custom-call(f32[2,448,768]{2,1,0:T(8,128)S(1)} %get-tuple-element.34.cells, f32[3,448,768]{2,1,0:T(8,128)S(1)} %get-tuple-element.39.acc, f32[2,2,32,512]{3,2,1,0:T(8,128)S(1)} %bitcast.5, ...), custom_call_target="tpu_custom_call", output_to_operand_aliasing={{0}: (4, {}), {1}: (5, {})} | custom-call | tf_op jit(solution)/shard_map/finish_edges/pallas_call | solution.py:677
Async XLA Ops:
  2.3 6.7 %collective-permute-start = (f32[72,512]{1,0:T(8,128)S(1)}, f32[72,512]{1,0:T(8,128)S(1)}, u32[]{:S(2)}, u32[]{:S(2)}) collective-permute-start(f32[72,512]{1,0:T(8,128)S(1)} %get-tuple-element.25.own), channel_id=1, source_target_pairs={{0,1},{1,0},{2,3},{3,2},{4,8},{5,9},{6,10},{7,11},{8,4},{9,5},{10,... | collective-permute-start | bytes 442376 | tf_op jit(solution)/shard_map/ppermute | solution.py:543
  9.2 6.1 %collective-permute-start.1 = (f32[232,128]{1,0:T(8,128)S(1)}, f32[232,128]{1,0:T(8,128)S(1)}, u32[]{:S(2)}, u32[]{:S(2)}) collective-permute-start(f32[232,128]{1,0:T(8,128)S(1)} %get-tuple-element.32), channel_id=1, source_target_pairs={{0,1},{2,3},{1,0},{3,2},{4,5},{6,7},{5,4},{7,6},{8,9},{10,11},{9,8... | collective-permute-start | bytes 356360 | tf_op jit(solution)/shard_map/ppermute | solution.py:547
  10.9 5.2 %collective-permute-start.2 = (f32[232,128]{1,0:T(8,128)S(1)}, f32[232,128]{1,0:T(8,128)S(1)}, u32[]{:S(2)}, u32[]{:S(2)}) collective-permute-start(f32[232,128]{1,0:T(8,128)S(1)} %get-tuple-element.33), channel_id=1, source_target_pairs={{0,4},{1,2},{2,1},{3,7},{4,0},{5,6},{6,5},{7,3},{8,12},{9,10},{10,... | collective-permute-start | bytes 356360 | tf_op jit(solution)/shard_map/ppermute | solution.py:543
  18.9 6.9 %collective-permute-start.3 = (f32[224,128]{1,0:T(8,128)S(1)}, f32[224,128]{1,0:T(8,128)S(1)}, u32[]{:S(2)}, u32[]{:S(2)}) collective-permute-start(f32[224,128]{1,0:T(8,128)S(1)} %get-tuple-element.37), channel_id=1, source_target_pairs={{0,1},{2,3},{1,0},{3,2},{4,5},{6,7},{5,4},{7,6},{8,9},{10,11},{9,8... | collective-permute-start | bytes 344072 | tf_op jit(solution)/shard_map/ppermute | solution.py:547
  19.0 6.8 %collective-permute-start.4 = (f32[224,128]{1,0:T(8,128)S(1)}, f32[224,128]{1,0:T(8,128)S(1)}, u32[]{:S(2)}, u32[]{:S(2)}) collective-permute-start(f32[224,128]{1,0:T(8,128)S(1)} %get-tuple-element.38), channel_id=1, source_target_pairs={{0,4},{1,2},{2,1},{3,7},{4,0},{5,6},{6,5},{7,3},{8,12},{9,10},{10,... | collective-permute-start | bytes 344072 | tf_op jit(solution)/shard_map/ppermute | solution.py:543
  26.1 6.1 %collective-permute-start.5 = (f32[2,32,512]{2,1,0:T(8,128)S(1)}, f32[2,32,512]{2,1,0:T(8,128)S(1)}, u32[]{:S(2)}, u32[]{:S(2)}) collective-permute-start(f32[2,32,512]{2,1,0:T(8,128)S(1)} %get-tuple-element.41), channel_id=1, source_target_pairs={{0,1},{1,0},{2,3},{3,2},{4,8},{5,9},{6,10},{7,11},{8,4},{9,5},{10,... | collective-permute-start | bytes 393224 | tf_op jit(solution)/shard_map/ppermute | solution.py:543

commit v2 on v0

--- a/solution.py
+++ b/solution.py
@@ -81,13 +81,13 @@
 def times_table(x, table, which):
     high, low = split(x)
     t_high, t_low = table[2 * which], table[2 * which + 1]
-    return product(high, t_high) + (product(high, t_low) + product(low, t_high))
+    return product(beside(high, high, low), below(t_high, t_low, t_high))
 
 
 def table_times(table, which, x):
     high, low = split(x)
     t_high, t_low = table[2 * which], table[2 * which + 1]
-    return product(t_high, high) + (product(t_low, high) + product(t_high, low))
+    return product(beside(t_high, t_low, t_high), below(high, high, low))
 
 
 def beside(*blocks):
@@ -209,24 +209,6 @@
         acc[layer, pl.ds(row, term.shape[0]), pl.ds(base + t * LANES, LANES)] += parts[t]
 
 
-def load_state(
-    obj_re, obj_im, probe_re_far, probe_im_far, table_far, frames_far,
-    cells, probe_re, probe_im, table, frames, sems,
-):
-    tile_r, tile_c = obj_re.shape
-    inner = slice(HALO, HALO + tile_r)
-    middle = slice(LANES, LANES + tile_c)
-    pairs = (
-        (table_far, table),
-        (frames_far, frames),
-        (obj_re, cells.at[0, inner, middle]),
-        (obj_im, cells.at[1, inner, middle]),
-        (probe_re_far, probe_re),
-        (probe_im_far, probe_im),
-    )
-    finish_all(fetch(pairs, sems))
-
-
 def fill_strip(strip, parts):
     done = 0
     for part in parts:
@@ -245,11 +227,8 @@
     index = lax.axis_index(axis)
     inside = (index > 0) & (index < lax.axis_size(axis) - 1)
     by_outer = jnp.where(inside, by_outer[...], 0.0)
-    if len(by_inner.shape) > len(by_outer.shape):
-        before, after = by_inner[0], by_inner[1]
-    else:
-        before = after = by_inner[...]
-    return jnp.where(odd, before, by_outer), jnp.where(odd, by_outer, after)
+    by_inner = by_inner[...]
+    return jnp.where(odd, by_inner, by_outer), jnp.where(odd, by_outer, by_inner)
 
 
 def pieces(packed, layers, rows):
@@ -293,28 +272,43 @@
     return count
 
 
-def run_windows(wanted, slots, cells, acc, probe_re, probe_im, table, frames, order):
-    tile_c = cells.shape[2] - 2 * LANES
+FIRST, BEFORE, OVER, AFTER, LAST = range(5)
+
+
+def run_windows(phase, slots, cells, acc, probe_re, probe_im, table, frames, order):
+    tile_r, tile_c = cells.shape[1] - 2 * HALO, cells.shape[2] - 2 * LANES
     count = live_slots(slots, cells)
-    every = range(slots.shape[1])
-    over = []
-    for slot in every:
-        col = slots[1, slot]
-        over.append((col < 0) | (col > tile_c - P_SIZE))
-    total = jnp.int32(0)
-    for slot in every:
-        total += ((slot < count) & ~over[slot]).astype(jnp.int32)
-    limit = jnp.where(total < len(every) - 1, PAIR, 2 * PAIR)
-    seen, found = jnp.int32(0), jnp.int32(0)
-    for slot in every:
+    kinds = []
+    n_inside, n_row = jnp.int32(0), jnp.int32(0)
+    for slot in range(slots.shape[1]):
+        row, col = slots[0, slot], slots[1, slot]
         live = slot < count
-        mine = live & wanted(over[slot], seen, limit)
+        over_col = (col < 0) | (col > tile_c - P_SIZE)
+        over_row = (row < 0) | (row > tile_r - P_SIZE)
+        inside, by_row = live & ~over_col & ~over_row, live & ~over_col & over_row
+        kinds.append((live & over_col, inside, by_row, n_inside, n_row))
+        n_inside += inside.astype(jnp.int32)
+        n_row += by_row.astype(jnp.int32)
+    first = jnp.minimum(n_inside, PAIR)
+    rest = n_inside - first + n_row
+    last = jnp.clip(rest - 2 * PAIR, 0, jnp.minimum(n_inside - first, PAIR))
+    before = jnp.minimum(rest - last, PAIR)
+    found = jnp.int32(0)
+    for slot, (over, inside, by_row, inside_rank, row_rank) in enumerate(kinds):
+        rank = jnp.where(by_row, row_rank, n_row + inside_rank - first)
+        later = by_row | (inside & (inside_rank >= first))
+        mine = {
+            FIRST: lambda: inside & (inside_rank < first),
+            BEFORE: lambda: later & (rank < before),
+            OVER: lambda: over,
+            AFTER: lambda: later & (rank >= before) & (rank < rest - last),
+            LAST: lambda: later & (rank >= rest - last),
+        }[phase]()
 
         @pl.when(mine)
         def _():
             order[found] = slot
 
-        seen += (live & ~over[slot]).astype(jnp.int32)
         found += mine.astype(jnp.int32)
 
     lane = lane_index(P_SIZE)
@@ -335,9 +329,8 @@
         return (where, keep, w_re, w_im), exit_re, exit_im
 
     def frame_of(slot):
-        sort, unsort = table[8], table[9]
-        half = product(sort, frames[slots[2, slot]]).astype(jnp.bfloat16)
-        return product(half, unsort)
+        half = product(table[8], frames[slots[2, slot]]).astype(jnp.bfloat16)
+        return product(half, table[9])
 
     def place(at, back_re, back_im):
         where, keep, w_re, w_im = at
@@ -366,10 +359,30 @@
         step([order[found - 1]])
 
 
+def windows_first(
+    slots, obj_re, obj_im, probe_re_far, probe_im_far, table_far, frames_far,
+    cells, acc, probe_re, probe_im, table, frames, order, sems,
+):
+    tile_r, tile_c = obj_re.shape
+    inner = slice(HALO, HALO + tile_r)
+    middle = slice(LANES, LANES + tile_c)
+    pairs = (
+        (table_far, table),
+        (frames_far, frames),
+        (obj_re, cells.at[0, inner, middle]),
+        (obj_im, cells.at[1, inner, middle]),
+        (probe_re_far, probe_re),
+        (probe_im_far, probe_im),
+    )
+    copies = fetch(pairs, sems)
+    acc[...] = jnp.zeros_like(acc)
+    finish_all(copies)
+    run_windows(FIRST, slots, cells, acc, probe_re, probe_im, table, frames, order)
+
+
 def windows_before(
-    slots, cells, probe_re, probe_im, table, frames, acc, order, power,
+    slots, cells, acc_in, probe_re, probe_im, table, frames, acc, order, power,
 ):
-    acc[...] = jnp.zeros_like(acc)
     power[...] = probe_re[...] * probe_re[...] + probe_im[...] * probe_im[...]
     lane = lane_index(P_SIZE)
 
@@ -379,10 +392,7 @@
         return carry
 
     lax.fori_loop(0, live_slots(slots, cells), step, 0)
-    run_windows(
-        lambda over, seen, limit: ~over & (seen < limit),
-        slots, cells, acc, probe_re, probe_im, table, frames, order,
-    )
+    run_windows(BEFORE, slots, cells, acc, probe_re, probe_im, table, frames, order)
 
 
 def reaching(place, right, tile_r, tile_c):
@@ -443,10 +453,7 @@
     copy = pltpu.make_async_copy(whole, places, sem)
     copy.start()
     power[...] = probe_re[...] * probe_re[...] + probe_im[...] * probe_im[...]
-    run_windows(
-        lambda over, seen, limit: ~over & (seen >= limit),
-        slots, cells, acc, probe_re, probe_im, table, frames, order,
-    )
+    run_windows(AFTER, slots, cells, acc, probe_re, probe_im, table, frames, order)
     copy.wait()
     add_neighbours_light(places, acc, power)
 
@@ -461,10 +468,7 @@
         cells[layer, row : row + part.shape[0], 0:LANES] = part
     for layer, row, part in pieces(after, 2, rows):
         cells[layer, row : row + part.shape[0], width - LANES :] = part
-    run_windows(
-        lambda over, seen, limit: over,
-        slots, cells, acc, probe_re, probe_im, table, frames, order,
-    )
+    run_windows(OVER, slots, cells, acc, probe_re, probe_im, table, frames, order)
     group_rows = 2 * rows // GROUPS
     fill_strip(strip, (acc[0, :, 0:LANES], acc[1, :, 0:LANES]))
     to_left = pack_lanes(strip, group_rows, LANES - HALO)
@@ -502,7 +506,10 @@
     new_im[start : start + size, :] = cells[1, here, middle] - part[1] * scale
 
 
-def finish_inner(cells, acc, new_re, new_im, near_re, near_im, sems):
+def finish_inner(
+    slots, cells, acc_in, probe_re, probe_im, table, frames, acc, new_re, new_im, order, near_re, near_im, sems,
+):
+    run_windows(LAST, slots, cells, acc, probe_re, probe_im, table, frames, order)
     tile_r = near_re.shape[0]
     new_rows(cells, acc, None, HALO, tile_r - 2 * HALO, near_re, near_im)
     rows = slice(HALO, tile_r - HALO)
@@ -520,7 +527,7 @@
     finish_all(copies)
 
 
-def swap(to_inner, to_outer, axis, gather):
+def swap(to_inner, to_outer, axis):
     devices = lax.axis_size(axis)
     inner = [(i, i + 1) for i in range(0, devices, 2)]
     partner = {i: i + 1 if i % 2 else i - 1 for i in range(1, devices - 1)}
@@ -534,10 +541,7 @@
                 there = (row, partner[col]) if col in partner else (row ^ 1, col)
             pairs.append((row * n_col + col, there[0] * n_col + there[1]))
     by_outer = lax.ppermute(to_outer, ("row", "col"), pairs)
-    if gather:
-        by_inner = lax.all_gather(to_inner, axis, axis_index_groups=[list(pair) for pair in inner])
-    else:
-        by_inner = lax.ppermute(to_inner, axis, inner + [(j, i) for i, j in inner])
+    by_inner = lax.ppermute(to_inner, axis, inner + [(j, i) for i, j in inner])
     return by_inner, by_outer
 
 
@@ -572,21 +576,22 @@
         compiler_params=SMALL,
         name="row_edges",
     )(counts, far(object_re), far(object_im), far(places), far(frame_index))
-    by_inner, by_outer = swap(to_inner, to_outer, "row", True)
-
-    cells, *fixed = pl.pallas_call(
-        load_state,
+    by_inner, by_outer = swap(to_inner, to_outer, "row")
+
+    order = pltpu.SMEM((slots,), jnp.int32)
+    cells, acc, *fixed = pl.pallas_call(
+        windows_first,
         out_shape=(
-            cells_shape, f32(*probe_re.shape), f32(*probe_im.shape),
+            cells_shape, acc_shape, f32(*probe_re.shape), f32(*probe_im.shape),
             jax.ShapeDtypeStruct(table.shape, table.dtype), jax.ShapeDtypeStruct(frames.shape, frames.dtype),
         ),
-        in_specs=[HBM] * 6,
-        out_specs=(VMEM,) * 5,
-        scratch_shapes=[dma((6,))],
-        compiler_params=SMALL,
+        in_specs=[SMEM] + [HBM] * 6,
+        out_specs=(VMEM,) * 6,
+        scratch_shapes=[order, dma((6,))],
+        compiler_params=PARAMS,
         cost_estimate=BUSY,
-        name="load_state",
-    )(*map(far, (object_re, object_im, probe_re, probe_im, table, frames)))
+        name="windows_first",
+    )(marked, *map(far, (object_re, object_im, probe_re, probe_im, table, frames)))
 
     strip = pltpu.VMEM((2 * rows, LANES), jnp.float32)
     packed = f32(2 * rows // GROUPS + MARKS, LANES)
@@ -600,19 +605,19 @@
         compiler_params=SMALL,
         name="row_halos",
     )(cells, to_outer, by_inner, by_outer)
-    edges = swap(to_inner, to_outer, "col", False)
-
-    order = pltpu.SMEM((slots,), jnp.int32)
+    edges = swap(to_inner, to_outer, "col")
+
     acc = pl.pallas_call(
         windows_before,
         out_shape=acc_shape,
-        in_specs=[SMEM] + [VMEM] * 5,
+        in_specs=[SMEM] + [VMEM] * 6,
         out_specs=VMEM,
         scratch_shapes=[order, pltpu.VMEM(probe_re.shape, jnp.float32)],
+        input_output_aliases={2: 0},
         compiler_params=PARAMS,
         cost_estimate=BUSY,
         name="windows_before",
-    )(marked, cells, *fixed)
+    )(marked, cells, acc, *fixed)
 
     packed = f32(2 * rows // GROUPS, LANES)
     cells, acc, to_inner, to_outer = pl.pallas_call(
@@ -626,7 +631,7 @@
         cost_estimate=BUSY,
         name="windows_over_edge",
     )(marked, cells, acc, *fixed, *edges)
-    by_inner, by_outer = swap(to_inner, to_outer, "col", False)
+    by_inner, by_outer = swap(to_inner, to_outer, "col")
 
     acc = pl.pallas_call(
         windows_after,
@@ -653,20 +658,21 @@
         compiler_params=SMALL,
         name="row_spill",
     )(acc, by_inner, by_outer)
-    by_inner, by_outer = swap(to_inner, to_outer, "row", True)
+    by_inner, by_outer = swap(to_inner, to_outer, "row")
 
     near = [pltpu.VMEM((tile_r, tile_c), jnp.float32)] * 2
     new = (f32(tile_r, tile_c), f32(tile_r, tile_c))
-    new_re, new_im = pl.pallas_call(
+    acc, new_re, new_im = pl.pallas_call(
         finish_inner,
-        out_shape=new,
-        in_specs=[VMEM] * 2,
-        out_specs=(HBM, HBM),
-        scratch_shapes=near + [dma((2,))],
-        compiler_params=SMALL,
+        out_shape=(acc_shape, *new),
+        in_specs=[SMEM] + [VMEM] * 6,
+        out_specs=(VMEM, HBM, HBM),
+        scratch_shapes=[order] + near + [dma((2,))],
+        input_output_aliases={2: 0},
+        compiler_params=PARAMS,
         cost_estimate=BUSY,
         name="finish_inner",
-    )(cells, acc)
+    )(marked, cells, acc, *fixed)
     return pl.pallas_call(
         finish_edges,
         out_shape=new,

time: 33.4 us -> 32.4 us (0.970)
  the two profiles are of different devices: /device:TPU:0 before, /device:TPU:20 now
where the time goes in v2:
time: 32.4 us
  Pallas kernels  12.9 us (40%)
  waiting for transfers between devices  11 us (34%)
  starting transfers between devices  6.93 us (21%)
  between operations  1.55 us (5%)
    ppermute x4, waiting for transfers between devices, swap(): by_outer = lax.ppermute(to_outer, ('row', 'col'), pairs)  5.84 us
    ppermute x4, waiting for transfers between devices, swap(): by_inner = lax.ppermute(to_inner, axis, inner + [(j, i) for i, j in inner])  5.12 us
    ppermute x4, starting transfers between devices, swap(): by_outer = lax.ppermute(to_outer, ('row', 'col'), pairs)  5.07 us
    pallas_call x1, Pallas kernels, shards(): pl.pallas_call(windows_over_edge, out_shape=(cells_shape, acc_shape, pack...  3.02 us
    pallas_call x1, Pallas kernels, shards(): pl.pallas_call(windows_first, out_shape=(cells_shape, acc_shape, f32(*pro...  2.88 us
    pallas_call x1, Pallas kernels, shards(): pl.pallas_call(windows_after, out_shape=acc_shape, in_specs=[SMEM] + [VME...  1.94 us
    pallas_call x1, Pallas kernels, shards(): pl.pallas_call(finish_inner, out_shape=(acc_shape, *new), in_specs=[SMEM]...  1.91 us
    ppermute x4, starting transfers between devices, swap(): by_inner = lax.ppermute(to_inner, axis, inner + [(j, i) for i, j in inner])  1.85 us
  transfers between devices with their start and end apart: 8, of which 6 were waited for; matrix products, arithmetic and copies ran while one was open for 0% of the time, Pallas kernels for 24%

profile of v2, /device:TPU:20, one launch (start us, length us, event | category | flops | bytes accessed | tf_op | source)
XLA Modules:
  0.0 32.4 jit_solution(7951594135196836943)
XLA Ops:
  1.3 1.0 %row_edges.1 = (f32[72,512]{1,0:T(8,128)S(1)}, f32[72,512]{1,0:T(8,128)S(1)}, s32[3,8]{1,0:T(4,128)S(1)}) custom-call(s32[1,1]{1,0:T(1,128)S(6)} %copy.29.counts, f32[384,512]{1,0:T(8,128)} %obj_re.3, f32[384,512]{1,0:T(8,128)} %obj_im.3, s32[1,1,2,8]{3,2,1,0:T(2,128)} %bitcast.2, s32[1,1,8]{2,1,0:T(1,128)} %chosen.1), custom_call_target="tpu_custom_call" | custom-call | tf_op jit(solution)/shard_map/row_edges/pallas_call | solution.py:568
  2.3 0.1 collective-permute-start
  2.4 1.5 %collective-permute-start.1 = (f32[72,512]{1,0:T(8,128)S(1)}, f32[72,512]{1,0:T(8,128)S(1)}, u32[]{:S(2)}, u32[]{:S(2)}) collective-permute-start(f32[72,512]{1,0:T(8,128)S(1)} %get-tuple-element.27.own), channel_id=1, source_target_pairs={{0,1},{1,0},{2,3},{3,2},{4,8},{5,9},{6,10},{7,11},{8,4},{9,5},{10,... | collective-permute-start | bytes 442376 | tf_op jit(solution)/shard_map/ppermute | solution.py:543
  3.9 2.9 %windows_first.1 = (f32[2,448,768]{2,1,0:T(8,128)S(1)}, f32[3,448,768]{2,1,0:T(8,128)S(1)}, f32[256,256]{1,0:T(8,128)S(1)}, f32[256,256]{1,0:T(8,128)S(1)}, bf16...) custom-call(s32[3,8]{1,0:T(4,128)S(1)} %get-tuple-element.25.slots, f32[384,512]{1,0:T(8,128)} %obj_re.3, ...), custom_call_target="tpu_custom_call" | custom-call | flops 4000000000 | bytes 8000000 | tf_op jit(solution)/shard_map/windows_first/pallas_call | solution.py:582
  6.8 0.0 collective-permute-done.by_inner
  6.8 2.3 %collective-permute-done.1.by_outer = f32[72,512]{1,0:T(8,128)S(1)} collective-permute-done((f32[72,512]{1,0:T(8,128)S(1)}, f32[72,512]{1,0:T(8,128)S(1)}, u32[]{:S(2)}, u32[]{:S(2)}) %collective-permute-start.1) | collective-permute-done | bytes 147488 | tf_op jit(solution)/shard_map/ppermute | solution.py:543
  9.1 0.3 row_halos.1
  9.4 1.6 %collective-permute-start.2 = (f32[232,128]{1,0:T(8,128)S(1)}, f32[232,128]{1,0:T(8,128)S(1)}, u32[]{:S(2)}, u32[]{:S(2)}) collective-permute-start(f32[232,128]{1,0:T(8,128)S(1)} %get-tuple-element.35), channel_id=1, source_target_pairs={{0,1},{2,3},{1,0},{3,2},{4,5},{6,7},{5,4},{7,6},{8,9},{10,11},{9,8... | collective-permute-start | bytes 356360 | tf_op jit(solution)/shard_map/ppermute | solution.py:544
  11.1 0.0 collective-permute-start.3
  11.1 0.9 %windows_before.1.acc_in = f32[3,448,768]{2,1,0:T(8,128)S(1)} custom-call(s32[3,8]{1,0:T(4,128)S(1)} %get-tuple-element.25.slots, f32[2,448,768]{2,1,0:T(8,128)S(1)} %get-tuple-element.29.cells.cells_in, f32[3,448,768]{2,1,0:T(8,128)S(1)} %get-tuple-element.30.acc_in, f32[256,256]{1,0:T(8,128)S(1)} %get-tuple-element.31.probe_re, ...), custom_call_target="tpu_custom_call", output_to_operand_aliasing={{}: (2, {})} | custom-call | flops 4000000000 | bytes 8000000 | tf_op jit(solution)/shard_map/windows_before/pallas_call | solution.py:610
  12.0 2.4 %collective-permute-done.2.by_inner = f32[232,128]{1,0:T(8,128)S(1)} collective-permute-done((f32[232,128]{1,0:T(8,128)S(1)}, f32[232,128]{1,0:T(8,128)S(1)}, u32[]{:S(2)}, u32[]{:S(2)}) %collective-permute-start.2) | collective-permute-done | bytes 118816 | tf_op jit(solution)/shard_map/ppermute | solution.py:544
  14.3 1.6 %collective-permute-done.3.by_outer = f32[232,128]{1,0:T(8,128)S(1)} collective-permute-done((f32[232,128]{1,0:T(8,128)S(1)}, f32[232,128]{1,0:T(8,128)S(1)}, u32[]{:S(2)}, u32[]{:S(2)}) %collective-permute-start.3) | collective-permute-done | bytes 118816 | tf_op jit(solution)/shard_map/ppermute | solution.py:543
  15.9 3.0 %windows_over_edge.1 = (f32[2,448,768]{2,1,0:T(8,128)S(1)}, f32[3,448,768]{2,1,0:T(8,128)S(1)}, f32[224,128]{1,0:T(8,128)S(1)}, f32[224,128]{1,0:T(8,128)S(1)}) custom-call(s32[3,8]{1,0:T(4,128)S(1)} %get-tuple-element.25.slots, f32[2,448,768]{2,1,0:T(8,128)S(1)} %get-tuple-element.29.cells.cells_in, ...), custom_call_target="tpu_custom_call", output_to_operand_aliasing={{0}: (1, {}), {1}: (2, {})} | custom-call | flops 4000000000 | bytes 8000000 | tf_op jit(solution)/shard_map/windows_over_edge/pallas_call | solution.py:623
  18.9 0.1 collective-permute-start.4
  19.0 0.1 collective-permute-start.5
  19.1 1.9 %windows_after.1.acc_in = f32[3,448,768]{2,1,0:T(8,128)S(1)} custom-call(s32[3,8]{1,0:T(4,128)S(1)} %get-tuple-element.25.slots, f32[2,448,768]{2,1,0:T(8,128)S(1)} %get-tuple-element.37.cells, f32[3,448,768]{2,1,0:T(8,128)S(1)} %get-tuple-element.38.acc_in, f32[256,256]{1,0:T(8,128)S(1)} %get-tuple-element.31.probe_re, ...), custom_call_target="tpu_custom_call", output_to_operand_aliasing={{}: (2, {})} | custom-call | flops 4000000000 | bytes 8000000 | tf_op jit(solution)/shard_map/windows_after/pallas_call | solution.py:636
  21.0 2.8 %collective-permute-done.4.by_inner = f32[224,128]{1,0:T(8,128)S(1)} collective-permute-done((f32[224,128]{1,0:T(8,128)S(1)}, f32[224,128]{1,0:T(8,128)S(1)}, u32[]{:S(2)}, u32[]{:S(2)}) %collective-permute-start.4) | collective-permute-done | bytes 114720 | tf_op jit(solution)/shard_map/ppermute | solution.py:544
  23.8 0.1 collective-permute-done.5.by_outer
  23.8 0.3 row_spill.1
  24.1 0.1 collective-permute-start.6
  24.2 3.5 %collective-permute-start.7 = (f32[2,32,512]{2,1,0:T(8,128)S(1)}, f32[2,32,512]{2,1,0:T(8,128)S(1)}, u32[]{:S(2)}, u32[]{:S(2)}) collective-permute-start(f32[2,32,512]{2,1,0:T(8,128)S(1)} %get-tuple-element.45), channel_id=1, source_target_pairs={{0,1},{1,0},{2,3},{3,2},{4,8},{5,9},{6,10},{7,11},{8,4},{9,5},{10,... | collective-permute-start | bytes 393224 | tf_op jit(solution)/shard_map/ppermute | solution.py:543
  27.7 1.9 %finish_inner.1 = (f32[3,448,768]{2,1,0:T(8,128)S(1)}, f32[384,512]{1,0:T(8,128)}, f32[384,512]{1,0:T(8,128)}) custom-call(s32[3,8]{1,0:T(4,128)S(1)} %get-tuple-element.25.slots, f32[2,448,768]{2,1,0:T(8,128)S(1)} %get-tuple-element.37.cells, f32[3,448,768]{2,1,0:T(8,128)S(1)} %get-tuple-element.42.acc_in, ...), custom_call_target="tpu_custom_call", output_to_operand_aliasing={{0}: (2, {})} | custom-call | flops 4000000000 | bytes 8000000 | tf_op jit(solution)/shard_map/finish_inner/pallas_call | solution.py:665
  29.6 0.0 collective-permute-done.6.by_inner
  29.6 1.9 %collective-permute-done.7.by_outer = f32[2,32,512]{2,1,0:T(8,128)S(1)} collective-permute-done((f32[2,32,512]{2,1,0:T(8,128)S(1)}, f32[2,32,512]{2,1,0:T(8,128)S(1)}, u32[]{:S(2)}, u32[]{:S(2)}) %collective-permute-start.7) | collective-permute-done | bytes 131104 | tf_op jit(solution)/shard_map/ppermute | solution.py:543
  31.5 0.8 %finish_edges.1 = (f32[384,512]{1,0:T(8,128)}, f32[384,512]{1,0:T(8,128)}) custom-call(f32[2,448,768]{2,1,0:T(8,128)S(1)} %get-tuple-element.37.cells, f32[3,448,768]{2,1,0:T(8,128)S(1)} %get-tuple-element.43.acc, f32[2,32,512]{2,1,0:T(8,128)S(1)} %collective-permute-done.6.by_inner, ...), custom_call_target="tpu_custom_call", output_to_operand_aliasing={{0}: (4, {}), {1}: (5, {})} | custom-call | tf_op jit(solution)/shard_map/finish_edges/pallas_call | solution.py:676
Async XLA Ops:
  2.3 4.5 %collective-permute-start = (f32[72,512]{1,0:T(8,128)S(1)}, f32[72,512]{1,0:T(8,128)S(1)}, u32[]{:S(2)}, u32[]{:S(2)}) collective-permute-start(f32[72,512]{1,0:T(8,128)S(1)} %get-tuple-element.28), channel_id=1, source_target_pairs={{0,4},{8,12},{16,20},{24,28},{4,0},{12,8},{20,16},{28,24},{1,5},{9... | collective-permute-start | bytes 442376 | tf_op jit(solution)/shard_map/ppermute | solution.py:544
  2.4 6.8 %collective-permute-start.1 = (f32[72,512]{1,0:T(8,128)S(1)}, f32[72,512]{1,0:T(8,128)S(1)}, u32[]{:S(2)}, u32[]{:S(2)}) collective-permute-start(f32[72,512]{1,0:T(8,128)S(1)} %get-tuple-element.27.own), channel_id=1, source_target_pairs={{0,1},{1,0},{2,3},{3,2},{4,8},{5,9},{6,10},{7,11},{8,4},{9,5},{10,... | collective-permute-start | bytes 442376 | tf_op jit(solution)/shard_map/ppermute | solution.py:543
  9.4 4.9 %collective-permute-start.2 = (f32[232,128]{1,0:T(8,128)S(1)}, f32[232,128]{1,0:T(8,128)S(1)}, u32[]{:S(2)}, u32[]{:S(2)}) collective-permute-start(f32[232,128]{1,0:T(8,128)S(1)} %get-tuple-element.35), channel_id=1, source_target_pairs={{0,1},{2,3},{1,0},{3,2},{4,5},{6,7},{5,4},{7,6},{8,9},{10,11},{9,8... | collective-permute-start | bytes 356360 | tf_op jit(solution)/shard_map/ppermute | solution.py:544
  11.1 4.8 %collective-permute-start.3 = (f32[232,128]{1,0:T(8,128)S(1)}, f32[232,128]{1,0:T(8,128)S(1)}, u32[]{:S(2)}, u32[]{:S(2)}) collective-permute-start(f32[232,128]{1,0:T(8,128)S(1)} %get-tuple-element.36), channel_id=1, source_target_pairs={{0,4},{1,2},{2,1},{3,7},{4,0},{5,6},{6,5},{7,3},{8,12},{9,10},{10,... | collective-permute-start | bytes 356360 | tf_op jit(solution)/shard_map/ppermute | solution.py:543
  18.9 4.9 %collective-permute-start.4 = (f32[224,128]{1,0:T(8,128)S(1)}, f32[224,128]{1,0:T(8,128)S(1)}, u32[]{:S(2)}, u32[]{:S(2)}) collective-permute-start(f32[224,128]{1,0:T(8,128)S(1)} %get-tuple-element.40), channel_id=1, source_target_pairs={{0,1},{2,3},{1,0},{3,2},{4,5},{6,7},{5,4},{7,6},{8,9},{10,11},{9,8... | collective-permute-start | bytes 344072 | tf_op jit(solution)/shard_map/ppermute | solution.py:544
  19.0 4.9 %collective-permute-start.5 = (f32[224,128]{1,0:T(8,128)S(1)}, f32[224,128]{1,0:T(8,128)S(1)}, u32[]{:S(2)}, u32[]{:S(2)}) collective-permute-start(f32[224,128]{1,0:T(8,128)S(1)} %get-tuple-element.41), channel_id=1, source_target_pairs={{0,4},{1,2},{2,1},{3,7},{4,0},{5,6},{6,5},{7,3},{8,12},{9,10},{10,... | collective-permute-start | bytes 344072 | tf_op jit(solution)/shard_map/ppermute | solution.py:543
  24.1 5.5 %collective-permute-start.6 = (f32[2,32,512]{2,1,0:T(8,128)S(1)}, f32[2,32,512]{2,1,0:T(8,128)S(1)}, u32[]{:S(2)}, u32[]{:S(2)}) collective-permute-start(f32[2,32,512]{2,1,0:T(8,128)S(1)} %get-tuple-element.44), channel_id=1, source_target_pairs={{0,4},{8,12},{16,20},{24,28},{4,0},{12,8},{20,16},{28,24},{1,5},{9... | collective-permute-start | bytes 393224 | tf_op jit(solution)/shard_map/ppermute | solution.py:544
  24.2 7.3 %collective-permute-start.7 = (f32[2,32,512]{2,1,0:T(8,128)S(1)}, f32[2,32,512]{2,1,0:T(8,128)S(1)}, u32[]{:S(2)}, u32[]{:S(2)}) collective-permute-start(f32[2,32,512]{2,1,0:T(8,128)S(1)} %get-tuple-element.45), channel_id=1, source_target_pairs={{0,1},{1,0},{2,3},{3,2},{4,8},{5,9},{6,10},{7,11},{8,4},{9,5},{10,... | collective-permute-start | bytes 393224 | tf_op jit(solution)/shard_map/ppermute | solution.py:543

commit v3 on v2

--- a/solution.py
+++ b/solution.py
@@ -52,11 +52,13 @@
     return lax.broadcasted_iota(jnp.int32, (rows, LANES), 1)
 
 
-def pack_lanes(ref, rows, first):
-    lane = lane_index(rows)
+def pack_lanes(field, top, size, tile, first):
+    half = size // 2
+    lane = lane_index(half)
     packed = None
     for g in range(GROUPS):
-        part = ref[g * rows : (g + 1) * rows, :]
+        start = top + g % 2 * half
+        part = field[g // 2, start : start + half, tile]
         if g:
             part = pltpu.roll(part, HALO * g, 1)
         low = (first + HALO * g) % LANES
@@ -209,13 +211,6 @@
         acc[layer, pl.ds(row, term.shape[0]), pl.ds(base + t * LANES, LANES)] += parts[t]
 
 
-def fill_strip(strip, parts):
-    done = 0
-    for part in parts:
-        strip[done : done + part.shape[0], :] = part
-        done += part.shape[0]
-
-
 def send_columns(to_left, to_right, to_inner, to_outer):
     odd = is_odd("col")
     to_inner[0 : to_left.shape[0], :] = jnp.where(odd, to_left, to_right)
@@ -231,19 +226,35 @@
     return jnp.where(odd, by_inner, by_outer), jnp.where(odd, by_outer, by_inner)
 
 
-def pieces(packed, layers, rows):
-    group_rows = layers * rows // GROUPS
+def pieces(packed, size):
+    half = size // 2
     for g in range(GROUPS):
-        part = unpack_lanes(packed, g)
-        done = 0
-        while done < group_rows:
-            layer, row = divmod(g * group_rows + done, rows)
-            size = min(group_rows - done, rows - row)
-            yield layer, row, part[done : done + size]
-            done += size
-
-
-def row_halos(cells_in, own, by_inner, by_outer, cells, marks, to_inner, to_outer, strip):
+        yield g // 2, g % 2 * half, unpack_lanes(packed[:half], g)
+
+
+def pack_corners(field, rows):
+    width = field.shape[2]
+    left = [field[k, rows, 0:LANES] for k in (0, 1)]
+    right = [field[k, rows, width - LANES : width] for k in (0, 1)]
+    lane = lane_index(HALO)
+    low = jnp.where(lane < HALO, right[0], pltpu.roll(right[1], HALO, 1))
+    high = jnp.where(lane < 3 * HALO, pltpu.roll(left[1], 3 * HALO, 1), left[0])
+    packed = jnp.where(lane < 2 * HALO, low, high)
+    return beside(*(packed[i : i + MARKS] for i in range(0, HALO, MARKS)))
+
+
+def unpack_corners(packed):
+    packed = below(*(packed[:, i : i + LANES] for i in range(0, GROUPS * LANES, LANES)))
+    lane = lane_index(HALO)
+    for k, left, right in ((0, 0, 0), (1, HALO, 3 * HALO)):
+        yield (
+            k,
+            jnp.where(lane >= 3 * HALO, pltpu.roll(packed, left, 1) if left else packed, 0.0),
+            jnp.where(lane < HALO, pltpu.roll(packed, right, 1) if right else packed, 0.0),
+        )
+
+
+def row_halos(cells_in, own, by_inner, by_outer, cells, marks, to_inner, to_outer):
     rows, width = cells.shape[1:]
     middle = slice(LANES, width - LANES)
     before, after = received(by_inner, by_outer, "row")
@@ -253,15 +264,12 @@
     first_mark = 2 * HALO
     for i, message in enumerate((own[...], before, after)):
         marks[2 * i : 2 * i + 2, :] = message[first_mark : first_mark + 2, 0:LANES]
-    group_rows = 2 * rows // GROUPS
-    first, last = slice(LANES, 2 * LANES), slice(width - 2 * LANES, width - LANES)
-    fill_strip(strip, (cells[0, :, first], cells[1, :, first]))
-    to_left = pack_lanes(strip, group_rows, 0)
-    fill_strip(strip, (cells[0, :, last], cells[1, :, last]))
-    to_right = pack_lanes(strip, group_rows, LANES - HALO)
+    half = rows // 2
+    to_left = pack_lanes(cells, 0, rows, slice(LANES, 2 * LANES), 0)
+    to_right = pack_lanes(cells, 0, rows, slice(width - 2 * LANES, width - LANES), LANES - HALO)
     send_columns(to_left, to_right, to_inner, to_outer)
-    to_inner[group_rows:, :] = marks[...]
-    to_outer[group_rows:, :] = marks[...]
+    to_inner[half:, :] = marks[...]
+    to_outer[half:, :] = marks[...]
 
 
 def live_slots(slots, cells):
@@ -279,30 +287,30 @@
     tile_r, tile_c = cells.shape[1] - 2 * HALO, cells.shape[2] - 2 * LANES
     count = live_slots(slots, cells)
     kinds = []
-    n_inside, n_row = jnp.int32(0), jnp.int32(0)
+    n_inside, n_row, n_col = jnp.int32(0), jnp.int32(0), jnp.int32(0)
     for slot in range(slots.shape[1]):
         row, col = slots[0, slot], slots[1, slot]
         live = slot < count
         over_col = (col < 0) | (col > tile_c - P_SIZE)
         over_row = (row < 0) | (row > tile_r - P_SIZE)
         inside, by_row = live & ~over_col & ~over_row, live & ~over_col & over_row
-        kinds.append((live & over_col, inside, by_row, n_inside, n_row))
+        by_col, by_both = live & over_col & ~over_row, live & over_col & over_row
+        kinds.append((inside, by_row, by_col, by_both, n_inside, n_row))
         n_inside += inside.astype(jnp.int32)
         n_row += by_row.astype(jnp.int32)
+        n_col += by_col.astype(jnp.int32)
     first = jnp.minimum(n_inside, PAIR)
-    rest = n_inside - first + n_row
-    last = jnp.clip(rest - 2 * PAIR, 0, jnp.minimum(n_inside - first, PAIR))
-    before = jnp.minimum(rest - last, PAIR)
+    before = first + jnp.minimum(n_inside - first, PAIR - jnp.minimum(n_row, PAIR))
+    rest = n_inside - before
+    after = n_inside - jnp.clip(n_col + rest - 2 * PAIR, 0, jnp.minimum(rest, PAIR))
     found = jnp.int32(0)
-    for slot, (over, inside, by_row, inside_rank, row_rank) in enumerate(kinds):
-        rank = jnp.where(by_row, row_rank, n_row + inside_rank - first)
-        later = by_row | (inside & (inside_rank >= first))
+    for slot, (inside, by_row, by_col, by_both, rank, row_rank) in enumerate(kinds):
         mine = {
-            FIRST: lambda: inside & (inside_rank < first),
-            BEFORE: lambda: later & (rank < before),
-            OVER: lambda: over,
-            AFTER: lambda: later & (rank >= before) & (rank < rest - last),
-            LAST: lambda: later & (rank >= rest - last),
+            FIRST: lambda: inside & (rank < first),
+            BEFORE: lambda: (by_row & (row_rank < PAIR)) | (inside & (rank >= first) & (rank < before)),
+            OVER: lambda: by_both | (by_row & (row_rank >= PAIR)),
+            AFTER: lambda: by_col | (inside & (rank >= before) & (rank < after)),
+            LAST: lambda: inside & (rank >= after),
         }[phase]()
 
         @pl.when(mine)
@@ -460,69 +468,71 @@
 
 def windows_over_edge(
     slots, cells_in, acc_in, probe_re, probe_im, table, frames, by_inner, by_outer,
-    cells, acc, to_inner, to_outer, order, strip,
+    cells, acc, to_inner, to_outer, order,
 ):
     rows, width = acc.shape[1:]
     before, after = received(by_inner, by_outer, "col")
-    for layer, row, part in pieces(before, 2, rows):
-        cells[layer, row : row + part.shape[0], 0:LANES] = part
-    for layer, row, part in pieces(after, 2, rows):
-        cells[layer, row : row + part.shape[0], width - LANES :] = part
+    for tile, packed in ((slice(0, LANES), before), (slice(width - LANES, width), after)):
+        for layer, row, part in pieces(packed, rows):
+            cells[layer, row : row + part.shape[0], tile] = part
     run_windows(OVER, slots, cells, acc, probe_re, probe_im, table, frames, order)
-    group_rows = 2 * rows // GROUPS
-    fill_strip(strip, (acc[0, :, 0:LANES], acc[1, :, 0:LANES]))
-    to_left = pack_lanes(strip, group_rows, LANES - HALO)
-    fill_strip(strip, (acc[0, :, width - LANES :], acc[1, :, width - LANES :]))
-    to_right = pack_lanes(strip, group_rows, 0)
+    odd = is_odd("row")
+    strips = []
+    for here in (slice(0, HALO), slice(rows - HALO, rows)):
+        middle = [acc[k, here, LANES : width - LANES] for k in (0, 1)]
+        strips.append(below(*middle, pack_corners(acc, here)))
+    to_inner[...] = jnp.where(odd, strips[0], strips[1])
+    to_outer[...] = jnp.where(odd, strips[1], strips[0])
+
+
+def column_spill(acc_in, by_inner, by_outer, acc, to_inner, to_outer):
+    rows, width = acc.shape[1:]
+    before, after = received(by_inner, by_outer, "row")
+    for start, came in ((HALO, before), (rows - 2 * HALO, after)):
+        here = slice(start, start + HALO)
+        for k in (0, 1):
+            acc[k, here, LANES : width - LANES] += came[k * HALO : (k + 1) * HALO]
+        for k, left, right in unpack_corners(came[2 * HALO :]):
+            acc[k, here, 0:LANES] += left
+            acc[k, here, width - LANES :] += right
+    tile_r = rows - 2 * HALO
+    to_left = pack_lanes(acc, HALO, tile_r, slice(0, LANES), LANES - HALO)
+    to_right = pack_lanes(acc, HALO, tile_r, slice(width - LANES, width), 0)
     send_columns(to_left, to_right, to_inner, to_outer)
 
 
-def row_spill(acc_in, by_inner, by_outer, acc, to_inner, to_outer):
-    rows, width = acc.shape[1:]
-    before, after = received(by_inner, by_outer, "col")
-    lane = lane_index(rows)[0:1]
-    for layer, row, part in pieces(before, 2, rows):
-        here = slice(row, row + part.shape[0])
-        acc[layer, here, LANES : 2 * LANES] += jnp.where(lane < HALO, part, 0.0)
-    for layer, row, part in pieces(after, 2, rows):
-        here = slice(row, row + part.shape[0])
-        acc[layer, here, width - 2 * LANES : width - LANES] += jnp.where(lane >= LANES - HALO, part, 0.0)
-    odd = is_odd("row")
-    for k in (0, 1):
-        up = acc[k, 0:HALO, LANES : width - LANES]
-        down = acc[k, rows - HALO : rows, LANES : width - LANES]
-        to_inner[k] = jnp.where(odd, up, down)
-        to_outer[k] = jnp.where(odd, down, up)
-
-
-def new_rows(cells, acc, extra, start, size, new_re, new_im):
-    here = slice(HALO + start, HALO + start + size)
-    middle = slice(LANES, acc.shape[2] - LANES)
-    part = [acc[k, here, middle] for k in range(acc.shape[0])]
-    if extra is not None:
-        part[:2] = [part[k] + extra[k] for k in (0, 1)]
+def new_columns(cells, acc, spill, start, size, near_re, near_im):
+    rows = acc.shape[1]
+    here, there = slice(HALO, rows - HALO), slice(LANES + start, LANES + start + size)
+    part = [acc[k, here, there] for k in range(acc.shape[0])]
+    if spill is not None:
+        part[:2] = [part[k] + spill[k] for k in (0, 1)]
     scale = 1.0 / (part[2] + ridge)
-    new_re[start : start + size, :] = cells[0, here, middle] - part[0] * scale
-    new_im[start : start + size, :] = cells[1, here, middle] - part[1] * scale
+    near_re[:, start : start + size] = cells[0, here, there] - part[0] * scale
+    near_im[:, start : start + size] = cells[1, here, there] - part[1] * scale
 
 
 def finish_inner(
     slots, cells, acc_in, probe_re, probe_im, table, frames, acc, new_re, new_im, order, near_re, near_im, sems,
 ):
     run_windows(LAST, slots, cells, acc, probe_re, probe_im, table, frames, order)
-    tile_r = near_re.shape[0]
-    new_rows(cells, acc, None, HALO, tile_r - 2 * HALO, near_re, near_im)
-    rows = slice(HALO, tile_r - HALO)
-    finish_all(fetch([(near_re.at[rows], new_re.at[rows]), (near_im.at[rows], new_im.at[rows])], sems))
+    size = near_re.shape[1] - 2 * LANES
+    new_columns(cells, acc, None, LANES, size, near_re, near_im)
+    there = slice(LANES, LANES + size)
+    finish_all(fetch([(near_re.at[:, there], new_re.at[:, there]), (near_im.at[:, there], new_im.at[:, there])], sems))
 
 
 def finish_edges(cells, acc, by_inner, by_outer, re_in, im_in, new_re, new_im, near_re, near_im, sems):
-    tile_r = near_re.shape[0]
+    tile_r, tile_c = near_re.shape
+    lane = lane_index(tile_r)
+    sides = ((0, lane < HALO), (tile_c - LANES, lane >= LANES - HALO))
     copies = []
-    for i, (start, extra) in enumerate(zip((0, tile_r - HALO), received(by_inner, by_outer, "row"))):
-        new_rows(cells, acc, extra, start, HALO, near_re, near_im)
-        rows = slice(start, start + HALO)
-        pairs = ((near_re.at[rows], new_re.at[rows]), (near_im.at[rows], new_im.at[rows]))
+    for i, ((start, mine), packed) in enumerate(zip(sides, received(by_inner, by_outer, "col"))):
+        parts = [part for _, _, part in pieces(packed, tile_r)]
+        spill = [jnp.where(mine, below(*parts[2 * k : 2 * k + 2]), 0.0) for k in (0, 1)]
+        new_columns(cells, acc, spill, start, LANES, near_re, near_im)
+        there = slice(start, start + LANES)
+        pairs = ((near_re.at[:, there], new_re.at[:, there]), (near_im.at[:, there], new_im.at[:, there]))
         copies += fetch(pairs, sems.at[2 * i : 2 * i + 2])
     finish_all(copies)
 
@@ -593,14 +603,12 @@
         name="windows_first",
     )(marked, *map(far, (object_re, object_im, probe_re, probe_im, table, frames)))
 
-    strip = pltpu.VMEM((2 * rows, LANES), jnp.float32)
-    packed = f32(2 * rows // GROUPS + MARKS, LANES)
+    packed = f32(rows // 2 + MARKS, LANES)
     cells, marks, to_inner, to_outer = pl.pallas_call(
         row_halos,
         out_shape=(cells_shape, f32(MARKS, LANES), packed, packed),
         in_specs=[VMEM] * 4,
         out_specs=(VMEM,) * 4,
-        scratch_shapes=[strip],
         input_output_aliases={0: 0},
         compiler_params=SMALL,
         name="row_halos",
@@ -619,19 +627,18 @@
         name="windows_before",
     )(marked, cells, acc, *fixed)
 
-    packed = f32(2 * rows // GROUPS, LANES)
     cells, acc, to_inner, to_outer = pl.pallas_call(
         windows_over_edge,
-        out_shape=(cells_shape, acc_shape, packed, packed),
+        out_shape=(cells_shape, acc_shape, edge, edge),
         in_specs=[SMEM] + [VMEM] * 8,
         out_specs=(VMEM,) * 4,
-        scratch_shapes=[order, strip],
+        scratch_shapes=[order],
         input_output_aliases={1: 0, 2: 1},
         compiler_params=PARAMS,
         cost_estimate=BUSY,
         name="windows_over_edge",
     )(marked, cells, acc, *fixed, *edges)
-    by_inner, by_outer = swap(to_inner, to_outer, "col")
+    by_inner, by_outer = swap(to_inner, to_outer, "row")
 
     acc = pl.pallas_call(
         windows_after,
@@ -648,17 +655,17 @@
         name="windows_after",
     )(marked, cells, acc, *fixed, marks, *edges)
 
-    edge = f32(2, HALO, tile_c)
+    packed = f32(tile_r // 2, LANES)
     acc, to_inner, to_outer = pl.pallas_call(
-        row_spill,
-        out_shape=(acc_shape, edge, edge),
+        column_spill,
+        out_shape=(acc_shape, packed, packed),
         in_specs=[VMEM] * 3,
         out_specs=(VMEM,) * 3,
         input_output_aliases={0: 0},
         compiler_params=SMALL,
-        name="row_spill",
+        name="column_spill",
     )(acc, by_inner, by_outer)
-    by_inner, by_outer = swap(to_inner, to_outer, "row")
+    by_inner, by_outer = swap(to_inner, to_outer, "col")
 
     near = [pltpu.VMEM((tile_r, tile_c), jnp.float32)] * 2
     new = (f32(tile_r, tile_c), f32(tile_r, tile_c))

time: 32.4 us -> 31.9 us (0.985)
  the two profiles are of different devices: /device:TPU:20 before, /device:TPU:0 now
where the time goes in v3:
time: 31.9 us; the launch traced here: 31.7 us
  Pallas kernels  12.6 us (39%)
  starting transfers between devices  11.8 us (37%)
  waiting for transfers between devices  5.78 us (18%)
  between operations  1.53 us (5%)
    ppermute x4, starting transfers between devices, swap(): by_outer = lax.ppermute(to_outer, ('row', 'col'), pairs)  8.38 us
    pallas_call x1, Pallas kernels, shards(): pl.pallas_call(windows_first, out_shape=(cells_shape, acc_shape, f32(*pro...  4.66 us
    ppermute x4, waiting for transfers between devices, swap(): by_inner = lax.ppermute(to_inner, axis, inner + [(j, i) for i, j in inner])  4.3 us
    ppermute x4, starting transfers between devices, swap(): by_inner = lax.ppermute(to_inner, axis, inner + [(j, i) for i, j in inner])  3.43 us
    pallas_call x1, Pallas kernels, shards(): pl.pallas_call(finish_inner, out_shape=(acc_shape, *new), in_specs=[SMEM]...  1.72 us
    pallas_call x1, Pallas kernels, shards(): pl.pallas_call(windows_after, out_shape=acc_shape, in_specs=[SMEM] + [VME...  1.63 us
    ppermute x4, waiting for transfers between devices, swap(): by_outer = lax.ppermute(to_outer, ('row', 'col'), pairs)  1.48 us
    pallas_call x1, Pallas kernels, shards(): pl.pallas_call(windows_over_edge, out_shape=(cells_shape, acc_shape, edge...  1.08 us
  transfers between devices with their start and end apart: 8, of which 3 were waited for; matrix products, arithmetic and copies ran while one was open for 0% of the time, Pallas kernels for 28%

profile of v3, /device:TPU:0, one launch (start us, length us, event | category | flops | bytes accessed | tf_op | source)
XLA Modules:
  0.0 31.7 jit_solution(17844997720116752266)
XLA Ops:
  1.3 1.0 %row_edges.1 = (f32[72,512]{1,0:T(8,128)S(1)}, f32[72,512]{1,0:T(8,128)S(1)}, s32[3,8]{1,0:T(4,128)S(1)}) custom-call(s32[1,1]{1,0:T(1,128)S(6)} %copy.29.counts, f32[384,512]{1,0:T(8,128)} %obj_re.3, f32[384,512]{1,0:T(8,128)} %obj_im.3, s32[1,1,2,8]{3,2,1,0:T(2,128)} %bitcast.2, s32[1,1,8]{2,1,0:T(1,128)} %chosen.1), custom_call_target="tpu_custom_call" | custom-call | tf_op jit(solution)/shard_map/row_edges/pallas_call | solution.py:578
  2.3 0.5 %collective-permute-start = (f32[72,512]{1,0:T(8,128)S(1)}, f32[72,512]{1,0:T(8,128)S(1)}, u32[]{:S(2)}, u32[]{:S(2)}) collective-permute-start(f32[72,512]{1,0:T(8,128)S(1)} %get-tuple-element.28), channel_id=1, source_target_pairs={{0,4},{8,12},{16,20},{24,28},{4,0},{12,8},{20,16},{28,24},{1,5},{9... | collective-permute-start | bytes 442376 | tf_op jit(solution)/shard_map/ppermute | solution.py:554
  2.8 2.6 %collective-permute-start.1 = (f32[72,512]{1,0:T(8,128)S(1)}, f32[72,512]{1,0:T(8,128)S(1)}, u32[]{:S(2)}, u32[]{:S(2)}) collective-permute-start(f32[72,512]{1,0:T(8,128)S(1)} %get-tuple-element.27.own), channel_id=1, source_target_pairs={{0,1},{1,0},{2,3},{3,2},{4,8},{5,9},{6,10},{7,11},{8,4},{9,5},{10,... | collective-permute-start | bytes 442376 | tf_op jit(solution)/shard_map/ppermute | solution.py:553
  5.5 4.7 %windows_first.1 = (f32[2,448,768]{2,1,0:T(8,128)S(1)}, f32[3,448,768]{2,1,0:T(8,128)S(1)}, f32[256,256]{1,0:T(8,128)S(1)}, f32[256,256]{1,0:T(8,128)S(1)}, bf16...) custom-call(s32[3,8]{1,0:T(4,128)S(1)} %get-tuple-element.25.slots, f32[384,512]{1,0:T(8,128)} %obj_re.3, ...), custom_call_target="tpu_custom_call" | custom-call | flops 4000000000 | bytes 8000000 | tf_op jit(solution)/shard_map/windows_first/pallas_call | solution.py:592
  10.1 0.0 collective-permute-done.by_inner
  10.1 0.0 collective-permute-done.1.by_outer
  10.2 0.3 row_halos.1
  10.4 0.7 %collective-permute-start.2 = (f32[232,128]{1,0:T(8,128)S(1)}, f32[232,128]{1,0:T(8,128)S(1)}, u32[]{:S(2)}, u32[]{:S(2)}) collective-permute-start(f32[232,128]{1,0:T(8,128)S(1)} %get-tuple-element.35), channel_id=1, source_target_pairs={{0,1},{2,3},{1,0},{3,2},{4,5},{6,7},{5,4},{7,6},{8,9},{10,11},{9,8... | collective-permute-start | bytes 356360 | tf_op jit(solution)/shard_map/ppermute | solution.py:554
  11.2 1.3 %collective-permute-start.3 = (f32[232,128]{1,0:T(8,128)S(1)}, f32[232,128]{1,0:T(8,128)S(1)}, u32[]{:S(2)}, u32[]{:S(2)}) collective-permute-start(f32[232,128]{1,0:T(8,128)S(1)} %get-tuple-element.36), channel_id=1, source_target_pairs={{0,4},{1,2},{2,1},{3,7},{4,0},{5,6},{6,5},{7,3},{8,12},{9,10},{10,... | collective-permute-start | bytes 356360 | tf_op jit(solution)/shard_map/ppermute | solution.py:553
  12.5 0.9 %windows_before.1.acc_in = f32[3,448,768]{2,1,0:T(8,128)S(1)} custom-call(s32[3,8]{1,0:T(4,128)S(1)} %get-tuple-element.25.slots, f32[2,448,768]{2,1,0:T(8,128)S(1)} %get-tuple-element.29.cells.cells_in, f32[3,448,768]{2,1,0:T(8,128)S(1)} %get-tuple-element.30.acc_in, f32[256,256]{1,0:T(8,128)S(1)} %get-tuple-element.31.probe_re, ...), custom_call_target="tpu_custom_call", output_to_operand_aliasing={{}: (2, {})} | custom-call | flops 4000000000 | bytes 8000000 | tf_op jit(solution)/shard_map/windows_before/pallas_call | solution.py:618
  13.4 2.8 %collective-permute-done.2.by_inner = f32[232,128]{1,0:T(8,128)S(1)} collective-permute-done((f32[232,128]{1,0:T(8,128)S(1)}, f32[232,128]{1,0:T(8,128)S(1)}, u32[]{:S(2)}, u32[]{:S(2)}) %collective-permute-start.2) | collective-permute-done | bytes 118816 | tf_op jit(solution)/shard_map/ppermute | solution.py:554
  16.2 0.0 collective-permute-done.3.by_outer
  16.2 1.1 %windows_over_edge.1 = (f32[2,448,768]{2,1,0:T(8,128)S(1)}, f32[3,448,768]{2,1,0:T(8,128)S(1)}, f32[72,512]{1,0:T(8,128)S(1)}, f32[72,512]{1,0:T(8,128)S(1)}) custom-call(s32[3,8]{1,0:T(4,128)S(1)} %get-tuple-element.25.slots, f32[2,448,768]{2,1,0:T(8,128)S(1)} %get-tuple-element.29.cells.cells_in, ...), custom_call_target="tpu_custom_call", output_to_operand_aliasing={{0}: (1, {}), {1}: (2, {})} | custom-call | flops 4000000000 | bytes 8000000 | tf_op jit(solution)/shard_map/windows_over_edge/pallas_call | solution.py:630
  17.2 0.1 collective-permute-start.4
  17.3 4.2 %collective-permute-start.5 = (f32[72,512]{1,0:T(8,128)S(1)}, f32[72,512]{1,0:T(8,128)S(1)}, u32[]{:S(2)}, u32[]{:S(2)}) collective-permute-start(f32[72,512]{1,0:T(8,128)S(1)} %get-tuple-element.41), channel_id=1, source_target_pairs={{0,1},{1,0},{2,3},{3,2},{4,8},{5,9},{6,10},{7,11},{8,4},{9,5},{10,... | collective-permute-start | bytes 442376 | tf_op jit(solution)/shard_map/ppermute | solution.py:553
  21.6 1.6 %windows_after.1.acc_in = f32[3,448,768]{2,1,0:T(8,128)S(1)} custom-call(s32[3,8]{1,0:T(4,128)S(1)} %get-tuple-element.25.slots, f32[2,448,768]{2,1,0:T(8,128)S(1)} %get-tuple-element.37.cells, f32[3,448,768]{2,1,0:T(8,128)S(1)} %get-tuple-element.38.acc_in, f32[256,256]{1,0:T(8,128)S(1)} %get-tuple-element.31.probe_re, ...), custom_call_target="tpu_custom_call", output_to_operand_aliasing={{}: (2, {})} | custom-call | flops 4000000000 | bytes 8000000 | tf_op jit(solution)/shard_map/windows_after/pallas_call | solution.py:643
  23.2 0.0 collective-permute-done.4.by_inner
  23.2 1.5 %collective-permute-done.5.by_outer = f32[72,512]{1,0:T(8,128)S(1)} collective-permute-done((f32[72,512]{1,0:T(8,128)S(1)}, f32[72,512]{1,0:T(8,128)S(1)}, u32[]{:S(2)}, u32[]{:S(2)}) %collective-permute-start.5) | collective-permute-done | bytes 147488 | tf_op jit(solution)/shard_map/ppermute | solution.py:553
  24.7 0.3 column_spill.1
  25.0 2.1 %collective-permute-start.6 = (f32[192,128]{1,0:T(8,128)S(1)}, f32[192,128]{1,0:T(8,128)S(1)}, u32[]{:S(2)}, u32[]{:S(2)}) collective-permute-start(f32[192,128]{1,0:T(8,128)S(1)} %get-tuple-element.44), channel_id=1, source_target_pairs={{0,1},{2,3},{1,0},{3,2},{4,5},{6,7},{5,4},{7,6},{8,9},{10,11},{9,8... | collective-permute-start | bytes 294920 | tf_op jit(solution)/shard_map/ppermute | solution.py:554
  27.1 0.2 collective-permute-start.7
  27.3 1.7 %finish_inner.1 = (f32[3,448,768]{2,1,0:T(8,128)S(1)}, f32[384,512]{1,0:T(8,128)}, f32[384,512]{1,0:T(8,128)}) custom-call(s32[3,8]{1,0:T(4,128)S(1)} %get-tuple-element.25.slots, f32[2,448,768]{2,1,0:T(8,128)S(1)} %get-tuple-element.37.cells, f32[3,448,768]{2,1,0:T(8,128)S(1)} %get-tuple-element.42.acc_in, ...), custom_call_target="tpu_custom_call", output_to_operand_aliasing={{0}: (2, {})} | custom-call | flops 4000000000 | bytes 8000000 | tf_op jit(solution)/shard_map/finish_inner/pallas_call | solution.py:672
  29.0 1.5 %collective-permute-done.6.by_inner = f32[192,128]{1,0:T(8,128)S(1)} collective-permute-done((f32[192,128]{1,0:T(8,128)S(1)}, f32[192,128]{1,0:T(8,128)S(1)}, u32[]{:S(2)}, u32[]{:S(2)}) %collective-permute-start.6) | collective-permute-done | bytes 98336 | tf_op jit(solution)/shard_map/ppermute | solution.py:554
  30.5 0.0 collective-permute-done.7.by_outer
  30.5 1.0 %finish_edges.1 = (f32[384,512]{1,0:T(8,128)}, f32[384,512]{1,0:T(8,128)}) custom-call(f32[2,448,768]{2,1,0:T(8,128)S(1)} %get-tuple-element.37.cells, f32[3,448,768]{2,1,0:T(8,128)S(1)} %get-tuple-element.43.acc, f32[192,128]{1,0:T(8,128)S(1)} %collective-permute-done.6.by_inner, ...), custom_call_target="tpu_custom_call", output_to_operand_aliasing={{0}: (4, {}), {1}: (5, {})} | custom-call | tf_op jit(solution)/shard_map/finish_edges/pallas_call | solution.py:683
Async XLA Ops:
  2.3 7.8 %collective-permute-start = (f32[72,512]{1,0:T(8,128)S(1)}, f32[72,512]{1,0:T(8,128)S(1)}, u32[]{:S(2)}, u32[]{:S(2)}) collective-permute-start(f32[72,512]{1,0:T(8,128)S(1)} %get-tuple-element.28), channel_id=1, source_target_pairs={{0,4},{8,12},{16,20},{24,28},{4,0},{12,8},{20,16},{28,24},{1,5},{9... | collective-permute-start | bytes 442376 | tf_op jit(solution)/shard_map/ppermute | solution.py:554
  2.8 7.3 %collective-permute-start.1 = (f32[72,512]{1,0:T(8,128)S(1)}, f32[72,512]{1,0:T(8,128)S(1)}, u32[]{:S(2)}, u32[]{:S(2)}) collective-permute-start(f32[72,512]{1,0:T(8,128)S(1)} %get-tuple-element.27.own), channel_id=1, source_target_pairs={{0,1},{1,0},{2,3},{3,2},{4,8},{5,9},{6,10},{7,11},{8,4},{9,5},{10,... | collective-permute-start | bytes 442376 | tf_op jit(solution)/shard_map/ppermute | solution.py:553
  10.4 5.7 %collective-permute-start.2 = (f32[232,128]{1,0:T(8,128)S(1)}, f32[232,128]{1,0:T(8,128)S(1)}, u32[]{:S(2)}, u32[]{:S(2)}) collective-permute-start(f32[232,128]{1,0:T(8,128)S(1)} %get-tuple-element.35), channel_id=1, source_target_pairs={{0,1},{2,3},{1,0},{3,2},{4,5},{6,7},{5,4},{7,6},{8,9},{10,11},{9,8... | collective-permute-start | bytes 356360 | tf_op jit(solution)/shard_map/ppermute | solution.py:554
  11.2 5.0 %collective-permute-start.3 = (f32[232,128]{1,0:T(8,128)S(1)}, f32[232,128]{1,0:T(8,128)S(1)}, u32[]{:S(2)}, u32[]{:S(2)}) collective-permute-start(f32[232,128]{1,0:T(8,128)S(1)} %get-tuple-element.36), channel_id=1, source_target_pairs={{0,4},{1,2},{2,1},{3,7},{4,0},{5,6},{6,5},{7,3},{8,12},{9,10},{10,... | collective-permute-start | bytes 356360 | tf_op jit(solution)/shard_map/ppermute | solution.py:553
  17.2 6.0 %collective-permute-start.4 = (f32[72,512]{1,0:T(8,128)S(1)}, f32[72,512]{1,0:T(8,128)S(1)}, u32[]{:S(2)}, u32[]{:S(2)}) collective-permute-start(f32[72,512]{1,0:T(8,128)S(1)} %get-tuple-element.40), channel_id=1, source_target_pairs={{0,4},{8,12},{16,20},{24,28},{4,0},{12,8},{20,16},{28,24},{1,5},{9... | collective-permute-start | bytes 442376 | tf_op jit(solution)/shard_map/ppermute | solution.py:554
  17.3 7.4 %collective-permute-start.5 = (f32[72,512]{1,0:T(8,128)S(1)}, f32[72,512]{1,0:T(8,128)S(1)}, u32[]{:S(2)}, u32[]{:S(2)}) collective-permute-start(f32[72,512]{1,0:T(8,128)S(1)} %get-tuple-element.41), channel_id=1, source_target_pairs={{0,1},{1,0},{2,3},{3,2},{4,8},{5,9},{6,10},{7,11},{8,4},{9,5},{10,... | collective-permute-start | bytes 442376 | tf_op jit(solution)/shard_map/ppermute | solution.py:553
  25.0 5.5 %collective-permute-start.6 = (f32[192,128]{1,0:T(8,128)S(1)}, f32[192,128]{1,0:T(8,128)S(1)}, u32[]{:S(2)}, u32[]{:S(2)}) collective-permute-start(f32[192,128]{1,0:T(8,128)S(1)} %get-tuple-element.44), channel_id=1, source_target_pairs={{0,1},{2,3},{1,0},{3,2},{4,5},{6,7},{5,4},{7,6},{8,9},{10,11},{9,8... | collective-permute-start | bytes 294920 | tf_op jit(solution)/shard_map/ppermute | solution.py:554
  27.1 3.4 %collective-permute-start.7 = (f32[192,128]{1,0:T(8,128)S(1)}, f32[192,128]{1,0:T(8,128)S(1)}, u32[]{:S(2)}, u32[]{:S(2)}) collective-permute-start(f32[192,128]{1,0:T(8,128)S(1)} %get-tuple-element.45), channel_id=1, source_target_pairs={{0,4},{1,2},{2,1},{3,7},{4,0},{5,6},{6,5},{7,3},{8,12},{9,10},{10,... | collective-permute-start | bytes 294920 | tf_op jit(solution)/shard_map/ppermute | solution.py:553

commit v4 on v3

--- a/solution.py
+++ b/solution.py
@@ -174,16 +174,19 @@
         copy.wait()
 
 
-def row_edges(counts, obj_re, obj_im, offsets, chosen, to_inner, to_outer, marked, places, frame_of, sems):
+def row_edges(counts, obj_re, obj_im, offsets, chosen, to_outer, to_inner, marked, places, frame_of, sems):
     tile_r = obj_re.shape[0]
     odd = is_odd("row")
     low = pl.multiple_of(jnp.where(odd, 0, tile_r - HALO), 16)
     high = pl.multiple_of(jnp.where(odd, tile_r - HALO, 0), 16)
     pairs = [(offsets, places), (chosen, frame_of)]
+    tiles = obj_re.shape[1] // LANES
     for k, ref in enumerate((obj_re, obj_im)):
-        rows = slice(k * HALO, (k + 1) * HALO)
-        pairs.append((ref.at[pl.ds(high, HALO)], to_outer.at[rows]))
-        pairs.append((ref.at[pl.ds(low, HALO)], to_inner.at[rows]))
+        for t in range(tiles):
+            lanes = slice(t * LANES, (t + 1) * LANES)
+            rows = slice((2 * t + k) * HALO, (2 * t + k + 1) * HALO)
+            pairs.append((ref.at[pl.ds(high, HALO), lanes], to_outer.at[rows]))
+            pairs.append((ref.at[pl.ds(low, HALO), lanes], to_inner.at[rows]))
     copies = fetch(pairs, sems)
     finish_all(copies[:2])
     place = places[0, 0]
@@ -192,7 +195,8 @@
     marked[0:2, :] = place
     marked[2:3, :] = frame_of[0]
     for message in (to_inner, to_outer):
-        message[2 * HALO : 2 * HALO + 2, 0 : place.shape[1]] = place.astype(jnp.float32)
+        first = 2 * HALO * tiles
+        message[first : first + 2, 0 : place.shape[1]] = place.astype(jnp.float32)
     finish_all(copies[2:])
 
 
@@ -254,16 +258,19 @@
         )
 
 
-def row_halos(cells_in, own, by_inner, by_outer, cells, marks, to_inner, to_outer):
+def row_halos(cells_in, own, by_outer, by_inner, cells, marks, to_inner, to_outer):
     rows, width = cells.shape[1:]
-    middle = slice(LANES, width - LANES)
     before, after = received(by_inner, by_outer, "row")
+    tiles = width // LANES - 2
     for k in (0, 1):
-        cells[k, 0:HALO, middle] = before[k * HALO : (k + 1) * HALO]
-        cells[k, rows - HALO : rows, middle] = after[k * HALO : (k + 1) * HALO]
-    first_mark = 2 * HALO
+        for t in range(tiles):
+            lanes = slice((t + 1) * LANES, (t + 2) * LANES)
+            part = slice((2 * t + k) * HALO, (2 * t + k + 1) * HALO)
+            cells[k, 0:HALO, lanes] = before[part]
+            cells[k, rows - HALO : rows, lanes] = after[part]
+    first = 2 * HALO * tiles
     for i, message in enumerate((own[...], before, after)):
-        marks[2 * i : 2 * i + 2, :] = message[first_mark : first_mark + 2, 0:LANES]
+        marks[2 * i : 2 * i + 2, :] = message[first : first + 2]
     half = rows // 2
     to_left = pack_lanes(cells, 0, rows, slice(LANES, 2 * LANES), 0)
     to_right = pack_lanes(cells, 0, rows, slice(width - 2 * LANES, width - LANES), LANES - HALO)
@@ -467,14 +474,17 @@
 
 
 def windows_over_edge(
-    slots, cells_in, acc_in, probe_re, probe_im, table, frames, by_inner, by_outer,
-    cells, acc, to_inner, to_outer, order,
+    marked, cells_in, acc_in, probe_re, probe_im, table, frames, by_inner, by_outer,
+    cells, acc, to_outer, to_inner, order, slots, sem,
 ):
+    scalars = pltpu.make_async_copy(marked, slots, sem)
+    scalars.start()
     rows, width = acc.shape[1:]
     before, after = received(by_inner, by_outer, "col")
     for tile, packed in ((slice(0, LANES), before), (slice(width - LANES, width), after)):
         for layer, row, part in pieces(packed, rows):
             cells[layer, row : row + part.shape[0], tile] = part
+    scalars.wait()
     run_windows(OVER, slots, cells, acc, probe_re, probe_im, table, frames, order)
     odd = is_odd("row")
     strips = []
@@ -485,7 +495,7 @@
     to_outer[...] = jnp.where(odd, strips[1], strips[0])
 
 
-def column_spill(acc_in, by_inner, by_outer, acc, to_inner, to_outer):
+def column_spill(acc_in, by_outer, by_inner, acc, to_inner, to_outer):
     rows, width = acc.shape[1:]
     before, after = received(by_inner, by_outer, "row")
     for start, came in ((HALO, before), (rows - 2 * HALO, after)):
@@ -550,8 +560,8 @@
             else:
                 there = (row, partner[col]) if col in partner else (row ^ 1, col)
             pairs.append((row * n_col + col, there[0] * n_col + there[1]))
+    by_inner = lax.ppermute(to_inner, axis, inner + [(j, i) for i, j in inner])
     by_outer = lax.ppermute(to_outer, ("row", "col"), pairs)
-    by_inner = lax.ppermute(to_inner, axis, inner + [(j, i) for i, j in inner])
     return by_inner, by_outer
 
 
@@ -574,14 +584,15 @@
     dma = pltpu.SemaphoreType.DMA
 
     places = jnp.swapaxes(offsets, 2, 3)
-    edge = f32(2 * HALO + MARKS, tile_c)
-    to_inner, to_outer, marked = pl.pallas_call(
+    edge = f32(2 * HALO * (tile_c // LANES) + MARKS, LANES)
+    to_outer, to_inner, marked = pl.pallas_call(
         row_edges,
         out_shape=(edge, edge, jax.ShapeDtypeStruct((3, slots), jnp.int32)),
         in_specs=[SMEM] + [HBM] * 4,
         out_specs=(VMEM, VMEM, VMEM),
         scratch_shapes=[
-            pltpu.VMEM(places.shape, jnp.int32), pltpu.VMEM(frame_index.shape, jnp.int32), dma((6,)),
+            pltpu.VMEM(places.shape, jnp.int32), pltpu.VMEM(frame_index.shape, jnp.int32),
+            dma((2 + 4 * (tile_c // LANES),)),
         ],
         compiler_params=SMALL,
         name="row_edges",
@@ -612,7 +623,7 @@
         input_output_aliases={0: 0},
         compiler_params=SMALL,
         name="row_halos",
-    )(cells, to_outer, by_inner, by_outer)
+    )(cells, to_outer, by_outer, by_inner)
     edges = swap(to_inner, to_outer, "col")
 
     acc = pl.pallas_call(
@@ -627,12 +638,13 @@
         name="windows_before",
     )(marked, cells, acc, *fixed)
 
-    cells, acc, to_inner, to_outer = pl.pallas_call(
+    edge = f32(2 * HALO + MARKS, tile_c)
+    cells, acc, to_outer, to_inner = pl.pallas_call(
         windows_over_edge,
         out_shape=(cells_shape, acc_shape, edge, edge),
-        in_specs=[SMEM] + [VMEM] * 8,
+        in_specs=[VMEM] * 9,
         out_specs=(VMEM,) * 4,
-        scratch_shapes=[order],
+        scratch_shapes=[order, pltpu.SMEM((3, slots), jnp.int32), dma(())],
         input_output_aliases={1: 0, 2: 1},
         compiler_params=PARAMS,
         cost_estimate=BUSY,
@@ -664,7 +676,7 @@
         input_output_aliases={0: 0},
         compiler_params=SMALL,
         name="column_spill",
-    )(acc, by_inner, by_outer)
+    )(acc, by_outer, by_inner)
     by_inner, by_outer = swap(to_inner, to_outer, "col")
 
     near = [pltpu.VMEM((tile_r, tile_c), jnp.float32)] * 2

time: 31.9 us -> 31 us (0.972)
  the two profiles are of different devices: /device:TPU:0 before, /device:TPU:20 now
where the time goes in v4:
time: 31 us; the launch traced here: 31.4 us
  Pallas kernels  12.4 us (40%)
  waiting for transfers between devices  12.4 us (40%)
  starting transfers between devices  5.04 us (16%)
  between operations  1.52 us (5%)
    ppermute x4, waiting for transfers between devices, swap(): by_outer = lax.ppermute(to_outer, ('row', 'col'), pairs)  7.56 us
    ppermute x4, waiting for transfers between devices, swap(): by_inner = lax.ppermute(to_inner, axis, inner + [(j, i) for i, j in inner])  4.85 us
    pallas_call x1, Pallas kernels, shards(): pl.pallas_call(windows_first, out_shape=(cells_shape, acc_shape, f32(*pro...  4.67 us
    ppermute x4, starting transfers between devices, swap(): by_inner = lax.ppermute(to_inner, axis, inner + [(j, i) for i, j in inner])  3.03 us
    ppermute x4, starting transfers between devices, swap(): by_outer = lax.ppermute(to_outer, ('row', 'col'), pairs)  2 us
    pallas_call x1, Pallas kernels, shards(): pl.pallas_call(finish_inner, out_shape=(acc_shape, *new), in_specs=[SMEM]...  1.72 us
    pallas_call x1, Pallas kernels, shards(): pl.pallas_call(windows_after, out_shape=acc_shape, in_specs=[SMEM] + [VME...  1.48 us
    pallas_call x1, Pallas kernels, shards(): pl.pallas_call(row_edges, out_shape=(edge, edge, jax.ShapeDtypeStruct((3,...  1.08 us
  transfers between devices with their start and end apart: 8, of which 6 were waited for; matrix products, arithmetic and copies ran while one was open for 0% of the time, Pallas kernels for 28%

profile of v4, /device:TPU:20, one launch (start us, length us, event | category | flops | bytes accessed | tf_op | source)
XLA Modules:
  0.0 31.4 jit_solution(12735298061197281103)
XLA Ops:
  1.3 1.1 %row_edges.1 = (f32[264,128]{1,0:T(8,128)S(1)}, f32[264,128]{1,0:T(8,128)S(1)}, s32[3,8]{1,0:T(4,128)S(1)}) custom-call(s32[1,1]{1,0:T(1,128)S(6)} %copy.29.counts, f32[384,512]{1,0:T(8,128)} %obj_re.3, f32[384,512]{1,0:T(8,128)} %obj_im.3, s32[1,1,2,8]{3,2,1,0:T(2,128)} %bitcast.2, s32[1,1,8]{2,1,0:T(1,128)} %chosen.1), custom_call_target="tpu_custom_call" | custom-call | tf_op jit(solution)/shard_map/row_edges/pallas_call | solution.py:588
  2.4 0.1 collective-permute-start.1
  2.4 1.5 %collective-permute-start = (f32[264,128]{1,0:T(8,128)S(1)}, f32[264,128]{1,0:T(8,128)S(1)}, u32[]{:S(2)}, u32[]{:S(2)}) collective-permute-start(f32[264,128]{1,0:T(8,128)S(1)} %get-tuple-element.27.own), channel_id=1, source_target_pairs={{0,1},{1,0},{2,3},{3,2},{4,8},{5,9},{6,10},{7,11},{8,4},{9,5},{10,... | collective-permute-start | bytes 405512 | tf_op jit(solution)/shard_map/ppermute | solution.py:564
  4.0 4.7 %windows_first.1 = (f32[2,448,768]{2,1,0:T(8,128)S(1)}, f32[3,448,768]{2,1,0:T(8,128)S(1)}, f32[256,256]{1,0:T(8,128)S(1)}, f32[256,256]{1,0:T(8,128)S(1)}, bf16...) custom-call(s32[3,8]{1,0:T(4,128)S(1)} %get-tuple-element.25.slots.marked, f32[384,512]{1,0:T(8,128)} %obj_re.3, ...), custom_call_target="tpu_custom_call" | custom-call | flops 4000000000 | bytes 8000000 | tf_op jit(solution)/shard_map/windows_first/pallas_call | solution.py:603
  8.7 0.0 collective-permute-done.1.by_inner
  8.7 0.3 collective-permute-done.by_outer
  8.9 0.3 row_halos.1
  9.2 1.6 %collective-permute-start.2 = (f32[232,128]{1,0:T(8,128)S(1)}, f32[232,128]{1,0:T(8,128)S(1)}, u32[]{:S(2)}, u32[]{:S(2)}) collective-permute-start(f32[232,128]{1,0:T(8,128)S(1)} %get-tuple-element.35), channel_id=1, source_target_pairs={{0,1},{2,3},{1,0},{3,2},{4,5},{6,7},{5,4},{7,6},{8,9},{10,11},{9,8... | collective-permute-start | bytes 356360 | tf_op jit(solution)/shard_map/ppermute | solution.py:563
  10.9 0.0 collective-permute-start.3
  10.9 0.9 %windows_before.1.acc_in = f32[3,448,768]{2,1,0:T(8,128)S(1)} custom-call(s32[3,8]{1,0:T(4,128)S(1)} %get-tuple-element.25.slots.marked, f32[2,448,768]{2,1,0:T(8,128)S(1)} %get-tuple-element.29.cells.cells_in, f32[3,448,768]{2,1,0:T(8,128)S(1)} %get-tuple-element.30.acc_in, ...), custom_call_target="tpu_custom_call", output_to_operand_aliasing={{}: (2, {})} | custom-call | flops 4000000000 | bytes 8000000 | tf_op jit(solution)/shard_map/windows_before/pallas_call | solution.py:629
  11.8 3.0 %collective-permute-done.2.by_inner = f32[232,128]{1,0:T(8,128)S(1)} collective-permute-done((f32[232,128]{1,0:T(8,128)S(1)}, f32[232,128]{1,0:T(8,128)S(1)}, u32[]{:S(2)}, u32[]{:S(2)}) %collective-permute-start.2) | collective-permute-done | bytes 118816 | tf_op jit(solution)/shard_map/ppermute | solution.py:563
  14.8 1.5 %collective-permute-done.3.by_outer = f32[232,128]{1,0:T(8,128)S(1)} collective-permute-done((f32[232,128]{1,0:T(8,128)S(1)}, f32[232,128]{1,0:T(8,128)S(1)}, u32[]{:S(2)}, u32[]{:S(2)}) %collective-permute-start.3) | collective-permute-done | bytes 118816 | tf_op jit(solution)/shard_map/ppermute | solution.py:564
  16.2 1.0 %windows_over_edge.1 = (f32[2,448,768]{2,1,0:T(8,128)S(1)}, f32[3,448,768]{2,1,0:T(8,128)S(1)}, f32[72,512]{1,0:T(8,128)S(1)}, f32[72,512]{1,0:T(8,128)S(1)}) custom-call(s32[3,8]{1,0:T(4,128)S(1)} %get-tuple-element.25.slots.marked, f32[2,448,768]{2,1,0:T(8,128)S(1)} %get-tuple-element.29.cells.cells_in, ...), custom_call_target="tpu_custom_call", output_to_operand_aliasing={{0}: (1, {}), {1}: (2, {})} | custom-call | flops 4000000000 | bytes 8000000 | tf_op jit(solution)/shard_map/windows_over_edge/pallas_call | solution.py:642
  17.2 0.5 %collective-permute-start.4 = (f32[72,512]{1,0:T(8,128)S(1)}, f32[72,512]{1,0:T(8,128)S(1)}, u32[]{:S(2)}, u32[]{:S(2)}) collective-permute-start(f32[72,512]{1,0:T(8,128)S(1)} %get-tuple-element.40), channel_id=1, source_target_pairs={{0,1},{1,0},{2,3},{3,2},{4,8},{5,9},{6,10},{7,11},{8,4},{9,5},{10,... | collective-permute-start | bytes 442376 | tf_op jit(solution)/shard_map/ppermute | solution.py:564
  17.7 0.2 collective-permute-start.5
  17.9 1.5 %windows_after.1.acc_in = f32[3,448,768]{2,1,0:T(8,128)S(1)} custom-call(s32[3,8]{1,0:T(4,128)S(1)} %get-tuple-element.25.slots.marked, f32[2,448,768]{2,1,0:T(8,128)S(1)} %get-tuple-element.37.cells, f32[3,448,768]{2,1,0:T(8,128)S(1)} %get-tuple-element.38.acc_in, f32[256,256]{1,0:T(8,128)S(1)} %get-tuple-element.31.probe_re, ...), custom_call_target="tpu_custom_call", output_to_operand_aliasing={{}: (2, {})} | custom-call | flops 4000000000 | bytes 8000000 | tf_op jit(solution)/shard_map/windows_after/pallas_call | solution.py:655
  19.4 4.8 %collective-permute-done.4.by_outer = f32[72,512]{1,0:T(8,128)S(1)} collective-permute-done((f32[72,512]{1,0:T(8,128)S(1)}, f32[72,512]{1,0:T(8,128)S(1)}, u32[]{:S(2)}, u32[]{:S(2)}) %collective-permute-start.4) | collective-permute-done | bytes 147488 | tf_op jit(solution)/shard_map/ppermute | solution.py:564
  24.1 0.0 collective-permute-done.5.by_inner
  24.1 0.3 column_spill.1
  24.4 1.1 %collective-permute-start.6 = (f32[192,128]{1,0:T(8,128)S(1)}, f32[192,128]{1,0:T(8,128)S(1)}, u32[]{:S(2)}, u32[]{:S(2)}) collective-permute-start(f32[192,128]{1,0:T(8,128)S(1)} %get-tuple-element.44), channel_id=1, source_target_pairs={{0,1},{2,3},{1,0},{3,2},{4,5},{6,7},{5,4},{7,6},{8,9},{10,11},{9,8... | collective-permute-start | bytes 294920 | tf_op jit(solution)/shard_map/ppermute | solution.py:563
  25.5 0.0 collective-permute-start.7
  25.5 1.7 %finish_inner.1 = (f32[3,448,768]{2,1,0:T(8,128)S(1)}, f32[384,512]{1,0:T(8,128)}, f32[384,512]{1,0:T(8,128)}) custom-call(s32[3,8]{1,0:T(4,128)S(1)} %get-tuple-element.25.slots.marked, f32[2,448,768]{2,1,0:T(8,128)S(1)} %get-tuple-element.37.cells, f32[3,448,768]{2,1,0:T(8,128)S(1)} %get-tuple-element.42.acc_in, ...), custom_call_target="tpu_custom_call", output_to_operand_aliasing={{0}: (2, {})} | custom-call | flops 4000000000 | bytes 8000000 | tf_op jit(solution)/shard_map/finish_inner/pallas_call | solution.py:684
  27.3 1.8 %collective-permute-done.6.by_inner = f32[192,128]{1,0:T(8,128)S(1)} collective-permute-done((f32[192,128]{1,0:T(8,128)S(1)}, f32[192,128]{1,0:T(8,128)S(1)}, u32[]{:S(2)}, u32[]{:S(2)}) %collective-permute-start.6) | collective-permute-done | bytes 98336 | tf_op jit(solution)/shard_map/ppermute | solution.py:563
  29.1 1.1 %collective-permute-done.7.by_outer = f32[192,128]{1,0:T(8,128)S(1)} collective-permute-done((f32[192,128]{1,0:T(8,128)S(1)}, f32[192,128]{1,0:T(8,128)S(1)}, u32[]{:S(2)}, u32[]{:S(2)}) %collective-permute-start.7) | collective-permute-done | bytes 98336 | tf_op jit(solution)/shard_map/ppermute | solution.py:564
  30.1 1.0 %finish_edges.1 = (f32[384,512]{1,0:T(8,128)}, f32[384,512]{1,0:T(8,128)}) custom-call(f32[2,448,768]{2,1,0:T(8,128)S(1)} %get-tuple-element.37.cells, f32[3,448,768]{2,1,0:T(8,128)S(1)} %get-tuple-element.43.acc, f32[192,128]{1,0:T(8,128)S(1)} %collective-permute-done.6.by_inner, ...), custom_call_target="tpu_custom_call", output_to_operand_aliasing={{0}: (4, {}), {1}: (5, {})} | custom-call | tf_op jit(solution)/shard_map/finish_edges/pallas_call | solution.py:695
Async XLA Ops:
  2.4 6.3 %collective-permute-start.1 = (f32[264,128]{1,0:T(8,128)S(1)}, f32[264,128]{1,0:T(8,128)S(1)}, u32[]{:S(2)}, u32[]{:S(2)}) collective-permute-start(f32[264,128]{1,0:T(8,128)S(1)} %get-tuple-element.28), channel_id=1, source_target_pairs={{0,4},{8,12},{16,20},{24,28},{4,0},{12,8},{20,16},{28,24},{1,5},{9... | collective-permute-start | bytes 405512 | tf_op jit(solution)/shard_map/ppermute | solution.py:563
  2.4 6.5 %collective-permute-start = (f32[264,128]{1,0:T(8,128)S(1)}, f32[264,128]{1,0:T(8,128)S(1)}, u32[]{:S(2)}, u32[]{:S(2)}) collective-permute-start(f32[264,128]{1,0:T(8,128)S(1)} %get-tuple-element.27.own), channel_id=1, source_target_pairs={{0,1},{1,0},{2,3},{3,2},{4,8},{5,9},{6,10},{7,11},{8,4},{9,5},{10,... | collective-permute-start | bytes 405512 | tf_op jit(solution)/shard_map/ppermute | solution.py:564
  9.2 5.6 %collective-permute-start.2 = (f32[232,128]{1,0:T(8,128)S(1)}, f32[232,128]{1,0:T(8,128)S(1)}, u32[]{:S(2)}, u32[]{:S(2)}) collective-permute-start(f32[232,128]{1,0:T(8,128)S(1)} %get-tuple-element.35), channel_id=1, source_target_pairs={{0,1},{2,3},{1,0},{3,2},{4,5},{6,7},{5,4},{7,6},{8,9},{10,11},{9,8... | collective-permute-start | bytes 356360 | tf_op jit(solution)/shard_map/ppermute | solution.py:563
  10.9 5.4 %collective-permute-start.3 = (f32[232,128]{1,0:T(8,128)S(1)}, f32[232,128]{1,0:T(8,128)S(1)}, u32[]{:S(2)}, u32[]{:S(2)}) collective-permute-start(f32[232,128]{1,0:T(8,128)S(1)} %get-tuple-element.36), channel_id=1, source_target_pairs={{0,4},{1,2},{2,1},{3,7},{4,0},{5,6},{6,5},{7,3},{8,12},{9,10},{10,... | collective-permute-start | bytes 356360 | tf_op jit(solution)/shard_map/ppermute | solution.py:564
  17.2 6.9 %collective-permute-start.4 = (f32[72,512]{1,0:T(8,128)S(1)}, f32[72,512]{1,0:T(8,128)S(1)}, u32[]{:S(2)}, u32[]{:S(2)}) collective-permute-start(f32[72,512]{1,0:T(8,128)S(1)} %get-tuple-element.40), channel_id=1, source_target_pairs={{0,1},{1,0},{2,3},{3,2},{4,8},{5,9},{6,10},{7,11},{8,4},{9,5},{10,... | collective-permute-start | bytes 442376 | tf_op jit(solution)/shard_map/ppermute | solution.py:564
  17.7 6.4 %collective-permute-start.5 = (f32[72,512]{1,0:T(8,128)S(1)}, f32[72,512]{1,0:T(8,128)S(1)}, u32[]{:S(2)}, u32[]{:S(2)}) collective-permute-start(f32[72,512]{1,0:T(8,128)S(1)} %get-tuple-element.41), channel_id=1, source_target_pairs={{0,4},{8,12},{16,20},{24,28},{4,0},{12,8},{20,16},{28,24},{1,5},{9... | collective-permute-start | bytes 442376 | tf_op jit(solution)/shard_map/ppermute | solution.py:563
  24.4 4.7 %collective-permute-start.6 = (f32[192,128]{1,0:T(8,128)S(1)}, f32[192,128]{1,0:T(8,128)S(1)}, u32[]{:S(2)}, u32[]{:S(2)}) collective-permute-start(f32[192,128]{1,0:T(8,128)S(1)} %get-tuple-element.44), channel_id=1, source_target_pairs={{0,1},{2,3},{1,0},{3,2},{4,5},{6,7},{5,4},{7,6},{8,9},{10,11},{9,8... | collective-permute-start | bytes 294920 | tf_op jit(solution)/shard_map/ppermute | solution.py:563
  25.5 4.6 %collective-permute-start.7 = (f32[192,128]{1,0:T(8,128)S(1)}, f32[192,128]{1,0:T(8,128)S(1)}, u32[]{:S(2)}, u32[]{:S(2)}) collective-permute-start(f32[192,128]{1,0:T(8,128)S(1)} %get-tuple-element.45), channel_id=1, source_target_pairs={{0,4},{1,2},{2,1},{3,7},{4,0},{5,6},{6,5},{7,3},{8,12},{9,10},{10,... | collective-permute-start | bytes 294920 | tf_op jit(solution)/shard_map/ppermute | solution.py:564

commit v5 on v4

--- a/solution.py
+++ b/solution.py
@@ -352,15 +352,18 @@
         add_window(acc, 0, where, keep, w_re * back_re + w_im * back_im)
         add_window(acc, 1, where, keep, w_re * back_im - w_im * back_re)
 
+    def rows_of(stacked):
+        return [stacked[i : i + P_SIZE] for i in range(0, stacked.shape[0], P_SIZE)]
+
     def step(group):
         frame = [frame_of(slot) for slot in group]
         loaded = [load(slot) for slot in group]
-        state = [forward_columns(x[1], x[2], table) for x in loaded]
-        state = [forward_rows(*x, table) for x in state]
+        stacked = forward_columns(below(*(x[1] for x in loaded)), below(*(x[2] for x in loaded)), table)
+        state = [forward_rows(*x, table) for x in zip(*map(rows_of, stacked))]
         state = [residual(x, f) for x, f in zip(state, frame)]
         state = [back_rows(x, table) for x in state]
-        state = [back_columns(x, table) for x in state]
-        for x, back in zip(loaded, state):
+        stacked = back_columns([below(*parts) for parts in zip(*state)], table)
+        for x, back in zip(loaded, zip(*map(rows_of, stacked))):
             place(x[0], *back)
 
     def pair_step(pair, carry):

time: 31 us -> 32.4 us (1.045); the launches traced: 31.4 us -> 31.8 us
  Pallas kernels: 12.4 us -> 16.8 us
  waiting for transfers between devices: 12.4 us -> 9.92 us
  starting transfers between devices: 5.04 us -> 3.53 us
    ppermute x4, waiting for transfers between devices: 7.56 us -> 4.24 us  [swap(): by_outer = lax.ppermute(to_outer, ('row', 'col'), pairs)]
    pallas_call x1, Pallas kernels: 0.97 us -> 3.57 us  [shards(): pl.pallas_call(windows_over_edge, out_shape=(cells_shape, acc_shape, edge...]
    pallas_call x1, Pallas kernels: 1.48 us -> 2.79 us  [shards(): pl.pallas_call(windows_after, out_shape=acc_shape, in_specs=[SMEM] + [VME...]
    ppermute x4, starting transfers between devices: 3.03 us -> 1.85 us  [swap(): by_inner = lax.ppermute(to_inner, axis, inner + [(j, i) for i, j in inner])]
    ppermute x4, waiting for transfers between devices: 4.85 us -> 5.68 us  [swap(): by_inner = lax.ppermute(to_inner, axis, inner + [(j, i) for i, j in inner])]
    pallas_call x1, Pallas kernels: 0.89 us -> 1.39 us  [shards(): pl.pallas_call(windows_before, out_shape=acc_shape, in_specs=[SMEM] + [VM...]
  transfers between devices with their start and end apart: 8 -> 8, of which waited for: 6 -> 6; matrix products, arithmetic and copies ran while one was open for 0% -> 0% of each run, Pallas kernels for 28% -> 33%
where the time goes in v5:
time: 32.4 us; the launch traced here: 31.8 us
  Pallas kernels  16.8 us (52%)
  waiting for transfers between devices  9.92 us (31%)
  starting transfers between devices  3.53 us (11%)
  between operations  1.55 us (5%)
    ppermute x4, waiting for transfers between devices, swap(): by_inner = lax.ppermute(to_inner, axis, inner + [(j, i) for i, j in inner])  5.68 us
    pallas_call x1, Pallas kernels, shards(): pl.pallas_call(windows_first, out_shape=(cells_shape, acc_shape, f32(*pro...  4.67 us
    ppermute x4, waiting for transfers between devices, swap(): by_outer = lax.ppermute(to_outer, ('row', 'col'), pairs)  4.24 us
    pallas_call x1, Pallas kernels, shards(): pl.pallas_call(windows_over_edge, out_shape=(cells_shape, acc_shape, edge...  3.57 us
    pallas_call x1, Pallas kernels, shards(): pl.pallas_call(windows_after, out_shape=acc_shape, in_specs=[SMEM] + [VME...  2.79 us
    ppermute x4, starting transfers between devices, swap(): by_inner = lax.ppermute(to_inner, axis, inner + [(j, i) for i, j in inner])  1.85 us
    pallas_call x1, Pallas kernels, shards(): pl.pallas_call(finish_inner, out_shape=(acc_shape, *new), in_specs=[SMEM]...  1.73 us
    ppermute x4, starting transfers between devices, swap(): by_outer = lax.ppermute(to_outer, ('row', 'col'), pairs)  1.68 us
  transfers between devices with their start and end apart: 8, of which 6 were waited for; matrix products, arithmetic and copies ran while one was open for 0% of the time, Pallas kernels for 33%

profile of v5, /device:TPU:20, one launch (start us, length us, event | category | flops | bytes accessed | tf_op | source)
XLA Modules:
  0.0 31.8 jit_solution(4490646101593921922)
XLA Ops:
  1.3 1.1 %row_edges.1 = (f32[264,128]{1,0:T(8,128)S(1)}, f32[264,128]{1,0:T(8,128)S(1)}, s32[3,8]{1,0:T(4,128)S(1)}) custom-call(s32[1,1]{1,0:T(1,128)S(6)} %copy.29.counts, f32[384,512]{1,0:T(8,128)} %obj_re.3, f32[384,512]{1,0:T(8,128)} %obj_im.3, s32[1,1,2,8]{3,2,1,0:T(2,128)} %bitcast.2, s32[1,1,8]{2,1,0:T(1,128)} %chosen.1), custom_call_target="tpu_custom_call" | custom-call | tf_op jit(solution)/shard_map/row_edges/pallas_call | solution.py:591
  2.4 0.1 collective-permute-start.1
  2.4 1.5 %collective-permute-start = (f32[264,128]{1,0:T(8,128)S(1)}, f32[264,128]{1,0:T(8,128)S(1)}, u32[]{:S(2)}, u32[]{:S(2)}) collective-permute-start(f32[264,128]{1,0:T(8,128)S(1)} %get-tuple-element.27.own), channel_id=1, source_target_pairs={{0,1},{1,0},{2,3},{3,2},{4,8},{5,9},{6,10},{7,11},{8,4},{9,5},{10,... | collective-permute-start | bytes 405512 | tf_op jit(solution)/shard_map/ppermute | solution.py:567
  4.0 4.7 %windows_first.1 = (f32[2,448,768]{2,1,0:T(8,128)S(1)}, f32[3,448,768]{2,1,0:T(8,128)S(1)}, f32[256,256]{1,0:T(8,128)S(1)}, f32[256,256]{1,0:T(8,128)S(1)}, bf16...) custom-call(s32[3,8]{1,0:T(4,128)S(1)} %get-tuple-element.25.slots.marked, f32[384,512]{1,0:T(8,128)} %obj_re.3, ...), custom_call_target="tpu_custom_call" | custom-call | flops 4000000000 | bytes 8000000 | tf_op jit(solution)/shard_map/windows_first/pallas_call | solution.py:606
  8.7 0.0 collective-permute-done.1.by_inner
  8.7 0.3 collective-permute-done.by_outer
  8.9 0.3 row_halos.1
  9.2 1.6 %collective-permute-start.2 = (f32[232,128]{1,0:T(8,128)S(1)}, f32[232,128]{1,0:T(8,128)S(1)}, u32[]{:S(2)}, u32[]{:S(2)}) collective-permute-start(f32[232,128]{1,0:T(8,128)S(1)} %get-tuple-element.35), channel_id=1, source_target_pairs={{0,1},{2,3},{1,0},{3,2},{4,5},{6,7},{5,4},{7,6},{8,9},{10,11},{9,8... | collective-permute-start | bytes 356360 | tf_op jit(solution)/shard_map/ppermute | solution.py:566
  10.9 0.0 collective-permute-start.3
  10.9 1.4 %windows_before.1.acc_in = f32[3,448,768]{2,1,0:T(8,128)S(1)} custom-call(s32[3,8]{1,0:T(4,128)S(1)} %get-tuple-element.25.slots.marked, f32[2,448,768]{2,1,0:T(8,128)S(1)} %get-tuple-element.29.cells.cells_in, f32[3,448,768]{2,1,0:T(8,128)S(1)} %get-tuple-element.30.acc_in, ...), custom_call_target="tpu_custom_call", output_to_operand_aliasing={{}: (2, {})} | custom-call | flops 4000000000 | bytes 8000000 | tf_op jit(solution)/shard_map/windows_before/pallas_call | solution.py:632
  12.3 2.9 %collective-permute-done.2.by_inner = f32[232,128]{1,0:T(8,128)S(1)} collective-permute-done((f32[232,128]{1,0:T(8,128)S(1)}, f32[232,128]{1,0:T(8,128)S(1)}, u32[]{:S(2)}, u32[]{:S(2)}) %collective-permute-start.2) | collective-permute-done | bytes 118816 | tf_op jit(solution)/shard_map/ppermute | solution.py:566
  15.1 1.3 %collective-permute-done.3.by_outer = f32[232,128]{1,0:T(8,128)S(1)} collective-permute-done((f32[232,128]{1,0:T(8,128)S(1)}, f32[232,128]{1,0:T(8,128)S(1)}, u32[]{:S(2)}, u32[]{:S(2)}) %collective-permute-start.3) | collective-permute-done | bytes 118816 | tf_op jit(solution)/shard_map/ppermute | solution.py:567
  16.4 3.6 %windows_over_edge.1 = (f32[2,448,768]{2,1,0:T(8,128)S(1)}, f32[3,448,768]{2,1,0:T(8,128)S(1)}, f32[72,512]{1,0:T(8,128)S(1)}, f32[72,512]{1,0:T(8,128)S(1)}) custom-call(s32[3,8]{1,0:T(4,128)S(1)} %get-tuple-element.25.slots.marked, f32[2,448,768]{2,1,0:T(8,128)S(1)} %get-tuple-element.29.cells.cells_in, ...), custom_call_target="tpu_custom_call", output_to_operand_aliasing={{0}: (1, {}), {1}: (2, {})} | custom-call | flops 4000000000 | bytes 8000000 | tf_op jit(solution)/shard_map/windows_over_edge/pallas_call | solution.py:645
  20.0 0.1 collective-permute-start.4
  20.1 0.1 collective-permute-start.5
  20.2 2.8 %windows_after.1.acc_in = f32[3,448,768]{2,1,0:T(8,128)S(1)} custom-call(s32[3,8]{1,0:T(4,128)S(1)} %get-tuple-element.25.slots.marked, f32[2,448,768]{2,1,0:T(8,128)S(1)} %get-tuple-element.37.cells, f32[3,448,768]{2,1,0:T(8,128)S(1)} %get-tuple-element.38.acc_in, f32[256,256]{1,0:T(8,128)S(1)} %get-tuple-element.31.probe_re, ...), custom_call_target="tpu_custom_call", output_to_operand_aliasing={{}: (2, {})} | custom-call | flops 4000000000 | bytes 8000000 | tf_op jit(solution)/shard_map/windows_after/pallas_call | solution.py:658
  23.0 2.6 %collective-permute-done.4.by_outer = f32[72,512]{1,0:T(8,128)S(1)} collective-permute-done((f32[72,512]{1,0:T(8,128)S(1)}, f32[72,512]{1,0:T(8,128)S(1)}, u32[]{:S(2)}, u32[]{:S(2)}) %collective-permute-start.4) | collective-permute-done | bytes 147488 | tf_op jit(solution)/shard_map/ppermute | solution.py:567
  25.6 0.0 collective-permute-done.5.by_inner
  25.6 0.3 column_spill.1
  25.9 0.1 collective-permute-start.6
  25.9 0.1 collective-permute-start.7
  26.0 1.7 %finish_inner.1 = (f32[3,448,768]{2,1,0:T(8,128)S(1)}, f32[384,512]{1,0:T(8,128)}, f32[384,512]{1,0:T(8,128)}) custom-call(s32[3,8]{1,0:T(4,128)S(1)} %get-tuple-element.25.slots.marked, f32[2,448,768]{2,1,0:T(8,128)S(1)} %get-tuple-element.37.cells, f32[3,448,768]{2,1,0:T(8,128)S(1)} %get-tuple-element.42.acc_in, ...), custom_call_target="tpu_custom_call", output_to_operand_aliasing={{0}: (2, {})} | custom-call | flops 4000000000 | bytes 8000000 | tf_op jit(solution)/shard_map/finish_inner/pallas_call | solution.py:687
  27.7 2.8 %collective-permute-done.6.by_inner = f32[192,128]{1,0:T(8,128)S(1)} collective-permute-done((f32[192,128]{1,0:T(8,128)S(1)}, f32[192,128]{1,0:T(8,128)S(1)}, u32[]{:S(2)}, u32[]{:S(2)}) %collective-permute-start.6) | collective-permute-done | bytes 98336 | tf_op jit(solution)/shard_map/ppermute | solution.py:566
  30.5 0.1 collective-permute-done.7.by_outer
  30.6 1.0 %finish_edges.1 = (f32[384,512]{1,0:T(8,128)}, f32[384,512]{1,0:T(8,128)}) custom-call(f32[2,448,768]{2,1,0:T(8,128)S(1)} %get-tuple-element.37.cells, f32[3,448,768]{2,1,0:T(8,128)S(1)} %get-tuple-element.43.acc, f32[192,128]{1,0:T(8,128)S(1)} %collective-permute-done.6.by_inner, ...), custom_call_target="tpu_custom_call", output_to_operand_aliasing={{0}: (4, {}), {1}: (5, {})} | custom-call | tf_op jit(solution)/shard_map/finish_edges/pallas_call | solution.py:698
Async XLA Ops:
  2.4 6.3 %collective-permute-start.1 = (f32[264,128]{1,0:T(8,128)S(1)}, f32[264,128]{1,0:T(8,128)S(1)}, u32[]{:S(2)}, u32[]{:S(2)}) collective-permute-start(f32[264,128]{1,0:T(8,128)S(1)} %get-tuple-element.28), channel_id=1, source_target_pairs={{0,4},{8,12},{16,20},{24,28},{4,0},{12,8},{20,16},{28,24},{1,5},{9... | collective-permute-start | bytes 405512 | tf_op jit(solution)/shard_map/ppermute | solution.py:566
  2.4 6.5 %collective-permute-start = (f32[264,128]{1,0:T(8,128)S(1)}, f32[264,128]{1,0:T(8,128)S(1)}, u32[]{:S(2)}, u32[]{:S(2)}) collective-permute-start(f32[264,128]{1,0:T(8,128)S(1)} %get-tuple-element.27.own), channel_id=1, source_target_pairs={{0,1},{1,0},{2,3},{3,2},{4,8},{5,9},{6,10},{7,11},{8,4},{9,5},{10,... | collective-permute-start | bytes 405512 | tf_op jit(solution)/shard_map/ppermute | solution.py:567
  9.2 5.9 %collective-permute-start.2 = (f32[232,128]{1,0:T(8,128)S(1)}, f32[232,128]{1,0:T(8,128)S(1)}, u32[]{:S(2)}, u32[]{:S(2)}) collective-permute-start(f32[232,128]{1,0:T(8,128)S(1)} %get-tuple-element.35), channel_id=1, source_target_pairs={{0,1},{2,3},{1,0},{3,2},{4,5},{6,7},{5,4},{7,6},{8,9},{10,11},{9,8... | collective-permute-start | bytes 356360 | tf_op jit(solution)/shard_map/ppermute | solution.py:566
  10.9 5.6 %collective-permute-start.3 = (f32[232,128]{1,0:T(8,128)S(1)}, f32[232,128]{1,0:T(8,128)S(1)}, u32[]{:S(2)}, u32[]{:S(2)}) collective-permute-start(f32[232,128]{1,0:T(8,128)S(1)} %get-tuple-element.36), channel_id=1, source_target_pairs={{0,4},{1,2},{2,1},{3,7},{4,0},{5,6},{6,5},{7,3},{8,12},{9,10},{10,... | collective-permute-start | bytes 356360 | tf_op jit(solution)/shard_map/ppermute | solution.py:567
  20.0 5.5 %collective-permute-start.4 = (f32[72,512]{1,0:T(8,128)S(1)}, f32[72,512]{1,0:T(8,128)S(1)}, u32[]{:S(2)}, u32[]{:S(2)}) collective-permute-start(f32[72,512]{1,0:T(8,128)S(1)} %get-tuple-element.40), channel_id=1, source_target_pairs={{0,1},{1,0},{2,3},{3,2},{4,8},{5,9},{6,10},{7,11},{8,4},{9,5},{10,... | collective-permute-start | bytes 442376 | tf_op jit(solution)/shard_map/ppermute | solution.py:567
  20.1 5.5 %collective-permute-start.5 = (f32[72,512]{1,0:T(8,128)S(1)}, f32[72,512]{1,0:T(8,128)S(1)}, u32[]{:S(2)}, u32[]{:S(2)}) collective-permute-start(f32[72,512]{1,0:T(8,128)S(1)} %get-tuple-element.41), channel_id=1, source_target_pairs={{0,4},{8,12},{16,20},{24,28},{4,0},{12,8},{20,16},{28,24},{1,5},{9... | collective-permute-start | bytes 442376 | tf_op jit(solution)/shard_map/ppermute | solution.py:566
  25.9 4.7 %collective-permute-start.6 = (f32[192,128]{1,0:T(8,128)S(1)}, f32[192,128]{1,0:T(8,128)S(1)}, u32[]{:S(2)}, u32[]{:S(2)}) collective-permute-start(f32[192,128]{1,0:T(8,128)S(1)} %get-tuple-element.44), channel_id=1, source_target_pairs={{0,1},{2,3},{1,0},{3,2},{4,5},{6,7},{5,4},{7,6},{8,9},{10,11},{9,8... | collective-permute-start | bytes 294920 | tf_op jit(solution)/shard_map/ppermute | solution.py:566
  25.9 4.7 %collective-permute-start.7 = (f32[192,128]{1,0:T(8,128)S(1)}, f32[192,128]{1,0:T(8,128)S(1)}, u32[]{:S(2)}, u32[]{:S(2)}) collective-permute-start(f32[192,128]{1,0:T(8,128)S(1)} %get-tuple-element.45), channel_id=1, source_target_pairs={{0,4},{1,2},{2,1},{3,7},{4,0},{5,6},{6,5},{7,3},{8,12},{9,10},{10,... | collective-permute-start | bytes 294920 | tf_op jit(solution)/shard_map/ppermute | solution.py:567

commit v6 on v4

--- a/solution.py
+++ b/solution.py
@@ -290,7 +290,7 @@
 FIRST, BEFORE, OVER, AFTER, LAST = range(5)
 
 
-def run_windows(phase, slots, cells, acc, probe_re, probe_im, table, frames, order):
+def run_windows(phase, slots, cells, acc, probe_re, probe_im, table, frames, order, largest=PAIR):
     tile_r, tile_c = cells.shape[1] - 2 * HALO, cells.shape[2] - 2 * LANES
     count = live_slots(slots, cells)
     kinds = []
@@ -363,15 +363,16 @@
         for x, back in zip(loaded, state):
             place(x[0], *back)
 
-    def pair_step(pair, carry):
-        step([order[pair * PAIR + i] for i in range(PAIR)])
+    def group_step(group, carry):
+        step([order[group * largest + i] for i in range(largest)])
         return carry
 
-    lax.fori_loop(0, found // PAIR, pair_step, 0)
-
-    @pl.when(found % PAIR == 1)
-    def _():
-        step([order[found - 1]])
+    lax.fori_loop(0, found // largest, group_step, 0)
+    for left in range(1, largest):
+
+        @pl.when(found % largest == left)
+        def _():
+            step([order[found - left + i] for i in range(left)])
 
 
 def windows_first(
@@ -468,7 +469,7 @@
     copy = pltpu.make_async_copy(whole, places, sem)
     copy.start()
     power[...] = probe_re[...] * probe_re[...] + probe_im[...] * probe_im[...]
-    run_windows(AFTER, slots, cells, acc, probe_re, probe_im, table, frames, order)
+    run_windows(AFTER, slots, cells, acc, probe_re, probe_im, table, frames, order, 2 * PAIR)
     copy.wait()
     add_neighbours_light(places, acc, power)
 

time: 31 us -> 31.9 us (1.029)
  the two profiles are of different devices: /device:TPU:20 before, /device:TPU:19 now
where the time goes in v6:
time: 31.9 us; the launch traced here: 31.4 us
  Pallas kernels  21.2 us (66%)
  starting transfers between devices  6.92 us (22%)
  waiting for transfers between devices  1.74 us (5%)
  between operations  1.59 us (5%)
    pallas_call x1, Pallas kernels, shards(): pl.pallas_call(windows_after, out_shape=acc_shape, in_specs=[SMEM] + [VME...  5.99 us
    pallas_call x1, Pallas kernels, shards(): pl.pallas_call(windows_first, out_shape=(cells_shape, acc_shape, f32(*pro...  5.32 us
    ppermute x4, starting transfers between devices, swap(): by_outer = lax.ppermute(to_outer, ('row', 'col'), pairs)  5.04 us
    pallas_call x1, Pallas kernels, shards(): pl.pallas_call(windows_before, out_shape=acc_shape, in_specs=[SMEM] + [VM...  4.51 us
    ppermute x4, starting transfers between devices, swap(): by_inner = lax.ppermute(to_inner, axis, inner + [(j, i) for i, j in inner])  1.88 us
    pallas_call x1, Pallas kernels, shards(): pl.pallas_call(finish_inner, out_shape=(acc_shape, *new), in_specs=[SMEM]...  1.73 us
    ppermute x4, waiting for transfers between devices, swap(): by_inner = lax.ppermute(to_inner, axis, inner + [(j, i) for i, j in inner])  1.65 us
    pallas_call x1, Pallas kernels, shards(): pl.pallas_call(row_edges, out_shape=(edge, edge, jax.ShapeDtypeStruct((3,...  1.08 us
  transfers between devices with their start and end apart: 8, of which 2 were waited for; matrix products, arithmetic and copies ran while one was open for 0% of the time, Pallas kernels for 56%

profile of v6, /device:TPU:19, one launch (start us, length us, event | category | flops | bytes accessed | tf_op | source)
XLA Modules:
  0.0 31.4 jit_solution(8260918850606152421)
XLA Ops:
  1.3 1.1 %row_edges.1 = (f32[264,128]{1,0:T(8,128)S(1)}, f32[264,128]{1,0:T(8,128)S(1)}, s32[3,8]{1,0:T(4,128)S(1)}) custom-call(s32[1,1]{1,0:T(1,128)S(6)} %copy.29.counts, f32[384,512]{1,0:T(8,128)} %obj_re.3, f32[384,512]{1,0:T(8,128)} %obj_im.3, s32[1,1,2,8]{3,2,1,0:T(2,128)} %bitcast.2, s32[1,1,8]{2,1,0:T(1,128)} %chosen.1), custom_call_target="tpu_custom_call" | custom-call | tf_op jit(solution)/shard_map/row_edges/pallas_call | solution.py:589
  2.4 0.7 %collective-permute-start.1 = (f32[264,128]{1,0:T(8,128)S(1)}, f32[264,128]{1,0:T(8,128)S(1)}, u32[]{:S(2)}, u32[]{:S(2)}) collective-permute-start(f32[264,128]{1,0:T(8,128)S(1)} %get-tuple-element.28), channel_id=1, source_target_pairs={{0,4},{8,12},{16,20},{24,28},{4,0},{12,8},{20,16},{28,24},{1,5},{9... | collective-permute-start | bytes 405512 | tf_op jit(solution)/shard_map/ppermute | solution.py:564
  3.1 1.2 %collective-permute-start = (f32[264,128]{1,0:T(8,128)S(1)}, f32[264,128]{1,0:T(8,128)S(1)}, u32[]{:S(2)}, u32[]{:S(2)}) collective-permute-start(f32[264,128]{1,0:T(8,128)S(1)} %get-tuple-element.27.own), channel_id=1, source_target_pairs={{0,1},{1,0},{2,3},{3,2},{4,8},{5,9},{6,10},{7,11},{8,4},{9,5},{10,... | collective-permute-start | bytes 405512 | tf_op jit(solution)/shard_map/ppermute | solution.py:565
  4.3 5.3 %windows_first.1 = (f32[2,448,768]{2,1,0:T(8,128)S(1)}, f32[3,448,768]{2,1,0:T(8,128)S(1)}, f32[256,256]{1,0:T(8,128)S(1)}, f32[256,256]{1,0:T(8,128)S(1)}, bf16...) custom-call(s32[3,8]{1,0:T(4,128)S(1)} %get-tuple-element.25.slots.marked, f32[384,512]{1,0:T(8,128)} %obj_re.3, ...), custom_call_target="tpu_custom_call" | custom-call | flops 4000000000 | bytes 8000000 | tf_op jit(solution)/shard_map/windows_first/pallas_call | solution.py:604
  9.6 0.0 collective-permute-done.1.by_inner
  9.6 0.0 collective-permute-done.by_outer
  9.6 0.3 row_halos.1
  9.9 1.1 %collective-permute-start.2 = (f32[232,128]{1,0:T(8,128)S(1)}, f32[232,128]{1,0:T(8,128)S(1)}, u32[]{:S(2)}, u32[]{:S(2)}) collective-permute-start(f32[232,128]{1,0:T(8,128)S(1)} %get-tuple-element.35), channel_id=1, source_target_pairs={{0,1},{2,3},{1,0},{3,2},{4,5},{6,7},{5,4},{7,6},{8,9},{10,11},{9,8... | collective-permute-start | bytes 356360 | tf_op jit(solution)/shard_map/ppermute | solution.py:564
  11.0 0.0 collective-permute-start.3
  11.0 4.5 %windows_before.1.acc_in = f32[3,448,768]{2,1,0:T(8,128)S(1)} custom-call(s32[3,8]{1,0:T(4,128)S(1)} %get-tuple-element.25.slots.marked, f32[2,448,768]{2,1,0:T(8,128)S(1)} %get-tuple-element.29.cells.cells_in, f32[3,448,768]{2,1,0:T(8,128)S(1)} %get-tuple-element.30.acc_in, ...), custom_call_target="tpu_custom_call", output_to_operand_aliasing={{}: (2, {})} | custom-call | flops 4000000000 | bytes 8000000 | tf_op jit(solution)/shard_map/windows_before/pallas_call | solution.py:630
  15.5 0.0 collective-permute-done.2.by_inner
  15.5 0.0 collective-permute-done.3.by_outer
  15.5 1.0 %windows_over_edge.1 = (f32[2,448,768]{2,1,0:T(8,128)S(1)}, f32[3,448,768]{2,1,0:T(8,128)S(1)}, f32[72,512]{1,0:T(8,128)S(1)}, f32[72,512]{1,0:T(8,128)S(1)}) custom-call(s32[3,8]{1,0:T(4,128)S(1)} %get-tuple-element.25.slots.marked, f32[2,448,768]{2,1,0:T(8,128)S(1)} %get-tuple-element.29.cells.cells_in, ...), custom_call_target="tpu_custom_call", output_to_operand_aliasing={{0}: (1, {}), {1}: (2, {})} | custom-call | flops 4000000000 | bytes 8000000 | tf_op jit(solution)/shard_map/windows_over_edge/pallas_call | solution.py:643
  16.5 3.8 %collective-permute-start.4 = (f32[72,512]{1,0:T(8,128)S(1)}, f32[72,512]{1,0:T(8,128)S(1)}, u32[]{:S(2)}, u32[]{:S(2)}) collective-permute-start(f32[72,512]{1,0:T(8,128)S(1)} %get-tuple-element.40), channel_id=1, source_target_pairs={{0,1},{1,0},{2,3},{3,2},{4,8},{5,9},{6,10},{7,11},{8,4},{9,5},{10,... | collective-permute-start | bytes 442376 | tf_op jit(solution)/shard_map/ppermute | solution.py:565
  20.3 0.0 collective-permute-start.5
  20.3 6.0 %windows_after.1.acc_in = f32[3,448,768]{2,1,0:T(8,128)S(1)} custom-call(s32[3,8]{1,0:T(4,128)S(1)} %get-tuple-element.25.slots.marked, f32[2,448,768]{2,1,0:T(8,128)S(1)} %get-tuple-element.37.cells, f32[3,448,768]{2,1,0:T(8,128)S(1)} %get-tuple-element.38.acc_in, f32[256,256]{1,0:T(8,128)S(1)} %get-tuple-element.31.probe_re, ...), custom_call_target="tpu_custom_call", output_to_operand_aliasing={{}: (2, {})} | custom-call | flops 4000000000 | bytes 8000000 | tf_op jit(solution)/shard_map/windows_after/pallas_call | solution.py:656
  26.3 0.0 collective-permute-done.4.by_outer
  26.3 0.0 collective-permute-done.5.by_inner
  26.3 0.3 column_spill.1
  26.6 0.1 collective-permute-start.6
  26.7 0.1 collective-permute-start.7
  26.8 1.7 %finish_inner.1 = (f32[3,448,768]{2,1,0:T(8,128)S(1)}, f32[384,512]{1,0:T(8,128)}, f32[384,512]{1,0:T(8,128)}) custom-call(s32[3,8]{1,0:T(4,128)S(1)} %get-tuple-element.25.slots.marked, f32[2,448,768]{2,1,0:T(8,128)S(1)} %get-tuple-element.37.cells, f32[3,448,768]{2,1,0:T(8,128)S(1)} %get-tuple-element.42.acc_in, ...), custom_call_target="tpu_custom_call", output_to_operand_aliasing={{0}: (2, {})} | custom-call | flops 4000000000 | bytes 8000000 | tf_op jit(solution)/shard_map/finish_inner/pallas_call | solution.py:685
  28.5 1.6 %collective-permute-done.6.by_inner = f32[192,128]{1,0:T(8,128)S(1)} collective-permute-done((f32[192,128]{1,0:T(8,128)S(1)}, f32[192,128]{1,0:T(8,128)S(1)}, u32[]{:S(2)}, u32[]{:S(2)}) %collective-permute-start.6) | collective-permute-done | bytes 98336 | tf_op jit(solution)/shard_map/ppermute | solution.py:564
  30.1 0.1 collective-permute-done.7.by_outer
  30.2 1.0 %finish_edges.1 = (f32[384,512]{1,0:T(8,128)}, f32[384,512]{1,0:T(8,128)}) custom-call(f32[2,448,768]{2,1,0:T(8,128)S(1)} %get-tuple-element.37.cells, f32[3,448,768]{2,1,0:T(8,128)S(1)} %get-tuple-element.43.acc, f32[192,128]{1,0:T(8,128)S(1)} %collective-permute-done.6.by_inner, ...), custom_call_target="tpu_custom_call", output_to_operand_aliasing={{0}: (4, {}), {1}: (5, {})} | custom-call | tf_op jit(solution)/shard_map/finish_edges/pallas_call | solution.py:696
Async XLA Ops:
  2.4 7.2 %collective-permute-start.1 = (f32[264,128]{1,0:T(8,128)S(1)}, f32[264,128]{1,0:T(8,128)S(1)}, u32[]{:S(2)}, u32[]{:S(2)}) collective-permute-start(f32[264,128]{1,0:T(8,128)S(1)} %get-tuple-element.28), channel_id=1, source_target_pairs={{0,4},{8,12},{16,20},{24,28},{4,0},{12,8},{20,16},{28,24},{1,5},{9... | collective-permute-start | bytes 405512 | tf_op jit(solution)/shard_map/ppermute | solution.py:564
  3.1 6.5 %collective-permute-start = (f32[264,128]{1,0:T(8,128)S(1)}, f32[264,128]{1,0:T(8,128)S(1)}, u32[]{:S(2)}, u32[]{:S(2)}) collective-permute-start(f32[264,128]{1,0:T(8,128)S(1)} %get-tuple-element.27.own), channel_id=1, source_target_pairs={{0,1},{1,0},{2,3},{3,2},{4,8},{5,9},{6,10},{7,11},{8,4},{9,5},{10,... | collective-permute-start | bytes 405512 | tf_op jit(solution)/shard_map/ppermute | solution.py:565
  9.9 5.6 %collective-permute-start.2 = (f32[232,128]{1,0:T(8,128)S(1)}, f32[232,128]{1,0:T(8,128)S(1)}, u32[]{:S(2)}, u32[]{:S(2)}) collective-permute-start(f32[232,128]{1,0:T(8,128)S(1)} %get-tuple-element.35), channel_id=1, source_target_pairs={{0,1},{2,3},{1,0},{3,2},{4,5},{6,7},{5,4},{7,6},{8,9},{10,11},{9,8... | collective-permute-start | bytes 356360 | tf_op jit(solution)/shard_map/ppermute | solution.py:564
  11.0 4.5 %collective-permute-start.3 = (f32[232,128]{1,0:T(8,128)S(1)}, f32[232,128]{1,0:T(8,128)S(1)}, u32[]{:S(2)}, u32[]{:S(2)}) collective-permute-start(f32[232,128]{1,0:T(8,128)S(1)} %get-tuple-element.36), channel_id=1, source_target_pairs={{0,4},{1,2},{2,1},{3,7},{4,0},{5,6},{6,5},{7,3},{8,12},{9,10},{10,... | collective-permute-start | bytes 356360 | tf_op jit(solution)/shard_map/ppermute | solution.py:565
  16.5 9.8 %collective-permute-start.4 = (f32[72,512]{1,0:T(8,128)S(1)}, f32[72,512]{1,0:T(8,128)S(1)}, u32[]{:S(2)}, u32[]{:S(2)}) collective-permute-start(f32[72,512]{1,0:T(8,128)S(1)} %get-tuple-element.40), channel_id=1, source_target_pairs={{0,1},{1,0},{2,3},{3,2},{4,8},{5,9},{6,10},{7,11},{8,4},{9,5},{10,... | collective-permute-start | bytes 442376 | tf_op jit(solution)/shard_map/ppermute | solution.py:565
  20.3 6.0 %collective-permute-start.5 = (f32[72,512]{1,0:T(8,128)S(1)}, f32[72,512]{1,0:T(8,128)S(1)}, u32[]{:S(2)}, u32[]{:S(2)}) collective-permute-start(f32[72,512]{1,0:T(8,128)S(1)} %get-tuple-element.41), channel_id=1, source_target_pairs={{0,4},{8,12},{16,20},{24,28},{4,0},{12,8},{20,16},{28,24},{1,5},{9... | collective-permute-start | bytes 442376 | tf_op jit(solution)/shard_map/ppermute | solution.py:564
  26.6 3.5 %collective-permute-start.6 = (f32[192,128]{1,0:T(8,128)S(1)}, f32[192,128]{1,0:T(8,128)S(1)}, u32[]{:S(2)}, u32[]{:S(2)}) collective-permute-start(f32[192,128]{1,0:T(8,128)S(1)} %get-tuple-element.44), channel_id=1, source_target_pairs={{0,1},{2,3},{1,0},{3,2},{4,5},{6,7},{5,4},{7,6},{8,9},{10,11},{9,8... | collective-permute-start | bytes 294920 | tf_op jit(solution)/shard_map/ppermute | solution.py:564
  26.7 3.5 %collective-permute-start.7 = (f32[192,128]{1,0:T(8,128)S(1)}, f32[192,128]{1,0:T(8,128)S(1)}, u32[]{:S(2)}, u32[]{:S(2)}) collective-permute-start(f32[192,128]{1,0:T(8,128)S(1)} %get-tuple-element.45), channel_id=1, source_target_pairs={{0,4},{1,2},{2,1},{3,7},{4,0},{5,6},{6,5},{7,3},{8,12},{9,10},{10,... | collective-permute-start | bytes 294920 | tf_op jit(solution)/shard_map/ppermute | solution.py:565

commit v7 on v4

--- a/solution.py
+++ b/solution.py
@@ -306,7 +306,7 @@
         n_inside += inside.astype(jnp.int32)
         n_row += by_row.astype(jnp.int32)
         n_col += by_col.astype(jnp.int32)
-    first = jnp.minimum(n_inside, PAIR)
+    first = jnp.where(count > 2 * PAIR, jnp.minimum(n_inside, PAIR), 0)
     before = first + jnp.minimum(n_inside - first, PAIR - jnp.minimum(n_row, PAIR))
     rest = n_inside - before
     after = n_inside - jnp.clip(n_col + rest - 2 * PAIR, 0, jnp.minimum(rest, PAIR))

time: 31 us -> 31.5 us (1.016)
  starting transfers between devices: 5.04 us -> 7.53 us
  waiting for transfers between devices: 12.4 us -> 10.3 us
    ppermute x4, waiting for transfers between devices: 4.85 us -> 1.05 us  [swap(): by_inner = lax.ppermute(to_inner, axis, inner + [(j, i) for i, j in inner])]
    ppermute x4, starting transfers between devices: 3.03 us -> 5.92 us  [swap(): by_inner = lax.ppermute(to_inner, axis, inner + [(j, i) for i, j in inner])]
    pallas_call x1, Pallas kernels: 0.89 us -> 2.68 us  [shards(): pl.pallas_call(windows_before, out_shape=acc_shape, in_specs=[SMEM] + [VM...]
    pallas_call x1, Pallas kernels: 4.67 us -> 2.88 us  [shards(): pl.pallas_call(windows_first, out_shape=(cells_shape, acc_shape, f32(*pro...]
    ppermute x4, waiting for transfers between devices: 7.56 us -> 9.28 us  [swap(): by_outer = lax.ppermute(to_outer, ('row', 'col'), pairs)]
    ppermute x4, starting transfers between devices: 2 us -> 1.61 us  [swap(): by_outer = lax.ppermute(to_outer, ('row', 'col'), pairs)]
where the time goes in v7:
time: 31.5 us; the launch traced here: 31.8 us
  Pallas kernels  12.4 us (39%)
  waiting for transfers between devices  10.3 us (33%)
  starting transfers between devices  7.53 us (24%)
  between operations  1.53 us (5%)
    ppermute x4, waiting for transfers between devices, swap(): by_outer = lax.ppermute(to_outer, ('row', 'col'), pairs)  9.28 us
    ppermute x4, starting transfers between devices, swap(): by_inner = lax.ppermute(to_inner, axis, inner + [(j, i) for i, j in inner])  5.92 us
    pallas_call x1, Pallas kernels, shards(): pl.pallas_call(windows_first, out_shape=(cells_shape, acc_shape, f32(*pro...  2.88 us
    pallas_call x1, Pallas kernels, shards(): pl.pallas_call(windows_before, out_shape=acc_shape, in_specs=[SMEM] + [VM...  2.68 us
    pallas_call x1, Pallas kernels, shards(): pl.pallas_call(finish_inner, out_shape=(acc_shape, *new), in_specs=[SMEM]...  1.72 us
    ppermute x4, starting transfers between devices, swap(): by_outer = lax.ppermute(to_outer, ('row', 'col'), pairs)  1.61 us
    pallas_call x1, Pallas kernels, shards(): pl.pallas_call(windows_after, out_shape=acc_shape, in_specs=[SMEM] + [VME...  1.48 us
    pallas_call x1, Pallas kernels, shards(): pl.pallas_call(row_edges, out_shape=(edge, edge, jax.ShapeDtypeStruct((3,...  1.08 us
  transfers between devices with their start and end apart: 8, of which 6 were waited for; matrix products, arithmetic and copies ran while one was open for 0% of the time, Pallas kernels for 28%

profile of v7, /device:TPU:20, one launch (start us, length us, event | category | flops | bytes accessed | tf_op | source)
XLA Modules:
  0.0 31.8 jit_solution(5296935670203305617)
XLA Ops:
  1.3 1.1 %row_edges.1 = (f32[264,128]{1,0:T(8,128)S(1)}, f32[264,128]{1,0:T(8,128)S(1)}, s32[3,8]{1,0:T(4,128)S(1)}) custom-call(s32[1,1]{1,0:T(1,128)S(6)} %copy.29.counts, f32[384,512]{1,0:T(8,128)} %obj_re.3, f32[384,512]{1,0:T(8,128)} %obj_im.3, s32[1,1,2,8]{3,2,1,0:T(2,128)} %bitcast.2, s32[1,1,8]{2,1,0:T(1,128)} %chosen.1), custom_call_target="tpu_custom_call" | custom-call | tf_op jit(solution)/shard_map/row_edges/pallas_call | solution.py:588
  2.4 0.1 collective-permute-start.1
  2.4 1.5 %collective-permute-start = (f32[264,128]{1,0:T(8,128)S(1)}, f32[264,128]{1,0:T(8,128)S(1)}, u32[]{:S(2)}, u32[]{:S(2)}) collective-permute-start(f32[264,128]{1,0:T(8,128)S(1)} %get-tuple-element.27.own), channel_id=1, source_target_pairs={{0,1},{1,0},{2,3},{3,2},{4,8},{5,9},{6,10},{7,11},{8,4},{9,5},{10,... | collective-permute-start | bytes 405512 | tf_op jit(solution)/shard_map/ppermute | solution.py:564
  4.0 2.9 %windows_first.1 = (f32[2,448,768]{2,1,0:T(8,128)S(1)}, f32[3,448,768]{2,1,0:T(8,128)S(1)}, f32[256,256]{1,0:T(8,128)S(1)}, f32[256,256]{1,0:T(8,128)S(1)}, bf16...) custom-call(s32[3,8]{1,0:T(4,128)S(1)} %get-tuple-element.25.slots.marked, f32[384,512]{1,0:T(8,128)} %obj_re.3, ...), custom_call_target="tpu_custom_call" | custom-call | flops 4000000000 | bytes 8000000 | tf_op jit(solution)/shard_map/windows_first/pallas_call | solution.py:603
  6.9 0.0 collective-permute-done.1.by_inner
  6.9 2.1 %collective-permute-done.by_outer = f32[264,128]{1,0:T(8,128)S(1)} collective-permute-done((f32[264,128]{1,0:T(8,128)S(1)}, f32[264,128]{1,0:T(8,128)S(1)}, u32[]{:S(2)}, u32[]{:S(2)}) %collective-permute-start) | collective-permute-done | bytes 135200 | tf_op jit(solution)/shard_map/ppermute | solution.py:564
  8.9 0.3 row_halos.1
  9.2 2.0 %collective-permute-start.2 = (f32[232,128]{1,0:T(8,128)S(1)}, f32[232,128]{1,0:T(8,128)S(1)}, u32[]{:S(2)}, u32[]{:S(2)}) collective-permute-start(f32[232,128]{1,0:T(8,128)S(1)} %get-tuple-element.35), channel_id=1, source_target_pairs={{0,1},{2,3},{1,0},{3,2},{4,5},{6,7},{5,4},{7,6},{8,9},{10,11},{9,8... | collective-permute-start | bytes 356360 | tf_op jit(solution)/shard_map/ppermute | solution.py:563
  11.2 0.0 collective-permute-start.3
  11.2 2.7 %windows_before.1.acc_in = f32[3,448,768]{2,1,0:T(8,128)S(1)} custom-call(s32[3,8]{1,0:T(4,128)S(1)} %get-tuple-element.25.slots.marked, f32[2,448,768]{2,1,0:T(8,128)S(1)} %get-tuple-element.29.cells.cells_in, f32[3,448,768]{2,1,0:T(8,128)S(1)} %get-tuple-element.30.acc_in, ...), custom_call_target="tpu_custom_call", output_to_operand_aliasing={{}: (2, {})} | custom-call | flops 4000000000 | bytes 8000000 | tf_op jit(solution)/shard_map/windows_before/pallas_call | solution.py:629
  13.9 0.2 collective-permute-done.2.by_inner
  14.1 2.0 %collective-permute-done.3.by_outer = f32[232,128]{1,0:T(8,128)S(1)} collective-permute-done((f32[232,128]{1,0:T(8,128)S(1)}, f32[232,128]{1,0:T(8,128)S(1)}, u32[]{:S(2)}, u32[]{:S(2)}) %collective-permute-start.3) | collective-permute-done | bytes 118816 | tf_op jit(solution)/shard_map/ppermute | solution.py:564
  16.1 1.0 %windows_over_edge.1 = (f32[2,448,768]{2,1,0:T(8,128)S(1)}, f32[3,448,768]{2,1,0:T(8,128)S(1)}, f32[72,512]{1,0:T(8,128)S(1)}, f32[72,512]{1,0:T(8,128)S(1)}) custom-call(s32[3,8]{1,0:T(4,128)S(1)} %get-tuple-element.25.slots.marked, f32[2,448,768]{2,1,0:T(8,128)S(1)} %get-tuple-element.29.cells.cells_in, ...), custom_call_target="tpu_custom_call", output_to_operand_aliasing={{0}: (1, {}), {1}: (2, {})} | custom-call | flops 4000000000 | bytes 8000000 | tf_op jit(solution)/shard_map/windows_over_edge/pallas_call | solution.py:642
  17.1 0.1 collective-permute-start.4
  17.1 0.7 %collective-permute-start.5 = (f32[72,512]{1,0:T(8,128)S(1)}, f32[72,512]{1,0:T(8,128)S(1)}, u32[]{:S(2)}, u32[]{:S(2)}) collective-permute-start(f32[72,512]{1,0:T(8,128)S(1)} %get-tuple-element.41), channel_id=1, source_target_pairs={{0,4},{8,12},{16,20},{24,28},{4,0},{12,8},{20,16},{28,24},{1,5},{9... | collective-permute-start | bytes 442376 | tf_op jit(solution)/shard_map/ppermute | solution.py:563
  17.9 1.5 %windows_after.1.acc_in = f32[3,448,768]{2,1,0:T(8,128)S(1)} custom-call(s32[3,8]{1,0:T(4,128)S(1)} %get-tuple-element.25.slots.marked, f32[2,448,768]{2,1,0:T(8,128)S(1)} %get-tuple-element.37.cells, f32[3,448,768]{2,1,0:T(8,128)S(1)} %get-tuple-element.38.acc_in, f32[256,256]{1,0:T(8,128)S(1)} %get-tuple-element.31.probe_re, ...), custom_call_target="tpu_custom_call", output_to_operand_aliasing={{}: (2, {})} | custom-call | flops 4000000000 | bytes 8000000 | tf_op jit(solution)/shard_map/windows_after/pallas_call | solution.py:655
  19.4 3.2 %collective-permute-done.4.by_outer = f32[72,512]{1,0:T(8,128)S(1)} collective-permute-done((f32[72,512]{1,0:T(8,128)S(1)}, f32[72,512]{1,0:T(8,128)S(1)}, u32[]{:S(2)}, u32[]{:S(2)}) %collective-permute-start.4) | collective-permute-done | bytes 147488 | tf_op jit(solution)/shard_map/ppermute | solution.py:564
  22.6 0.0 collective-permute-done.5.by_inner
  22.6 0.3 column_spill.1
  22.9 3.1 %collective-permute-start.6 = (f32[192,128]{1,0:T(8,128)S(1)}, f32[192,128]{1,0:T(8,128)S(1)}, u32[]{:S(2)}, u32[]{:S(2)}) collective-permute-start(f32[192,128]{1,0:T(8,128)S(1)} %get-tuple-element.44), channel_id=1, source_target_pairs={{0,1},{2,3},{1,0},{3,2},{4,5},{6,7},{5,4},{7,6},{8,9},{10,11},{9,8... | collective-permute-start | bytes 294920 | tf_op jit(solution)/shard_map/ppermute | solution.py:563
  26.0 0.0 collective-permute-start.7
  26.0 1.7 %finish_inner.1 = (f32[3,448,768]{2,1,0:T(8,128)S(1)}, f32[384,512]{1,0:T(8,128)}, f32[384,512]{1,0:T(8,128)}) custom-call(s32[3,8]{1,0:T(4,128)S(1)} %get-tuple-element.25.slots.marked, f32[2,448,768]{2,1,0:T(8,128)S(1)} %get-tuple-element.37.cells, f32[3,448,768]{2,1,0:T(8,128)S(1)} %get-tuple-element.42.acc_in, ...), custom_call_target="tpu_custom_call", output_to_operand_aliasing={{0}: (2, {})} | custom-call | flops 4000000000 | bytes 8000000 | tf_op jit(solution)/shard_map/finish_inner/pallas_call | solution.py:684
  27.7 0.9 %collective-permute-done.6.by_inner = f32[192,128]{1,0:T(8,128)S(1)} collective-permute-done((f32[192,128]{1,0:T(8,128)S(1)}, f32[192,128]{1,0:T(8,128)S(1)}, u32[]{:S(2)}, u32[]{:S(2)}) %collective-permute-start.6) | collective-permute-done | bytes 98336 | tf_op jit(solution)/shard_map/ppermute | solution.py:563
  28.6 2.0 %collective-permute-done.7.by_outer = f32[192,128]{1,0:T(8,128)S(1)} collective-permute-done((f32[192,128]{1,0:T(8,128)S(1)}, f32[192,128]{1,0:T(8,128)S(1)}, u32[]{:S(2)}, u32[]{:S(2)}) %collective-permute-start.7) | collective-permute-done | bytes 98336 | tf_op jit(solution)/shard_map/ppermute | solution.py:564
  30.6 1.0 %finish_edges.1 = (f32[384,512]{1,0:T(8,128)}, f32[384,512]{1,0:T(8,128)}) custom-call(f32[2,448,768]{2,1,0:T(8,128)S(1)} %get-tuple-element.37.cells, f32[3,448,768]{2,1,0:T(8,128)S(1)} %get-tuple-element.43.acc, f32[192,128]{1,0:T(8,128)S(1)} %collective-permute-done.6.by_inner, ...), custom_call_target="tpu_custom_call", output_to_operand_aliasing={{0}: (4, {}), {1}: (5, {})} | custom-call | tf_op jit(solution)/shard_map/finish_edges/pallas_call | solution.py:695
Async XLA Ops:
  2.4 4.5 %collective-permute-start.1 = (f32[264,128]{1,0:T(8,128)S(1)}, f32[264,128]{1,0:T(8,128)S(1)}, u32[]{:S(2)}, u32[]{:S(2)}) collective-permute-start(f32[264,128]{1,0:T(8,128)S(1)} %get-tuple-element.28), channel_id=1, source_target_pairs={{0,4},{8,12},{16,20},{24,28},{4,0},{12,8},{20,16},{28,24},{1,5},{9... | collective-permute-start | bytes 405512 | tf_op jit(solution)/shard_map/ppermute | solution.py:563
  2.4 6.5 %collective-permute-start = (f32[264,128]{1,0:T(8,128)S(1)}, f32[264,128]{1,0:T(8,128)S(1)}, u32[]{:S(2)}, u32[]{:S(2)}) collective-permute-start(f32[264,128]{1,0:T(8,128)S(1)} %get-tuple-element.27.own), channel_id=1, source_target_pairs={{0,1},{1,0},{2,3},{3,2},{4,8},{5,9},{6,10},{7,11},{8,4},{9,5},{10,... | collective-permute-start | bytes 405512 | tf_op jit(solution)/shard_map/ppermute | solution.py:564
  9.2 4.9 %collective-permute-start.2 = (f32[232,128]{1,0:T(8,128)S(1)}, f32[232,128]{1,0:T(8,128)S(1)}, u32[]{:S(2)}, u32[]{:S(2)}) collective-permute-start(f32[232,128]{1,0:T(8,128)S(1)} %get-tuple-element.35), channel_id=1, source_target_pairs={{0,1},{2,3},{1,0},{3,2},{4,5},{6,7},{5,4},{7,6},{8,9},{10,11},{9,8... | collective-permute-start | bytes 356360 | tf_op jit(solution)/shard_map/ppermute | solution.py:563
  11.2 4.8 %collective-permute-start.3 = (f32[232,128]{1,0:T(8,128)S(1)}, f32[232,128]{1,0:T(8,128)S(1)}, u32[]{:S(2)}, u32[]{:S(2)}) collective-permute-start(f32[232,128]{1,0:T(8,128)S(1)} %get-tuple-element.36), channel_id=1, source_target_pairs={{0,4},{1,2},{2,1},{3,7},{4,0},{5,6},{6,5},{7,3},{8,12},{9,10},{10,... | collective-permute-start | bytes 356360 | tf_op jit(solution)/shard_map/ppermute | solution.py:564
  17.1 5.5 %collective-permute-start.4 = (f32[72,512]{1,0:T(8,128)S(1)}, f32[72,512]{1,0:T(8,128)S(1)}, u32[]{:S(2)}, u32[]{:S(2)}) collective-permute-start(f32[72,512]{1,0:T(8,128)S(1)} %get-tuple-element.40), channel_id=1, source_target_pairs={{0,1},{1,0},{2,3},{3,2},{4,8},{5,9},{6,10},{7,11},{8,4},{9,5},{10,... | collective-permute-start | bytes 442376 | tf_op jit(solution)/shard_map/ppermute | solution.py:564
  17.1 5.5 %collective-permute-start.5 = (f32[72,512]{1,0:T(8,128)S(1)}, f32[72,512]{1,0:T(8,128)S(1)}, u32[]{:S(2)}, u32[]{:S(2)}) collective-permute-start(f32[72,512]{1,0:T(8,128)S(1)} %get-tuple-element.41), channel_id=1, source_target_pairs={{0,4},{8,12},{16,20},{24,28},{4,0},{12,8},{20,16},{28,24},{1,5},{9... | collective-permute-start | bytes 442376 | tf_op jit(solution)/shard_map/ppermute | solution.py:563
  22.9 5.7 %collective-permute-start.6 = (f32[192,128]{1,0:T(8,128)S(1)}, f32[192,128]{1,0:T(8,128)S(1)}, u32[]{:S(2)}, u32[]{:S(2)}) collective-permute-start(f32[192,128]{1,0:T(8,128)S(1)} %get-tuple-element.44), channel_id=1, source_target_pairs={{0,1},{2,3},{1,0},{3,2},{4,5},{6,7},{5,4},{7,6},{8,9},{10,11},{9,8... | collective-permute-start | bytes 294920 | tf_op jit(solution)/shard_map/ppermute | solution.py:563
  26.0 4.6 %collective-permute-start.7 = (f32[192,128]{1,0:T(8,128)S(1)}, f32[192,128]{1,0:T(8,128)S(1)}, u32[]{:S(2)}, u32[]{:S(2)}) collective-permute-start(f32[192,128]{1,0:T(8,128)S(1)} %get-tuple-element.45), channel_id=1, source_target_pairs={{0,4},{1,2},{2,1},{3,7},{4,0},{5,6},{6,5},{7,3},{8,12},{9,10},{10,... | collective-permute-start | bytes 294920 | tf_op jit(solution)/shard_map/ppermute | solution.py:564

commit v8 on v5

--- a/solution.py
+++ b/solution.py
@@ -514,15 +514,14 @@
     send_columns(to_left, to_right, to_inner, to_outer)
 
 
-def new_columns(cells, acc, spill, start, size, near_re, near_im):
-    rows = acc.shape[1]
-    here, there = slice(HALO, rows - HALO), slice(LANES + start, LANES + start + size)
+def new_columns(cells, acc, spill, top, tall, start, size, near_re, near_im):
+    here, there = slice(HALO + top, HALO + top + tall), slice(LANES + start, LANES + start + size)
     part = [acc[k, here, there] for k in range(acc.shape[0])]
     if spill is not None:
         part[:2] = [part[k] + spill[k] for k in (0, 1)]
     scale = 1.0 / (part[2] + ridge)
-    near_re[:, start : start + size] = cells[0, here, there] - part[0] * scale
-    near_im[:, start : start + size] = cells[1, here, there] - part[1] * scale
+    near_re[top : top + tall, start : start + size] = cells[0, here, there] - part[0] * scale
+    near_im[top : top + tall, start : start + size] = cells[1, here, there] - part[1] * scale
 
 
 def finish_inner(
@@ -530,23 +529,25 @@
 ):
     run_windows(LAST, slots, cells, acc, probe_re, probe_im, table, frames, order)
     size = near_re.shape[1] - 2 * LANES
-    new_columns(cells, acc, None, LANES, size, near_re, near_im)
+    new_columns(cells, acc, None, 0, near_re.shape[0], LANES, size, near_re, near_im)
     there = slice(LANES, LANES + size)
     finish_all(fetch([(near_re.at[:, there], new_re.at[:, there]), (near_im.at[:, there], new_im.at[:, there])], sems))
 
 
 def finish_edges(cells, acc, by_inner, by_outer, re_in, im_in, new_re, new_im, near_re, near_im, sems):
     tile_r, tile_c = near_re.shape
-    lane = lane_index(tile_r)
+    half = tile_r // 2
+    lane = lane_index(half)
     sides = ((0, lane < HALO), (tile_c - LANES, lane >= LANES - HALO))
     copies = []
     for i, ((start, mine), packed) in enumerate(zip(sides, received(by_inner, by_outer, "col"))):
-        parts = [part for _, _, part in pieces(packed, tile_r)]
-        spill = [jnp.where(mine, below(*parts[2 * k : 2 * k + 2]), 0.0) for k in (0, 1)]
-        new_columns(cells, acc, spill, start, LANES, near_re, near_im)
+        parts = [jnp.where(mine, part, 0.0) for _, _, part in pieces(packed, tile_r)]
         there = slice(start, start + LANES)
-        pairs = ((near_re.at[:, there], new_re.at[:, there]), (near_im.at[:, there], new_im.at[:, there]))
-        copies += fetch(pairs, sems.at[2 * i : 2 * i + 2])
+        for j in (0, 1):
+            new_columns(cells, acc, (parts[j], parts[2 + j]), j * half, half, start, LANES, near_re, near_im)
+            rows = slice(j * half, (j + 1) * half)
+            pairs = ((near_re.at[rows, there], new_re.at[rows, there]), (near_im.at[rows, there], new_im.at[rows, there]))
+            copies += fetch(pairs, sems.at[4 * i + 2 * j : 4 * i + 2 * j + 2])
     finish_all(copies)
 
 
@@ -700,7 +701,7 @@
         out_shape=new,
         in_specs=[VMEM] * 4 + [HBM] * 2,
         out_specs=(HBM, HBM),
-        scratch_shapes=near + [dma((4,))],
+        scratch_shapes=near + [dma((8,))],
         input_output_aliases={4: 0, 5: 1},
         compiler_params=SMALL,
         name="finish_edges",

time: 32.4 us -> 31.4 us (0.969)
  waiting for transfers between devices: 9.92 us -> 3.01 us
  Pallas kernels: 16.8 us -> 22.8 us
    ppermute x4, waiting for transfers between devices: 4.24 us -> 0.21 us  [swap(): by_outer = lax.ppermute(to_outer, ('row', 'col'), pairs)]
    pallas_call x1, Pallas kernels: 1.39 us -> 4.69 us  [shards(): pl.pallas_call(windows_before, out_shape=acc_shape, in_specs=[SMEM] + [VM...]
    ppermute x4, waiting for transfers between devices: 5.68 us -> 2.8 us  [swap(): by_inner = lax.ppermute(to_inner, axis, inner + [(j, i) for i, j in inner])]
    pallas_call x1, Pallas kernels: 2.79 us -> 5.43 us  [shards(): pl.pallas_call(windows_after, out_shape=acc_shape, in_specs=[SMEM] + [VME...]
    pallas_call x1, Pallas kernels: 4.67 us -> 5.52 us  [shards(): pl.pallas_call(windows_first, out_shape=(cells_shape, acc_shape, f32(*pro...]
    pallas_call x1, Pallas kernels: 3.57 us -> 2.75 us  [shards(): pl.pallas_call(windows_over_edge, out_shape=(cells_shape, acc_shape, edge...]
  transfers between devices with their start and end apart: 8 -> 8, of which waited for: 6 -> 3; matrix products, arithmetic and copies ran while one was open for 0% -> 0% of each run, Pallas kernels for 33% -> 56%
where the time goes in v8:
time: 31.4 us; the launch traced here: 30.8 us
  Pallas kernels  22.8 us (73%)
  starting transfers between devices  3.42 us (11%)
  waiting for transfers between devices  3.01 us (10%)
  between operations  1.57 us (5%)
    pallas_call x1, Pallas kernels, shards(): pl.pallas_call(windows_first, out_shape=(cells_shape, acc_shape, f32(*pro...  5.52 us
    pallas_call x1, Pallas kernels, shards(): pl.pallas_call(windows_after, out_shape=acc_shape, in_specs=[SMEM] + [VME...  5.43 us
    pallas_call x1, Pallas kernels, shards(): pl.pallas_call(windows_before, out_shape=acc_shape, in_specs=[SMEM] + [VM...  4.69 us
    ppermute x4, waiting for transfers between devices, swap(): by_inner = lax.ppermute(to_inner, axis, inner + [(j, i) for i, j in inner])  2.8 us
    pallas_call x1, Pallas kernels, shards(): pl.pallas_call(windows_over_edge, out_shape=(cells_shape, acc_shape, edge...  2.75 us
    ppermute x4, starting transfers between devices, swap(): by_inner = lax.ppermute(to_inner, axis, inner + [(j, i) for i, j in inner])  1.74 us
    pallas_call x1, Pallas kernels, shards(): pl.pallas_call(finish_inner, out_shape=(acc_shape, *new), in_specs=[SMEM]...  1.73 us
    ppermute x4, starting transfers between devices, swap(): by_outer = lax.ppermute(to_outer, ('row', 'col'), pairs)  1.68 us
  transfers between devices with their start and end apart: 8, of which 3 were waited for; matrix products, arithmetic and copies ran while one was open for 0% of the time, Pallas kernels for 56%

profile of v8, /device:TPU:20, one launch (start us, length us, event | category | flops | bytes accessed | tf_op | source)
XLA Modules:
  0.0 30.8 jit_solution(3508726024855160814)
XLA Ops:
  1.3 1.1 %row_edges.1 = (f32[264,128]{1,0:T(8,128)S(1)}, f32[264,128]{1,0:T(8,128)S(1)}, s32[3,8]{1,0:T(4,128)S(1)}) custom-call(s32[1,1]{1,0:T(1,128)S(6)} %copy.29.counts, f32[384,512]{1,0:T(8,128)} %obj_re.3, f32[384,512]{1,0:T(8,128)} %obj_im.3, s32[1,1,2,8]{3,2,1,0:T(2,128)} %bitcast.2, s32[1,1,8]{2,1,0:T(1,128)} %chosen.1), custom_call_target="tpu_custom_call" | custom-call | tf_op jit(solution)/shard_map/row_edges/pallas_call | solution.py:592
  2.4 0.1 collective-permute-start.1
  2.4 1.5 %collective-permute-start = (f32[264,128]{1,0:T(8,128)S(1)}, f32[264,128]{1,0:T(8,128)S(1)}, u32[]{:S(2)}, u32[]{:S(2)}) collective-permute-start(f32[264,128]{1,0:T(8,128)S(1)} %get-tuple-element.27.own), channel_id=1, source_target_pairs={{0,1},{1,0},{2,3},{3,2},{4,8},{5,9},{6,10},{7,11},{8,4},{9,5},{10,... | collective-permute-start | bytes 405512 | tf_op jit(solution)/shard_map/ppermute | solution.py:568
  4.0 5.5 %windows_first.1 = (f32[2,448,768]{2,1,0:T(8,128)S(1)}, f32[3,448,768]{2,1,0:T(8,128)S(1)}, f32[256,256]{1,0:T(8,128)S(1)}, f32[256,256]{1,0:T(8,128)S(1)}, bf16...) custom-call(s32[3,8]{1,0:T(4,128)S(1)} %get-tuple-element.25.slots.marked, f32[384,512]{1,0:T(8,128)} %obj_re.3, ...), custom_call_target="tpu_custom_call" | custom-call | flops 4000000000 | bytes 8000000 | tf_op jit(solution)/shard_map/windows_first/pallas_call | solution.py:607
  9.5 0.0 collective-permute-done.1.by_inner
  9.5 0.0 collective-permute-done.by_outer
  9.5 0.3 row_halos.1
  9.8 1.1 %collective-permute-start.2 = (f32[232,128]{1,0:T(8,128)S(1)}, f32[232,128]{1,0:T(8,128)S(1)}, u32[]{:S(2)}, u32[]{:S(2)}) collective-permute-start(f32[232,128]{1,0:T(8,128)S(1)} %get-tuple-element.35), channel_id=1, source_target_pairs={{0,1},{2,3},{1,0},{3,2},{4,5},{6,7},{5,4},{7,6},{8,9},{10,11},{9,8... | collective-permute-start | bytes 356360 | tf_op jit(solution)/shard_map/ppermute | solution.py:567
  10.9 0.0 collective-permute-start.3
  10.9 4.7 %windows_before.1.acc_in = f32[3,448,768]{2,1,0:T(8,128)S(1)} custom-call(s32[3,8]{1,0:T(4,128)S(1)} %get-tuple-element.25.slots.marked, f32[2,448,768]{2,1,0:T(8,128)S(1)} %get-tuple-element.29.cells.cells_in, f32[3,448,768]{2,1,0:T(8,128)S(1)} %get-tuple-element.30.acc_in, ...), custom_call_target="tpu_custom_call", output_to_operand_aliasing={{}: (2, {})} | custom-call | flops 4000000000 | bytes 8000000 | tf_op jit(solution)/shard_map/windows_before/pallas_call | solution.py:633
  15.6 0.0 collective-permute-done.2.by_inner
  15.6 0.1 collective-permute-done.3.by_outer
  15.7 2.7 %windows_over_edge.1 = (f32[2,448,768]{2,1,0:T(8,128)S(1)}, f32[3,448,768]{2,1,0:T(8,128)S(1)}, f32[72,512]{1,0:T(8,128)S(1)}, f32[72,512]{1,0:T(8,128)S(1)}) custom-call(s32[3,8]{1,0:T(4,128)S(1)} %get-tuple-element.25.slots.marked, f32[2,448,768]{2,1,0:T(8,128)S(1)} %get-tuple-element.29.cells.cells_in, ...), custom_call_target="tpu_custom_call", output_to_operand_aliasing={{0}: (1, {}), {1}: (2, {})} | custom-call | flops 4000000000 | bytes 8000000 | tf_op jit(solution)/shard_map/windows_over_edge/pallas_call | solution.py:646
  18.4 0.1 collective-permute-start.4
  18.5 0.5 %collective-permute-start.5 = (f32[72,512]{1,0:T(8,128)S(1)}, f32[72,512]{1,0:T(8,128)S(1)}, u32[]{:S(2)}, u32[]{:S(2)}) collective-permute-start(f32[72,512]{1,0:T(8,128)S(1)} %get-tuple-element.41), channel_id=1, source_target_pairs={{0,4},{8,12},{16,20},{24,28},{4,0},{12,8},{20,16},{28,24},{1,5},{9... | collective-permute-start | bytes 442376 | tf_op jit(solution)/shard_map/ppermute | solution.py:567
  19.1 5.4 %windows_after.1.acc_in = f32[3,448,768]{2,1,0:T(8,128)S(1)} custom-call(s32[3,8]{1,0:T(4,128)S(1)} %get-tuple-element.25.slots.marked, f32[2,448,768]{2,1,0:T(8,128)S(1)} %get-tuple-element.37.cells, f32[3,448,768]{2,1,0:T(8,128)S(1)} %get-tuple-element.38.acc_in, f32[256,256]{1,0:T(8,128)S(1)} %get-tuple-element.31.probe_re, ...), custom_call_target="tpu_custom_call", output_to_operand_aliasing={{}: (2, {})} | custom-call | flops 4000000000 | bytes 8000000 | tf_op jit(solution)/shard_map/windows_after/pallas_call | solution.py:659
  24.5 0.0 collective-permute-done.4.by_outer
  24.5 0.0 collective-permute-done.5.by_inner
  24.5 0.3 column_spill.1
  24.8 0.1 collective-permute-start.6
  24.9 0.1 collective-permute-start.7
  25.0 1.7 %finish_inner.1 = (f32[3,448,768]{2,1,0:T(8,128)S(1)}, f32[384,512]{1,0:T(8,128)}, f32[384,512]{1,0:T(8,128)}) custom-call(s32[3,8]{1,0:T(4,128)S(1)} %get-tuple-element.25.slots.marked, f32[2,448,768]{2,1,0:T(8,128)S(1)} %get-tuple-element.37.cells, f32[3,448,768]{2,1,0:T(8,128)S(1)} %get-tuple-element.42.acc_in, ...), custom_call_target="tpu_custom_call", output_to_operand_aliasing={{0}: (2, {})} | custom-call | flops 4000000000 | bytes 8000000 | tf_op jit(solution)/shard_map/finish_inner/pallas_call | solution.py:688
  26.7 2.8 %collective-permute-done.6.by_inner = f32[192,128]{1,0:T(8,128)S(1)} collective-permute-done((f32[192,128]{1,0:T(8,128)S(1)}, f32[192,128]{1,0:T(8,128)S(1)}, u32[]{:S(2)}, u32[]{:S(2)}) %collective-permute-start.6) | collective-permute-done | bytes 98336 | tf_op jit(solution)/shard_map/ppermute | solution.py:567
  29.5 0.1 collective-permute-done.7.by_outer
  29.6 1.1 %finish_edges.1 = (f32[384,512]{1,0:T(8,128)}, f32[384,512]{1,0:T(8,128)}) custom-call(f32[2,448,768]{2,1,0:T(8,128)S(1)} %get-tuple-element.37.cells, f32[3,448,768]{2,1,0:T(8,128)S(1)} %get-tuple-element.43.acc, f32[192,128]{1,0:T(8,128)S(1)} %collective-permute-done.6.by_inner, ...), custom_call_target="tpu_custom_call", output_to_operand_aliasing={{0}: (4, {}), {1}: (5, {})} | custom-call | tf_op jit(solution)/shard_map/finish_edges/pallas_call | solution.py:699
Async XLA Ops:
  2.4 7.1 %collective-permute-start.1 = (f32[264,128]{1,0:T(8,128)S(1)}, f32[264,128]{1,0:T(8,128)S(1)}, u32[]{:S(2)}, u32[]{:S(2)}) collective-permute-start(f32[264,128]{1,0:T(8,128)S(1)} %get-tuple-element.28), channel_id=1, source_target_pairs={{0,4},{8,12},{16,20},{24,28},{4,0},{12,8},{20,16},{28,24},{1,5},{9... | collective-permute-start | bytes 405512 | tf_op jit(solution)/shard_map/ppermute | solution.py:567
  2.4 7.1 %collective-permute-start = (f32[264,128]{1,0:T(8,128)S(1)}, f32[264,128]{1,0:T(8,128)S(1)}, u32[]{:S(2)}, u32[]{:S(2)}) collective-permute-start(f32[264,128]{1,0:T(8,128)S(1)} %get-tuple-element.27.own), channel_id=1, source_target_pairs={{0,1},{1,0},{2,3},{3,2},{4,8},{5,9},{6,10},{7,11},{8,4},{9,5},{10,... | collective-permute-start | bytes 405512 | tf_op jit(solution)/shard_map/ppermute | solution.py:568
  9.8 5.8 %collective-permute-start.2 = (f32[232,128]{1,0:T(8,128)S(1)}, f32[232,128]{1,0:T(8,128)S(1)}, u32[]{:S(2)}, u32[]{:S(2)}) collective-permute-start(f32[232,128]{1,0:T(8,128)S(1)} %get-tuple-element.35), channel_id=1, source_target_pairs={{0,1},{2,3},{1,0},{3,2},{4,5},{6,7},{5,4},{7,6},{8,9},{10,11},{9,8... | collective-permute-start | bytes 356360 | tf_op jit(solution)/shard_map/ppermute | solution.py:567
  10.9 4.8 %collective-permute-start.3 = (f32[232,128]{1,0:T(8,128)S(1)}, f32[232,128]{1,0:T(8,128)S(1)}, u32[]{:S(2)}, u32[]{:S(2)}) collective-permute-start(f32[232,128]{1,0:T(8,128)S(1)} %get-tuple-element.36), channel_id=1, source_target_pairs={{0,4},{1,2},{2,1},{3,7},{4,0},{5,6},{6,5},{7,3},{8,12},{9,10},{10,... | collective-permute-start | bytes 356360 | tf_op jit(solution)/shard_map/ppermute | solution.py:568
  18.4 6.1 %collective-permute-start.4 = (f32[72,512]{1,0:T(8,128)S(1)}, f32[72,512]{1,0:T(8,128)S(1)}, u32[]{:S(2)}, u32[]{:S(2)}) collective-permute-start(f32[72,512]{1,0:T(8,128)S(1)} %get-tuple-element.40), channel_id=1, source_target_pairs={{0,1},{1,0},{2,3},{3,2},{4,8},{5,9},{6,10},{7,11},{8,4},{9,5},{10,... | collective-permute-start | bytes 442376 | tf_op jit(solution)/shard_map/ppermute | solution.py:568
  18.5 6.0 %collective-permute-start.5 = (f32[72,512]{1,0:T(8,128)S(1)}, f32[72,512]{1,0:T(8,128)S(1)}, u32[]{:S(2)}, u32[]{:S(2)}) collective-permute-start(f32[72,512]{1,0:T(8,128)S(1)} %get-tuple-element.41), channel_id=1, source_target_pairs={{0,4},{8,12},{16,20},{24,28},{4,0},{12,8},{20,16},{28,24},{1,5},{9... | collective-permute-start | bytes 442376 | tf_op jit(solution)/shard_map/ppermute | solution.py:567
  24.8 4.7 %collective-permute-start.6 = (f32[192,128]{1,0:T(8,128)S(1)}, f32[192,128]{1,0:T(8,128)S(1)}, u32[]{:S(2)}, u32[]{:S(2)}) collective-permute-start(f32[192,128]{1,0:T(8,128)S(1)} %get-tuple-element.44), channel_id=1, source_target_pairs={{0,1},{2,3},{1,0},{3,2},{4,5},{6,7},{5,4},{7,6},{8,9},{10,11},{9,8... | collective-permute-start | bytes 294920 | tf_op jit(solution)/shard_map/ppermute | solution.py:567
  24.9 4.7 %collective-permute-start.7 = (f32[192,128]{1,0:T(8,128)S(1)}, f32[192,128]{1,0:T(8,128)S(1)}, u32[]{:S(2)}, u32[]{:S(2)}) collective-permute-start(f32[192,128]{1,0:T(8,128)S(1)} %get-tuple-element.45), channel_id=1, source_target_pairs={{0,4},{1,2},{2,1},{3,7},{4,0},{5,6},{6,5},{7,3},{8,12},{9,10},{10,... | collective-permute-start | bytes 294920 | tf_op jit(solution)/shard_map/ppermute | solution.py:568

commit v9 on v5

--- a/solution.py
+++ b/solution.py
@@ -306,7 +306,7 @@
         n_inside += inside.astype(jnp.int32)
         n_row += by_row.astype(jnp.int32)
         n_col += by_col.astype(jnp.int32)
-    first = jnp.minimum(n_inside, PAIR)
+    first = jnp.where(count > PAIR, jnp.minimum(n_inside, PAIR), 0)
     before = first + jnp.minimum(n_inside - first, PAIR - jnp.minimum(n_row, PAIR))
     rest = n_inside - before
     after = n_inside - jnp.clip(n_col + rest - 2 * PAIR, 0, jnp.minimum(rest, PAIR))

time: 32.4 us -> 33.1 us (1.022)
  the two profiles are of different devices: /device:TPU:20 before, /device:TPU:12 now
where the time goes in v9:
time: 33.1 us
  Pallas kernels  12.8 us (39%)
  waiting for transfers between devices  9.62 us (29%)
  starting transfers between devices  9.2 us (28%)
  between operations  1.53 us (5%)
    ppermute x4, waiting for transfers between devices, swap(): by_outer = lax.ppermute(to_outer, ('row', 'col'), pairs)  7.96 us
    ppermute x4, starting transfers between devices, swap(): by_inner = lax.ppermute(to_inner, axis, inner + [(j, i) for i, j in inner])  5.48 us
    ppermute x4, starting transfers between devices, swap(): by_outer = lax.ppermute(to_outer, ('row', 'col'), pairs)  3.72 us
    pallas_call x1, Pallas kernels, shards(): pl.pallas_call(windows_first, out_shape=(cells_shape, acc_shape, f32(*pro...  2.88 us
    pallas_call x1, Pallas kernels, shards(): pl.pallas_call(windows_over_edge, out_shape=(cells_shape, acc_shape, edge...  2.73 us
    pallas_call x1, Pallas kernels, shards(): pl.pallas_call(windows_after, out_shape=acc_shape, in_specs=[SMEM] + [VME...  1.91 us
    pallas_call x1, Pallas kernels, shards(): pl.pallas_call(finish_inner, out_shape=(acc_shape, *new), in_specs=[SMEM]...  1.72 us
    ppermute x4, waiting for transfers between devices, swap(): by_inner = lax.ppermute(to_inner, axis, inner + [(j, i) for i, j in inner])  1.66 us
  transfers between devices with their start and end apart: 8, of which 6 were waited for; matrix products, arithmetic and copies ran while one was open for 0% of the time, Pallas kernels for 22%

profile of v9, /device:TPU:12, one launch (start us, length us, event | category | flops | bytes accessed | tf_op | source)
XLA Modules:
  0.0 33.1 jit_solution(12480955189602498999)
XLA Ops:
  1.3 1.1 %row_edges.1 = (f32[264,128]{1,0:T(8,128)S(1)}, f32[264,128]{1,0:T(8,128)S(1)}, s32[3,8]{1,0:T(4,128)S(1)}) custom-call(s32[1,1]{1,0:T(1,128)S(6)} %copy.29.counts, f32[384,512]{1,0:T(8,128)} %obj_re.3, f32[384,512]{1,0:T(8,128)} %obj_im.3, s32[1,1,2,8]{3,2,1,0:T(2,128)} %bitcast.2, s32[1,1,8]{2,1,0:T(1,128)} %chosen.1), custom_call_target="tpu_custom_call" | custom-call | tf_op jit(solution)/shard_map/row_edges/pallas_call | solution.py:591
  2.4 0.1 collective-permute-start.1
  2.4 1.5 %collective-permute-start = (f32[264,128]{1,0:T(8,128)S(1)}, f32[264,128]{1,0:T(8,128)S(1)}, u32[]{:S(2)}, u32[]{:S(2)}) collective-permute-start(f32[264,128]{1,0:T(8,128)S(1)} %get-tuple-element.27.own), channel_id=1, source_target_pairs={{0,1},{1,0},{2,3},{3,2},{4,8},{5,9},{6,10},{7,11},{8,4},{9,5},{10,... | collective-permute-start | bytes 405512 | tf_op jit(solution)/shard_map/ppermute | solution.py:567
  4.0 2.9 %windows_first.1 = (f32[2,448,768]{2,1,0:T(8,128)S(1)}, f32[3,448,768]{2,1,0:T(8,128)S(1)}, f32[256,256]{1,0:T(8,128)S(1)}, f32[256,256]{1,0:T(8,128)S(1)}, bf16...) custom-call(s32[3,8]{1,0:T(4,128)S(1)} %get-tuple-element.25.slots.marked, f32[384,512]{1,0:T(8,128)} %obj_re.3, ...), custom_call_target="tpu_custom_call" | custom-call | flops 4000000000 | bytes 8000000 | tf_op jit(solution)/shard_map/windows_first/pallas_call | solution.py:606
  6.9 0.0 collective-permute-done.1.by_inner
  6.9 2.1 %collective-permute-done.by_outer = f32[264,128]{1,0:T(8,128)S(1)} collective-permute-done((f32[264,128]{1,0:T(8,128)S(1)}, f32[264,128]{1,0:T(8,128)S(1)}, u32[]{:S(2)}, u32[]{:S(2)}) %collective-permute-start) | collective-permute-done | bytes 135200 | tf_op jit(solution)/shard_map/ppermute | solution.py:567
  8.9 0.3 row_halos.1
  9.2 1.1 %collective-permute-start.2 = (f32[232,128]{1,0:T(8,128)S(1)}, f32[232,128]{1,0:T(8,128)S(1)}, u32[]{:S(2)}, u32[]{:S(2)}) collective-permute-start(f32[232,128]{1,0:T(8,128)S(1)} %get-tuple-element.35), channel_id=1, source_target_pairs={{0,1},{2,3},{1,0},{3,2},{4,5},{6,7},{5,4},{7,6},{8,9},{10,11},{9,8... | collective-permute-start | bytes 356360 | tf_op jit(solution)/shard_map/ppermute | solution.py:566
  10.3 2.1 %collective-permute-start.3 = (f32[232,128]{1,0:T(8,128)S(1)}, f32[232,128]{1,0:T(8,128)S(1)}, u32[]{:S(2)}, u32[]{:S(2)}) collective-permute-start(f32[232,128]{1,0:T(8,128)S(1)} %get-tuple-element.36), channel_id=1, source_target_pairs={{0,4},{1,2},{2,1},{3,7},{4,0},{5,6},{6,5},{7,3},{8,12},{9,10},{10,... | collective-permute-start | bytes 356360 | tf_op jit(solution)/shard_map/ppermute | solution.py:567
  12.4 0.9 %windows_before.1.acc_in = f32[3,448,768]{2,1,0:T(8,128)S(1)} custom-call(s32[3,8]{1,0:T(4,128)S(1)} %get-tuple-element.25.slots.marked, f32[2,448,768]{2,1,0:T(8,128)S(1)} %get-tuple-element.29.cells.cells_in, f32[3,448,768]{2,1,0:T(8,128)S(1)} %get-tuple-element.30.acc_in, ...), custom_call_target="tpu_custom_call", output_to_operand_aliasing={{}: (2, {})} | custom-call | flops 4000000000 | bytes 8000000 | tf_op jit(solution)/shard_map/windows_before/pallas_call | solution.py:632
  13.3 0.8 %collective-permute-done.2.by_inner = f32[232,128]{1,0:T(8,128)S(1)} collective-permute-done((f32[232,128]{1,0:T(8,128)S(1)}, f32[232,128]{1,0:T(8,128)S(1)}, u32[]{:S(2)}, u32[]{:S(2)}) %collective-permute-start.2) | collective-permute-done | bytes 118816 | tf_op jit(solution)/shard_map/ppermute | solution.py:566
  14.1 1.1 %collective-permute-done.3.by_outer = f32[232,128]{1,0:T(8,128)S(1)} collective-permute-done((f32[232,128]{1,0:T(8,128)S(1)}, f32[232,128]{1,0:T(8,128)S(1)}, u32[]{:S(2)}, u32[]{:S(2)}) %collective-permute-start.3) | collective-permute-done | bytes 118816 | tf_op jit(solution)/shard_map/ppermute | solution.py:567
  15.2 2.7 %windows_over_edge.1 = (f32[2,448,768]{2,1,0:T(8,128)S(1)}, f32[3,448,768]{2,1,0:T(8,128)S(1)}, f32[72,512]{1,0:T(8,128)S(1)}, f32[72,512]{1,0:T(8,128)S(1)}) custom-call(s32[3,8]{1,0:T(4,128)S(1)} %get-tuple-element.25.slots.marked, f32[2,448,768]{2,1,0:T(8,128)S(1)} %get-tuple-element.29.cells.cells_in, ...), custom_call_target="tpu_custom_call", output_to_operand_aliasing={{0}: (1, {}), {1}: (2, {})} | custom-call | flops 4000000000 | bytes 8000000 | tf_op jit(solution)/shard_map/windows_over_edge/pallas_call | solution.py:645
  18.0 0.1 collective-permute-start.4
  18.1 0.8 %collective-permute-start.5 = (f32[72,512]{1,0:T(8,128)S(1)}, f32[72,512]{1,0:T(8,128)S(1)}, u32[]{:S(2)}, u32[]{:S(2)}) collective-permute-start(f32[72,512]{1,0:T(8,128)S(1)} %get-tuple-element.41), channel_id=1, source_target_pairs={{0,4},{8,12},{16,20},{24,28},{4,0},{12,8},{20,16},{28,24},{1,5},{9... | collective-permute-start | bytes 442376 | tf_op jit(solution)/shard_map/ppermute | solution.py:566
  18.9 1.9 %windows_after.1.acc_in = f32[3,448,768]{2,1,0:T(8,128)S(1)} custom-call(s32[3,8]{1,0:T(4,128)S(1)} %get-tuple-element.25.slots.marked, f32[2,448,768]{2,1,0:T(8,128)S(1)} %get-tuple-element.37.cells, f32[3,448,768]{2,1,0:T(8,128)S(1)} %get-tuple-element.38.acc_in, f32[256,256]{1,0:T(8,128)S(1)} %get-tuple-element.31.probe_re, ...), custom_call_target="tpu_custom_call", output_to_operand_aliasing={{}: (2, {})} | custom-call | flops 4000000000 | bytes 8000000 | tf_op jit(solution)/shard_map/windows_after/pallas_call | solution.py:658
  20.8 2.7 %collective-permute-done.4.by_outer = f32[72,512]{1,0:T(8,128)S(1)} collective-permute-done((f32[72,512]{1,0:T(8,128)S(1)}, f32[72,512]{1,0:T(8,128)S(1)}, u32[]{:S(2)}, u32[]{:S(2)}) %collective-permute-start.4) | collective-permute-done | bytes 147488 | tf_op jit(solution)/shard_map/ppermute | solution.py:567
  23.5 0.0 collective-permute-done.5.by_inner
  23.5 0.3 column_spill.1
  23.8 3.5 %collective-permute-start.6 = (f32[192,128]{1,0:T(8,128)S(1)}, f32[192,128]{1,0:T(8,128)S(1)}, u32[]{:S(2)}, u32[]{:S(2)}) collective-permute-start(f32[192,128]{1,0:T(8,128)S(1)} %get-tuple-element.44), channel_id=1, source_target_pairs={{0,1},{2,3},{1,0},{3,2},{4,5},{6,7},{5,4},{7,6},{8,9},{10,11},{9,8... | collective-permute-start | bytes 294920 | tf_op jit(solution)/shard_map/ppermute | solution.py:566
  27.3 0.0 collective-permute-start.7
  27.3 1.7 %finish_inner.1 = (f32[3,448,768]{2,1,0:T(8,128)S(1)}, f32[384,512]{1,0:T(8,128)}, f32[384,512]{1,0:T(8,128)}) custom-call(s32[3,8]{1,0:T(4,128)S(1)} %get-tuple-element.25.slots.marked, f32[2,448,768]{2,1,0:T(8,128)S(1)} %get-tuple-element.37.cells, f32[3,448,768]{2,1,0:T(8,128)S(1)} %get-tuple-element.42.acc_in, ...), custom_call_target="tpu_custom_call", output_to_operand_aliasing={{0}: (2, {})} | custom-call | flops 4000000000 | bytes 8000000 | tf_op jit(solution)/shard_map/finish_inner/pallas_call | solution.py:687
  29.1 0.9 %collective-permute-done.6.by_inner = f32[192,128]{1,0:T(8,128)S(1)} collective-permute-done((f32[192,128]{1,0:T(8,128)S(1)}, f32[192,128]{1,0:T(8,128)S(1)}, u32[]{:S(2)}, u32[]{:S(2)}) %collective-permute-start.6) | collective-permute-done | bytes 98336 | tf_op jit(solution)/shard_map/ppermute | solution.py:566
  29.9 2.0 %collective-permute-done.7.by_outer = f32[192,128]{1,0:T(8,128)S(1)} collective-permute-done((f32[192,128]{1,0:T(8,128)S(1)}, f32[192,128]{1,0:T(8,128)S(1)}, u32[]{:S(2)}, u32[]{:S(2)}) %collective-permute-start.7) | collective-permute-done | bytes 98336 | tf_op jit(solution)/shard_map/ppermute | solution.py:567
  31.9 1.0 %finish_edges.1 = (f32[384,512]{1,0:T(8,128)}, f32[384,512]{1,0:T(8,128)}) custom-call(f32[2,448,768]{2,1,0:T(8,128)S(1)} %get-tuple-element.37.cells, f32[3,448,768]{2,1,0:T(8,128)S(1)} %get-tuple-element.43.acc, f32[192,128]{1,0:T(8,128)S(1)} %collective-permute-done.6.by_inner, ...), custom_call_target="tpu_custom_call", output_to_operand_aliasing={{0}: (4, {}), {1}: (5, {})} | custom-call | tf_op jit(solution)/shard_map/finish_edges/pallas_call | solution.py:698
Async XLA Ops:
  2.4 4.5 %collective-permute-start.1 = (f32[264,128]{1,0:T(8,128)S(1)}, f32[264,128]{1,0:T(8,128)S(1)}, u32[]{:S(2)}, u32[]{:S(2)}) collective-permute-start(f32[264,128]{1,0:T(8,128)S(1)} %get-tuple-element.28), channel_id=1, source_target_pairs={{0,4},{8,12},{16,20},{24,28},{4,0},{12,8},{20,16},{28,24},{1,5},{9... | collective-permute-start | bytes 405512 | tf_op jit(solution)/shard_map/ppermute | solution.py:566
  2.4 6.5 %collective-permute-start = (f32[264,128]{1,0:T(8,128)S(1)}, f32[264,128]{1,0:T(8,128)S(1)}, u32[]{:S(2)}, u32[]{:S(2)}) collective-permute-start(f32[264,128]{1,0:T(8,128)S(1)} %get-tuple-element.27.own), channel_id=1, source_target_pairs={{0,1},{1,0},{2,3},{3,2},{4,8},{5,9},{6,10},{7,11},{8,4},{9,5},{10,... | collective-permute-start | bytes 405512 | tf_op jit(solution)/shard_map/ppermute | solution.py:567
  9.2 4.9 %collective-permute-start.2 = (f32[232,128]{1,0:T(8,128)S(1)}, f32[232,128]{1,0:T(8,128)S(1)}, u32[]{:S(2)}, u32[]{:S(2)}) collective-permute-start(f32[232,128]{1,0:T(8,128)S(1)} %get-tuple-element.35), channel_id=1, source_target_pairs={{0,1},{2,3},{1,0},{3,2},{4,5},{6,7},{5,4},{7,6},{8,9},{10,11},{9,8... | collective-permute-start | bytes 356360 | tf_op jit(solution)/shard_map/ppermute | solution.py:566
  10.3 4.9 %collective-permute-start.3 = (f32[232,128]{1,0:T(8,128)S(1)}, f32[232,128]{1,0:T(8,128)S(1)}, u32[]{:S(2)}, u32[]{:S(2)}) collective-permute-start(f32[232,128]{1,0:T(8,128)S(1)} %get-tuple-element.36), channel_id=1, source_target_pairs={{0,4},{1,2},{2,1},{3,7},{4,0},{5,6},{6,5},{7,3},{8,12},{9,10},{10,... | collective-permute-start | bytes 356360 | tf_op jit(solution)/shard_map/ppermute | solution.py:567
  18.0 5.5 %collective-permute-start.4 = (f32[72,512]{1,0:T(8,128)S(1)}, f32[72,512]{1,0:T(8,128)S(1)}, u32[]{:S(2)}, u32[]{:S(2)}) collective-permute-start(f32[72,512]{1,0:T(8,128)S(1)} %get-tuple-element.40), channel_id=1, source_target_pairs={{0,1},{1,0},{2,3},{3,2},{4,8},{5,9},{6,10},{7,11},{8,4},{9,5},{10,... | collective-permute-start | bytes 442376 | tf_op jit(solution)/shard_map/ppermute | solution.py:567
  18.1 5.5 %collective-permute-start.5 = (f32[72,512]{1,0:T(8,128)S(1)}, f32[72,512]{1,0:T(8,128)S(1)}, u32[]{:S(2)}, u32[]{:S(2)}) collective-permute-start(f32[72,512]{1,0:T(8,128)S(1)} %get-tuple-element.41), channel_id=1, source_target_pairs={{0,4},{8,12},{16,20},{24,28},{4,0},{12,8},{20,16},{28,24},{1,5},{9... | collective-permute-start | bytes 442376 | tf_op jit(solution)/shard_map/ppermute | solution.py:566
  23.8 6.1 %collective-permute-start.6 = (f32[192,128]{1,0:T(8,128)S(1)}, f32[192,128]{1,0:T(8,128)S(1)}, u32[]{:S(2)}, u32[]{:S(2)}) collective-permute-start(f32[192,128]{1,0:T(8,128)S(1)} %get-tuple-element.44), channel_id=1, source_target_pairs={{0,1},{2,3},{1,0},{3,2},{4,5},{6,7},{5,4},{7,6},{8,9},{10,11},{9,8... | collective-permute-start | bytes 294920 | tf_op jit(solution)/shard_map/ppermute | solution.py:566
  27.3 4.6 %collective-permute-start.7 = (f32[192,128]{1,0:T(8,128)S(1)}, f32[192,128]{1,0:T(8,128)S(1)}, u32[]{:S(2)}, u32[]{:S(2)}) collective-permute-start(f32[192,128]{1,0:T(8,128)S(1)} %get-tuple-element.45), channel_id=1, source_target_pairs={{0,4},{1,2},{2,1},{3,7},{4,0},{5,6},{6,5},{7,3},{8,12},{9,10},{10,... | collective-permute-start | bytes 294920 | tf_op jit(solution)/shard_map/ppermute | solution.py:567
